TPU v7x, 32 devices: a whole 2x2x4 slice. The times are simulated.
32 devices in a mesh: cluster: 8 (over z, x), tile: 4 (over y, core).
Axes of the slice: x: 2, y: 2, z: 4, core: 2. Of those that a mesh axis runs over, the one named last changes fastest.
Arguments:
- points: bfloat16 [64, 8, 512], P('cluster', None, 'tile'), as said below
- charges: bfloat16 [64, 512, 256], P('cluster', 'tile'), may hold values from -6 to 6
- near_ids: int32 [64, 8], P('cluster'), may hold values from 0 to 63, as said below
- near_count: int32 [64], P('cluster'), may hold values from 1 to 8, as said below
- leaf_pivots: int32 [64, 256], P('cluster'), may hold values from 0 to 511, as said below
- merge_pivots: int32 [32, 6, 256], P('cluster'), may hold values from 0 to 511, as said below
Outputs:
- near_field: bfloat16 [64, 512, 256], P('cluster', 'tile')
- top_weights: bfloat16 [8, 256, 256], P('cluster', None, 'tile')
Inputs may be any that keep to these rules, and one draw needn't show every extreme that they name: `near_ids`: slot 0 of box b holds b itself and slots from near_count[b] on repeat b; the other used slots name distinct boxes other than b at most 4 boxes away from b; some box names a box exactly 4 away. `near_count`: some box uses all 8 slots. `leaf_pivots`: the pivots of a box are distinct. `merge_pivots`: the pivots of a row are distinct; rows q and q2 of level l are equal when q // 2^l == q2 // 2^l. The points of a box lie around a centre that moves along a smooth curve with the box number.
All inputs are finite; a program needn't handle non-finite values.
Results may differ from a plain program's by a relative error of at most 0.005.
Values may be sent and summed in bfloat16 or wider, within the bound.
No kernel may reach another device: no remote copies, remote signals or barrier semaphores. Data moves between devices by JAX's collectives and lax.ppermute only.
A program may use at most 192 MiB of HBM per device.

v0:
```python
import functools
import math

import jax
import jax.numpy as jnp
from jax import lax
from jax.experimental import pallas as pl
from jax.experimental.pallas import tpu as pltpu
from jax.sharding import PartitionSpec as P

SPAN = 4
lengthscale = 0.7
KAPPA = math.log2(math.e) / lengthscale
FLOOR = 1e-30
VMEM_LIMIT = 48 * 1024 * 1024
f32 = jnp.float32
bf16 = jnp.bfloat16
VMEM = pl.BlockSpec(memory_space=pltpu.VMEM)
SMEM = pl.BlockSpec(memory_space=pltpu.SMEM)


def features(coords, centre):
    shifted = (coords - centre) * KAPPA
    high = shifted.astype(bf16).astype(f32)
    low = (shifted - high).astype(bf16).astype(f32)
    both = high + low
    norm = jnp.sum(both * both, axis=0, keepdims=True)
    first = norm.astype(bf16).astype(f32)
    second = (norm - first).astype(bf16).astype(f32)
    third = norm - first - second
    row = lax.broadcasted_iota(jnp.int32, coords.shape, 0)
    one = jnp.ones_like(coords)
    nil = jnp.zeros_like(coords)

    def six(a, b, c, d, e, f):
        out = jnp.where(row == 0, a, jnp.where(row == 1, b, jnp.where(row == 2, c, nil)))
        return jnp.where(row == 3, d, jnp.where(row == 4, e, jnp.where(row == 5, f, out)))

    left = [-2 * high, -2 * high, -2 * low, -2 * low, six(first, second, third, one, one, one), nil]
    right = [high, low, high, low, six(one, one, one, first, second, third), nil]
    return jnp.concatenate(left, axis=0), jnp.concatenate(right, axis=0).astype(bf16)


def kernel_values(squares):
    squares = jnp.maximum(squares, FLOOR)
    return jnp.exp2(-(squares * lax.rsqrt(squares))).astype(bf16)


def dot(a, b):
    return jnp.dot(a, b, preferred_element_type=f32)


def choose(coords, pivots):
    place = lax.broadcasted_iota(jnp.int32, (coords.shape[1], pivots.shape[1]), 0)
    return dot(coords.astype(bf16), jnp.where(place == pivots, 1.0, 0.0).astype(bf16))


def lanes(*parts):
    return jnp.concatenate(parts, axis=1)


def centre_of(coords):
    return jnp.mean(coords.astype(f32), axis=1, keepdims=True)


def tree_kernel(info, pts0, pts1, pts2, pts3, own, mate, leaf_pv, merge_pv, out, held):
    half = leaf_pv.shape[0]
    group = info[1]
    tile = info[2]
    first = group * half
    points = [pts0, pts1, pts2, pts3]
    centre = centre_of(pts0[first + half // 2])
    coords, weights = [], []
    for i in range(half):
        box = first + i
        own_pts = pts0[box].astype(f32)
        mate_pts = pts1[box].astype(f32)
        whole = lanes(own_pts, mate_pts, pts2[box].astype(f32), pts3[box].astype(f32))
        chosen = choose(whole, leaf_pv[i : i + 1, :] ^ (tile * own_pts.shape[1]))
        left, _ = features(chosen, centre)
        _, right = features(lanes(own_pts, mate_pts), centre)
        values = kernel_values(dot(left.T.astype(bf16), right))
        charge = jnp.concatenate([own[box], mate[box]], axis=0)
        coords.append(chosen)
        weights.append(dot(values, charge).astype(bf16))
    level = 0
    row = 0
    while len(coords) > 1:
        next_coords, next_weights = [], []
        for i in range(len(coords) // 2):
            cand = lanes(coords[2 * i], coords[2 * i + 1])
            chosen = choose(cand, merge_pv[row : row + 1, :])
            row += 1
            left, _ = features(chosen, centre)
            _, right = features(cand, centre)
            values = kernel_values(dot(left.T.astype(bf16), right))
            charge = jnp.concatenate([weights[2 * i], weights[2 * i + 1]], axis=0)
            next_coords.append(chosen)
            next_weights.append(dot(values, charge))
        coords = next_coords
        if len(coords) > 1:
            weights = [w.astype(bf16) for w in next_weights]
        else:
            weights = next_weights
        level += 1
    held[...] = weights[0].T
    width = out.shape[1] - 16
    extra = jnp.concatenate([coords[0], jnp.zeros_like(coords[0])], axis=0).astype(bf16)
    for d in range(4):
        part = held[pl.ds(pl.multiple_of((tile ^ d) * width, width), width), :]
        out[d] = jnp.concatenate([part.astype(bf16), extra], axis=0)


def merge_body(cand_coords, cand_weights, pivots):
    chosen = choose(cand_coords, pivots)
    across = cand_coords.T
    squares = None
    for f in range(cand_coords.shape[0]):
        diff = across[:, f : f + 1] - chosen[f : f + 1, :]
        squares = diff * diff if squares is None else squares + diff * diff
    values = kernel_values(squares * (KAPPA * KAPPA))
    return chosen, dot(cand_weights, values)


def join_kernel(info, mine, got1, got2, got3, pivots, out):
    width = out.shape[0] - 16
    ours = (mine[:width, :].astype(f32) + got2[:width, :].astype(f32)).astype(bf16)
    theirs = (got1[:width, :].astype(f32) + got3[:width, :].astype(f32)).astype(bf16)
    coords = lanes(mine[width:, :].astype(f32)[:8], got1[width:, :].astype(f32)[:8])
    chosen, merged = merge_body(coords, lanes(ours, theirs), pivots[...] ^ (info[1] * mine.shape[1]))
    extra = jnp.concatenate([chosen, jnp.zeros_like(chosen)], axis=0)
    out[...] = jnp.concatenate([merged, extra], axis=0).astype(bf16)


def level_kernel(last, info, mine, got, pivots, out):
    width = mine.shape[0] - 16
    coords = lanes(mine[width:, :].astype(f32)[:8], got[width:, :].astype(f32)[:8])
    weights = lanes(mine[:width, :], got[:width, :])
    chosen, merged = merge_body(coords, weights, pivots[...] ^ (info[0] * mine.shape[1]))
    if last:
        out[...] = merged.T.astype(bf16)
    else:
        extra = jnp.concatenate([chosen, jnp.zeros_like(chosen)], axis=0)
        out[...] = jnp.concatenate([merged, extra], axis=0).astype(bf16)


def near_own_kernel(info, ids, count, pts0, pts1, pts2, pts3, own, mate, out, right_ref, left_ref):
    boxes = own.shape[0]
    half = out.shape[0]
    group = info[1]
    base = info[0]
    centre = centre_of(pts0[group * half + half // 2])
    for n in range(boxes):
        right_ref[n] = features(lanes(pts0[n], pts1[n]).astype(f32), centre)[1]

    def one(n):
        charge = jnp.concatenate([own[n], mate[n]], axis=0)
        return dot(kernel_values(dot(left_ref[...], right_ref[n])), charge)

    def box_step(u, _):
        box = group * half + u
        whole = lanes(pts0[box], pts1[box], pts2[box], pts3[box]).astype(f32)
        left_ref[...] = features(whole, centre)[0].T.astype(bf16)
        out[u] = one(box)

        def slot_step(slot, _):
            n = ids[box, slot] - base

            @pl.when((n >= 0) & (n < boxes))
            def _():
                out[u] += one(n)

            return 0

        lax.fori_loop(1, count[box], slot_step, 0)
        return 0

    lax.fori_loop(0, half, box_step, 0)


def near_halo_kernel(part, info, ids, count, pts0, pts1, pts2, pts3, total, *rest):
    halos = rest[: 2 * (part + 1)]
    keep, send, right_ref, left_ref, acc = rest[2 * (part + 1) :]
    boxes = pts0.shape[0]
    half = boxes // 2
    pair = half // 2
    group = info[1]
    base = info[0]
    centre = centre_of(pts0[group * half + half // 2])
    for k in range(part + 1):
        for i in range(pair):
            right_ref[k * pair + i] = features(halos[2 * k][i].astype(f32), centre)[1]
    start = jnp.where(group == 0, (1 - part) * pair, part * pair)
    rows = pts0.shape[2]

    def box_step(v, _):
        u = start + v
        box = group * half + u
        whole = lanes(pts0[box], pts1[box], pts2[box], pts3[box]).astype(f32)
        left_ref[...] = features(whole, centre)[0].T.astype(bf16)
        acc[...] = total[u]

        def slot_step(slot, _):
            n = ids[box, slot] - base

            @pl.when((n < 0) | (n >= boxes))
            def _():
                away = jnp.where(group == 0, -1 - n, n - boxes)
                chunk = away // pair
                inside = jnp.where(group == 0, pair - 1 - away % pair, away % pair)
                for k in range(part + 1):

                    @pl.when(chunk == k)
                    def _():
                        values = kernel_values(dot(left_ref[...], right_ref[k * pair + inside]))
                        acc[...] += dot(values, halos[2 * k + 1][inside])

            return 0

        lax.fori_loop(1, count[box], slot_step, 0)
        keep[v] = acc[:rows, :]
        for d in range(1, 4):
            send[d - 1, v] = acc[d * rows : (d + 1) * rows, :].astype(bf16)
        return 0

    lax.fori_loop(0, pair, box_step, 0)


def call(body, out_shape, n_smem, n_vmem, scratch=()):
    return pl.pallas_call(
        body,
        out_shape=out_shape,
        in_specs=[SMEM] * n_smem + [VMEM] * n_vmem,
        out_specs=jax.tree.map(lambda _: VMEM, out_shape),
        scratch_shapes=list(scratch),
        compiler_params=pltpu.CompilerParams(vmem_limit_bytes=VMEM_LIMIT),
    )


def on_device(points, charges, near_ids, near_count, leaf_pivots, merge_pivots):
    boxes, feat, rows = points.shape
    probes = charges.shape[2]
    rank = leaf_pivots.shape[1]
    half = boxes // 2
    pair = half // 2
    tiles = lax.axis_size("tile")
    clusters = lax.axis_size("cluster")
    c = lax.axis_index("cluster")
    t = lax.axis_index("tile")
    group = t % 2
    base = c * boxes
    info = jnp.stack([base, group, t]).astype(jnp.int32)

    def to_tile(x, d):
        return lax.ppermute(x, "tile", [(i, i ^ d) for i in range(tiles)])

    def to_halo(x):
        route = []
        for i in range(clusters):
            for k in range(tiles):
                target = i + 1 if k % 2 == 0 else i - 1
                if 0 <= target < clusters:
                    route.append((i * tiles + k, target * tiles + k))
        return lax.ppermute(x, ("cluster", "tile"), route)

    def partner(x, stride):
        route = [(i, i ^ stride) for i in range(clusters) if i ^ stride < clusters]
        return lax.ppermute(x, "cluster", route)

    pts = [points] + [to_tile(points, d) for d in range(1, 4)]
    mate = to_tile(charges, 1)

    halos = []
    for part in range(2):
        start = jnp.where(group == 0, boxes - (part + 1) * pair, part * pair)
        cut = lambda x: lax.dynamic_slice_in_dim(x, start, pair, 0)
        halo_pts = jnp.concatenate([cut(points), cut(pts[1])], axis=2)
        halo_charges = jnp.concatenate([cut(charges), cut(mate)], axis=1)
        halos += [to_halo(halo_pts), to_halo(halo_charges)]

    local_levels = boxes.bit_length() - 1
    leaf_pv = lax.dynamic_slice_in_dim(leaf_pivots, group * half, half, 0)
    pieces = []
    for level in range(local_levels - 1):
        stride = 2**level
        at_level = merge_pivots[::stride, level]
        pieces.append(lax.dynamic_slice_in_dim(at_level, group * (at_level.shape[0] // 2), at_level.shape[0] // 2, 0))
    merge_pv = jnp.concatenate(pieces, axis=0)
    width = probes // tiles
    tree = call(
        tree_kernel,
        jax.ShapeDtypeStruct((4, width + 16, rank), bf16),
        1,
        8,
        [pltpu.VMEM((probes, rank), f32)],
    )(info, *pts, charges, mate, leaf_pv, merge_pv)

    got = [to_tile(tree[d], d) for d in range(1, 4)]
    wide = call(join_kernel, jax.ShapeDtypeStruct((width + 16, rank), bf16), 1, 5)(
        info, tree[0], *got, merge_pivots[0, local_levels - 1][None]
    )

    out_shape = jax.ShapeDtypeStruct((half, 4 * rows, probes), f32)
    total = call(
        near_own_kernel,
        out_shape,
        3,
        6,
        [pltpu.VMEM((boxes, 48, 2 * rows), bf16), pltpu.VMEM((4 * rows, 48), bf16)],
    )(info, near_ids, near_count, *pts, charges, mate)

    levels_above = merge_pivots.shape[1] - local_levels
    for bit in range(levels_above):
        last = bit == levels_above - 1
        other = partner(wide, 2**bit)
        place = (c // 2**bit % 2).astype(jnp.int32)[None]
        shape = (rank, width) if last else (width + 16, rank)
        wide = call(functools.partial(level_kernel, last), jax.ShapeDtypeStruct(shape, bf16), 1, 3)(
            place, wide, other, merge_pivots[0, local_levels + bit][None]
        )

    sums = []
    for part in range(2):
        keep, send = call(
            functools.partial(near_halo_kernel, part),
            (
                jax.ShapeDtypeStruct((pair, rows, probes), f32),
                jax.ShapeDtypeStruct((3, pair, rows, probes), bf16),
            ),
            3,
            5 + 2 * (part + 1),
            [
                pltpu.VMEM((half, 48, 2 * rows), bf16),
                pltpu.VMEM((4 * rows, 48), bf16),
                pltpu.VMEM((4 * rows, probes), f32),
            ],
        )(info, near_ids, near_count, *pts, total, *halos[: 2 * (part + 1)])
        back = [to_tile(send[d - 1], d).astype(f32) for d in range(1, 4)]
        mine = (keep + back[1]).astype(bf16)
        theirs = (back[0] + back[2]).astype(bf16)
        low = jnp.where(group == 0, mine, theirs)
        high = jnp.where(group == 0, theirs, mine)
        sums.append((low, high))
    near_field = jnp.concatenate([sums[1][0], sums[0][0], sums[0][1], sums[1][1]], axis=0)
    return near_field, wide[None]


def solution(mesh):
    return jax.shard_map(
        on_device,
        mesh=mesh,
        in_specs=(
            P("cluster", None, "tile"),
            P("cluster", "tile", None),
            P("cluster", None),
            P("cluster"),
            P("cluster", None),
            P("cluster", None, None),
        ),
        out_specs=(P("cluster", "tile", None), P("cluster", None, "tile")),
        check_vma=False,
    )
```

profile of v0, /device:TPU:21, one launch (start us, length us, event | category | flops | bytes accessed | tf_op | source)
XLA Modules:
  0.0 74.6 jit_solution(640961778714316957)
XLA Ops:
  0.6 0.0 copy-start
  0.6 0.9 %collective-permute-start.2 = (bf16[8,8,128]{2,1,0:T(8,128)(2,1)}, bf16[8,8,128]{2,1,0:T(8,128)(2,1)S(1)}, u32[]{:S(2)}, u32[]{:S(2)}) collective-permute-start(bf16[8,8,128]{2,1,0:T(8,128)(2,1)} %pts0.7), channel_id=1, source_target_pairs={{0,3},{1,2},{2,1},{3,0},{4,7},{5,6},{6,5},{7,4},{8,11},{9,10},{10,... | collective-permute-start | bytes 49160 | tf_op jit(solution)/shard_map/ppermute | solution.py:255
  1.5 1.2 %collective-permute-start.1 = (bf16[8,8,128]{2,1,0:T(8,128)(2,1)}, bf16[8,8,128]{2,1,0:T(8,128)(2,1)S(1)}, u32[]{:S(2)}, u32[]{:S(2)}) collective-permute-start(bf16[8,8,128]{2,1,0:T(8,128)(2,1)} %pts0.7), channel_id=1, source_target_pairs={{0,2},{1,3},{2,0},{3,1},{4,6},{5,7},{6,4},{7,5},{8,10},{9,11},{10,... | collective-permute-start | bytes 49160 | tf_op jit(solution)/shard_map/ppermute | solution.py:255
  2.7 0.1 collective-permute-start
  2.9 0.4 collective-permute-start.3
  3.2 0.7 slice.55
  4.0 0.7 slice.54
  4.7 0.7 constant_dynamic-slice_fusion.6
  5.4 1.0 %constant_dynamic-slice_fusion.4 = (bf16[2,128,256]{2,1,0:T(8,128)(2,1)S(1)}, bf16[2,128,256]{2,1,0:T(8,128)(2,1)S(1)}) fusion(bf16[8,128,256]{2,1,0:T(8,128)(2,1)} %own.3, s32[]{:T(128)S(6)} %select_n.74, s32[]{:T(128)S(6)} %select_n.73), kind=kLoop, calls=%fused_computation.28 | loop fusion | bytes 524296 | tf_op jit(solution)/shard_map/dynamic_slice | solution.py:276
  6.5 0.7 slice_bitcast_fusion.10
  7.2 0.1 pad_add_fusion.1.info
  7.4 1.0 %copy-done.1 = bf16[8,128,256]{2,1,0:T(8,128)(2,1)S(1)} copy-done((bf16[8,128,256]{2,1,0:T(8,128)(2,1)S(1)}, bf16[8,128,256]{2,1,0:T(8,128)(2,1)}, u32[]{:S(2)}) %copy-start.1) | copy-done | bytes 524312
  8.4 0.7 copy-done.3
  9.1 2.9 %shard_map.80 = bf16[4,80,256]{2,1,0:T(8,128)(2,1)S(1)} custom-call(s32[3]{0:T(128)S(1)} %pad_add_fusion.1.info, bf16[8,8,128]{2,1,0:T(8,128)(2,1)S(1)} %copy-done.3, bf16[8,8,128]{2,1,0:T(8,128)(2,1)S(1)} %collective-permute-done.pts1, bf16[8,8,128]{2,1,0:T(8,128)(2,1)S(1)} %collective-permute-done.1.pts2, ...), custom_call_target="tpu_custom_call" | custom-call | tf_op jit(solution)/shard_map/pallas_call | solution.py:290
  12.1 0.4 collective-permute-start.16
  12.5 1.1 %collective-permute-start.15 = (bf16[80,256]{1,0:T(8,128)(2,1)S(1)}, bf16[80,256]{1,0:T(8,128)(2,1)S(1)}, u32[]{:S(2)}, u32[]{:S(2)}) collective-permute-start(bf16[80,256]{1,0:T(8,128)(2,1)S(1)} %get-tuple-element.27), channel_id=1, source_target_pairs={{0,2},{1,3},{2,0},{3,1},{4,6},{5,7},{6,4},{7,5},{8,10},{9,11},{10,... | collective-permute-start | bytes 122888 | tf_op jit(solution)/shard_map/ppermute | solution.py:255
  13.6 0.7 collective-permute-start.14
  14.3 0.7 pad_maximum_fusion.1
  15.0 3.0 %collective-permute-start.5 = (bf16[2,256,256]{2,1,0:T(8,128)(2,1)}, bf16[2,256,256]{2,1,0:T(8,128)(2,1)S(1)}, u32[]{:S(2)}, u32[]{:S(2)}) collective-permute-start(bf16[2,256,256]{2,1,0:T(8,128)(2,1)} %pad_maximum_fusion.1), channel_id=1, source_target_pairs={{0,4},{2,6},{4,8},{5,1},{6,10},{7,3},{8,12},{9,5},{10,14},{11,7},{... | collective-permute-start | bytes 786440 | tf_op jit(solution)/shard_map/ppermute | solution.py:264
  18.0 0.7 pad_maximum_fusion.2
  18.8 2.2 %collective-permute-start.7 = (bf16[2,256,256]{2,1,0:T(8,128)(2,1)}, bf16[2,256,256]{2,1,0:T(8,128)(2,1)}, u32[]{:S(2)}, u32[]{:S(2)}) collective-permute-start(bf16[2,256,256]{2,1,0:T(8,128)(2,1)} %pad_maximum_fusion.2), channel_id=1, source_target_pairs={{0,4},{2,6},{4,8},{5,1},{6,10},{7,3},{8,12},{9,5},{10,14},{11,7},{... | collective-permute-start | bytes 786440 | tf_op jit(solution)/shard_map/ppermute | solution.py:264
  21.0 1.5 %shard_map.81.mine = bf16[80,256]{1,0:T(8,128)(2,1)S(1)} custom-call(s32[3]{0:T(128)S(1)} %pad_add_fusion.1.info, bf16[80,256]{1,0:T(8,128)(2,1)S(1)} %get-tuple-element.29.mine, bf16[80,256]{1,0:T(8,128)(2,1)S(1)} %collective-permute-done.14.got1, bf16[80,256]{1,0:T(8,128)(2,1)S(1)} %collective-permute-done.15.got2, ...), custom_call_target="tpu_custom_call" | custom-call | tf_op jit(solution)/shard_map/pallas_call | solution.py:299
  22.5 1.3 %collective-permute-start.17 = (bf16[80,256]{1,0:T(8,128)(2,1)S(1)}, bf16[80,256]{1,0:T(8,128)(2,1)S(1)}, u32[]{:S(2)}, u32[]{:S(2)}) collective-permute-start(bf16[80,256]{1,0:T(8,128)(2,1)S(1)} %shard_map.81.mine), channel_id=1, source_target_pairs={{0,4},{4,0},{8,12},{12,8},{16,20},{20,16},{24,28},{28,24},{1,5},{5... | collective-permute-start | bytes 122888 | tf_op jit(solution)/shard_map/ppermute | solution.py:268
  23.8 7.9 %collective-permute-done.17.got = bf16[80,256]{1,0:T(8,128)(2,1)S(1)} collective-permute-done((bf16[80,256]{1,0:T(8,128)(2,1)S(1)}, bf16[80,256]{1,0:T(8,128)(2,1)S(1)}, u32[]{:S(2)}, u32[]{:S(2)}) %collective-permute-start.17) | collective-permute-done | bytes 40992 | tf_op jit(solution)/shard_map/ppermute | solution.py:268
  31.7 1.0 %shard_map.82.mine = bf16[80,256]{1,0:T(8,128)(2,1)S(1)} custom-call(s32[1]{0:T(128)} %bitcast.11.info, bf16[80,256]{1,0:T(8,128)(2,1)S(1)} %shard_map.81.mine, bf16[80,256]{1,0:T(8,128)(2,1)S(1)} %collective-permute-done.17.got, s32[1,256]{1,0:T(1,128)S(1)} %get-tuple-element.31.pivots), custom_call_target="tpu_custom_call" | custom-call | tf_op jit(solution)/shard_map/pallas_call | solution.py:318
  32.6 1.4 %collective-permute-start.18 = (bf16[80,256]{1,0:T(8,128)(2,1)S(1)}, bf16[80,256]{1,0:T(8,128)(2,1)S(1)}, u32[]{:S(2)}, u32[]{:S(2)}) collective-permute-start(bf16[80,256]{1,0:T(8,128)(2,1)S(1)} %shard_map.82.mine), channel_id=1, source_target_pairs={{0,8},{4,12},{8,0},{12,4},{16,24},{20,28},{24,16},{28,20},{1,9},{5... | collective-permute-start | bytes 122888 | tf_op jit(solution)/shard_map/ppermute | solution.py:268
  34.0 0.6 pad_maximum_fusion.3
  34.6 1.9 %collective-permute-start.4 = (bf16[2,8,256]{2,1,0:T(8,128)(2,1)}, bf16[2,8,256]{2,1,0:T(8,128)(2,1)S(1)}, u32[]{:S(2)}, u32[]{:S(2)}) collective-permute-start(bf16[2,8,256]{2,1,0:T(8,128)(2,1)} %pad_maximum_fusion.3), channel_id=1, source_target_pairs={{0,4},{2,6},{4,8},{5,1},{6,10},{7,3},{8,12},{9,5},{10,14},{11,7},{... | collective-permute-start | bytes 24584 | tf_op jit(solution)/shard_map/ppermute | solution.py:264
  36.5 1.0 %shard_map.83.mine = bf16[80,256]{1,0:T(8,128)(2,1)S(1)} custom-call(s32[1]{0:T(128)} %bitcast.10.info, bf16[80,256]{1,0:T(8,128)(2,1)S(1)} %shard_map.82.mine, bf16[80,256]{1,0:T(8,128)(2,1)S(1)} %collective-permute-done.18.got, s32[1,256]{1,0:T(1,128)S(1)} %get-tuple-element.33.pivots), custom_call_target="tpu_custom_call" | custom-call | tf_op jit(solution)/shard_map/pallas_call | solution.py:318
  37.5 0.1 collective-permute-start.19
  37.6 0.6 pad_maximum_fusion.4
  38.2 4.4 %collective-permute-start.6 = (bf16[2,8,256]{2,1,0:T(8,128)(2,1)}, bf16[2,8,256]{2,1,0:T(8,128)(2,1)S(1)}, u32[]{:S(2)}, u32[]{:S(2)}) collective-permute-start(bf16[2,8,256]{2,1,0:T(8,128)(2,1)} %pad_maximum_fusion.4), channel_id=1, source_target_pairs={{0,4},{2,6},{4,8},{5,1},{6,10},{7,3},{8,12},{9,5},{10,14},{11,7},{... | collective-permute-start | bytes 24584 | tf_op jit(solution)/shard_map/ppermute | solution.py:264
  42.7 10.2 %shard_map.77.total = f32[4,512,256]{2,1,0:T(8,128)S(1)} custom-call(s32[3]{0:T(128)S(1)} %pad_add_fusion.1.info, s32[8,8]{1,0:T(8,128)S(1)} %copy-done.5, s32[8]{0:T(128)S(1)} %copy-done.6, bf16[8,8,128]{2,1,0:T(8,128)(2,1)S(1)} %copy-done.4, bf16[8,8,128]{2,1,0:T(8,128)(2,1)S(1)} %collective-permute-done.pts1, ...), custom_call_target="tpu_custom_call" | custom-call | tf_op jit(solution)/shard_map/pallas_call | solution.py:304
  52.8 1.8 %shard_map.84 = bf16[256,64]{1,0:T(8,128)(2,1)S(1)} custom-call(s32[1]{0:T(128)} %bitcast.9.info, bf16[80,256]{1,0:T(8,128)(2,1)S(1)} %shard_map.83.mine, bf16[80,256]{1,0:T(8,128)(2,1)} %collective-permute-done.19.got, s32[1,256]{1,0:T(1,128)S(1)} %get-tuple-element.30.pivots), custom_call_target="tpu_custom_call" | custom-call | tf_op jit(solution)/shard_map/pallas_call | solution.py:318
  54.7 0.7 copy.8
  55.4 4.5 %shard_map.78 = (f32[2,128,256]{2,1,0:T(8,128)S(1)}, bf16[3,2,128,256]{3,2,1,0:T(8,128)(2,1)S(1)}) custom-call(s32[3]{0:T(128)S(1)} %pad_add_fusion.1.info, s32[8,8]{1,0:T(8,128)S(1)} %copy-done.5, s32[8]{0:T(128)S(1)} %copy-done.6, bf16[8,8,128]{2,1,0:T(8,128)(2,1)S(1)} %copy-done.4, bf16[8,8,128]{2,1,0:T(8,128)(2,1)S(1)} %collective-permute-done.pts1, ...), custom_call_target="tpu_custom_call" | custom-call | tf_op jit(solution)/shard_map/pallas_call | solution.py:324
  59.9 0.3 collective-permute-start.8
  60.2 2.2 %collective-permute-start.10 = (bf16[2,128,256]{2,1,0:T(8,128)(2,1)S(1)}, bf16[2,128,256]{2,1,0:T(8,128)(2,1)S(1)}, u32[]{:S(2)}, u32[]{:S(2)}) collective-permute-start(bf16[2,128,256]{2,1,0:T(8,128)(2,1)S(1)} %get-tuple-element.24), channel_id=1, source_target_pairs={{0,3},{1,2},{2,1},{3,0},{4,7},{5,6},{6,5},{7,4},{8,11},{9,10},{10,... | collective-permute-start | bytes 393224 | tf_op jit(solution)/shard_map/ppermute | solution.py:255
  62.4 2.5 %shard_map.79 = (f32[2,128,256]{2,1,0:T(8,128)S(1)}, bf16[3,2,128,256]{3,2,1,0:T(8,128)(2,1)S(1)}) custom-call(s32[3]{0:T(128)S(1)} %pad_add_fusion.1.info, s32[8,8]{1,0:T(8,128)S(1)} %copy-done.5, s32[8]{0:T(128)S(1)} %copy-done.6, bf16[8,8,128]{2,1,0:T(8,128)(2,1)S(1)} %copy-done.4, bf16[8,8,128]{2,1,0:T(8,128)(2,1)S(1)} %collective-permute-done.pts1, ...), custom_call_target="tpu_custom_call" | custom-call | tf_op jit(solution)/shard_map/pallas_call | solution.py:324
  64.9 0.3 collective-permute-start.11
  65.2 1.9 %collective-permute-start.13 = (bf16[2,128,256]{2,1,0:T(8,128)(2,1)S(1)}, bf16[2,128,256]{2,1,0:T(8,128)(2,1)S(1)}, u32[]{:S(2)}, u32[]{:S(2)}) collective-permute-start(bf16[2,128,256]{2,1,0:T(8,128)(2,1)S(1)} %get-tuple-element.21), channel_id=1, source_target_pairs={{0,3},{1,2},{2,1},{3,0},{4,7},{5,6},{6,5},{7,4},{8,11},{9,10},{10,... | collective-permute-start | bytes 393224 | tf_op jit(solution)/shard_map/ppermute | solution.py:255
  67.1 0.0 collective-permute-start.12
  67.1 1.5 %collective-permute-done.10 = bf16[2,128,256]{2,1,0:T(8,128)(2,1)S(1)} collective-permute-done((bf16[2,128,256]{2,1,0:T(8,128)(2,1)S(1)}, bf16[2,128,256]{2,1,0:T(8,128)(2,1)S(1)}, u32[]{:S(2)}, u32[]{:S(2)}) %collective-permute-start.10) | collective-permute-done | bytes 131104 | tf_op jit(solution)/shard_map/ppermute | solution.py:255
  68.6 0.1 broadcast_select_fusion.3
  68.7 1.8 %collective-permute-done.11 = bf16[2,128,256]{2,1,0:T(8,128)(2,1)S(1)} collective-permute-done((bf16[2,128,256]{2,1,0:T(8,128)(2,1)S(1)}, bf16[2,128,256]{2,1,0:T(8,128)(2,1)S(1)}, u32[]{:S(2)}, u32[]{:S(2)}) %collective-permute-start.11) | collective-permute-done | bytes 131104 | tf_op jit(solution)/shard_map/ppermute | solution.py:255
  70.5 3.1 %collective-permute-done.13 = bf16[2,128,256]{2,1,0:T(8,128)(2,1)S(1)} collective-permute-done((bf16[2,128,256]{2,1,0:T(8,128)(2,1)S(1)}, bf16[2,128,256]{2,1,0:T(8,128)(2,1)S(1)}, u32[]{:S(2)}, u32[]{:S(2)}) %collective-permute-start.13) | collective-permute-done | bytes 131104 | tf_op jit(solution)/shard_map/ppermute | solution.py:255
  73.7 0.1 broadcast_select_fusion.2
  73.7 0.9 %pad_maximum_fusion = bf16[8,128,256]{2,1,0:T(8,128)(2,1)} fusion(bf16[2,128,256]{2,1,0:T(8,128)(2,1)S(1)} %get-tuple-element.13, bf16[2,128,256]{2,1,0:T(8,128)(2,1)S(1)} %get-tuple-element.15, bf16[2,128,256]{2,1,0:T(8,128)(2,1)S(1)} %get-tuple-element.14, bf16[2,128,256]{2,1,0:T(8,128)(2,1)S(1)} %get-tuple-element.12), kind=kLoop, calls=%fused_computation | loop fusion | flops 786432 | bytes 1048576 | tf_op jit(solution)/shard_map/concatenate | solution.py:344
  (37 shorter events, 0.2 us)
Async XLA Ops:
  0.6 4.0 %copy-start = (s32[8,256]{1,0:T(8,128)S(1)}, s32[8,256]{1,0:T(8,128)}, u32[]{:S(2)}) copy-start(s32[8,256]{1,0:T(8,128)} %param.10) | copy-start | bytes 24580
  0.6 6.7 %collective-permute-start.2 = (bf16[8,8,128]{2,1,0:T(8,128)(2,1)}, bf16[8,8,128]{2,1,0:T(8,128)(2,1)S(1)}, u32[]{:S(2)}, u32[]{:S(2)}) collective-permute-start(bf16[8,8,128]{2,1,0:T(8,128)(2,1)} %pts0.7), channel_id=1, source_target_pairs={{0,3},{1,2},{2,1},{3,0},{4,7},{5,6},{6,5},{7,4},{8,11},{9,10},{10,... | collective-permute-start | bytes 49160 | tf_op jit(solution)/shard_map/ppermute | solution.py:255
  1.5 5.8 %collective-permute-start.1 = (bf16[8,8,128]{2,1,0:T(8,128)(2,1)}, bf16[8,8,128]{2,1,0:T(8,128)(2,1)S(1)}, u32[]{:S(2)}, u32[]{:S(2)}) collective-permute-start(bf16[8,8,128]{2,1,0:T(8,128)(2,1)} %pts0.7), channel_id=1, source_target_pairs={{0,2},{1,3},{2,0},{3,1},{4,6},{5,7},{6,4},{7,5},{8,10},{9,11},{10,... | collective-permute-start | bytes 49160 | tf_op jit(solution)/shard_map/ppermute | solution.py:255
  2.7 4.6 %collective-permute-start = (bf16[8,8,128]{2,1,0:T(8,128)(2,1)}, bf16[8,8,128]{2,1,0:T(8,128)(2,1)S(1)}, u32[]{:S(2)}, u32[]{:S(2)}) collective-permute-start(bf16[8,8,128]{2,1,0:T(8,128)(2,1)} %pts0.7), channel_id=1, source_target_pairs={{0,1},{1,0},{2,3},{3,2},{4,5},{5,4},{6,7},{7,6},{8,9},{9,8},{10,11... | collective-permute-start | bytes 49160 | tf_op jit(solution)/shard_map/ppermute | solution.py:255
  2.9 4.5 %collective-permute-start.3 = (bf16[8,128,256]{2,1,0:T(8,128)(2,1)}, bf16[8,128,256]{2,1,0:T(8,128)(2,1)S(1)}, u32[]{:S(2)}, u32[]{:S(2)}) collective-permute-start(bf16[8,128,256]{2,1,0:T(8,128)(2,1)} %own.3), channel_id=1, source_target_pairs={{0,1},{1,0},{2,3},{3,2},{4,5},{5,4},{6,7},{7,6},{8,9},{9,8},{10,11... | collective-permute-start | bytes 1572872 | tf_op jit(solution)/shard_map/ppermute | solution.py:255
  5.4 37.2 %copy-start.2 = (bf16[8,128,256]{2,1,0:T(8,128)(2,1)S(1)}, bf16[8,128,256]{2,1,0:T(8,128)(2,1)}, u32[]{:S(2)}) copy-start(bf16[8,128,256]{2,1,0:T(8,128)(2,1)} %own.3) | copy-start | bytes 1572868
  5.4 37.2 %copy-start.4 = (bf16[8,8,128]{2,1,0:T(8,128)(2,1)S(1)}, bf16[8,8,128]{2,1,0:T(8,128)(2,1)}, u32[]{:S(2)}) copy-start(bf16[8,8,128]{2,1,0:T(8,128)(2,1)} %pts0.7) | copy-start | bytes 49156
  5.4 37.2 %copy-start.5 = (s32[8,8]{1,0:T(8,128)S(1)}, s32[8,8]{1,0:T(8,128)}, u32[]{:S(2)}) copy-start(s32[8,8]{1,0:T(8,128)} %ids.5) | copy-start | bytes 772
  5.4 37.2 %copy-start.6 = (s32[8]{0:T(128)S(1)}, s32[8]{0:T(128)}, u32[]{:S(2)}) copy-start(s32[8]{0:T(128)} %count.5) | copy-start | bytes 100
  7.3 1.0 %copy-start.1 = (bf16[8,128,256]{2,1,0:T(8,128)(2,1)S(1)}, bf16[8,128,256]{2,1,0:T(8,128)(2,1)}, u32[]{:S(2)}) copy-start(bf16[8,128,256]{2,1,0:T(8,128)(2,1)} %own.3) | copy-start | bytes 1572868
  8.4 0.7 copy-start.3
  12.1 8.9 %collective-permute-start.16 = (bf16[80,256]{1,0:T(8,128)(2,1)S(1)}, bf16[80,256]{1,0:T(8,128)(2,1)S(1)}, u32[]{:S(2)}, u32[]{:S(2)}) collective-permute-start(bf16[80,256]{1,0:T(8,128)(2,1)S(1)} %get-tuple-element.26), channel_id=1, source_target_pairs={{0,3},{1,2},{2,1},{3,0},{4,7},{5,6},{6,5},{7,4},{8,11},{9,10},{10,... | collective-permute-start | bytes 122888 | tf_op jit(solution)/shard_map/ppermute | solution.py:255
  12.5 8.5 %collective-permute-start.15 = (bf16[80,256]{1,0:T(8,128)(2,1)S(1)}, bf16[80,256]{1,0:T(8,128)(2,1)S(1)}, u32[]{:S(2)}, u32[]{:S(2)}) collective-permute-start(bf16[80,256]{1,0:T(8,128)(2,1)S(1)} %get-tuple-element.27), channel_id=1, source_target_pairs={{0,2},{1,3},{2,0},{3,1},{4,6},{5,7},{6,4},{7,5},{8,10},{9,11},{10,... | collective-permute-start | bytes 122888 | tf_op jit(solution)/shard_map/ppermute | solution.py:255
  13.6 7.4 %collective-permute-start.14 = (bf16[80,256]{1,0:T(8,128)(2,1)S(1)}, bf16[80,256]{1,0:T(8,128)(2,1)S(1)}, u32[]{:S(2)}, u32[]{:S(2)}) collective-permute-start(bf16[80,256]{1,0:T(8,128)(2,1)S(1)} %get-tuple-element.28), channel_id=1, source_target_pairs={{0,1},{1,0},{2,3},{3,2},{4,5},{5,4},{6,7},{7,6},{8,9},{9,8},{10,11... | collective-permute-start | bytes 122888 | tf_op jit(solution)/shard_map/ppermute | solution.py:255
  15.0 40.4 %collective-permute-start.5 = (bf16[2,256,256]{2,1,0:T(8,128)(2,1)}, bf16[2,256,256]{2,1,0:T(8,128)(2,1)S(1)}, u32[]{:S(2)}, u32[]{:S(2)}) collective-permute-start(bf16[2,256,256]{2,1,0:T(8,128)(2,1)} %pad_maximum_fusion.1), channel_id=1, source_target_pairs={{0,4},{2,6},{4,8},{5,1},{6,10},{7,3},{8,12},{9,5},{10,14},{11,7},{... | collective-permute-start | bytes 786440 | tf_op jit(solution)/shard_map/ppermute | solution.py:264
  18.8 36.6 %collective-permute-start.7 = (bf16[2,256,256]{2,1,0:T(8,128)(2,1)}, bf16[2,256,256]{2,1,0:T(8,128)(2,1)}, u32[]{:S(2)}, u32[]{:S(2)}) collective-permute-start(bf16[2,256,256]{2,1,0:T(8,128)(2,1)} %pad_maximum_fusion.2), channel_id=1, source_target_pairs={{0,4},{2,6},{4,8},{5,1},{6,10},{7,3},{8,12},{9,5},{10,14},{11,7},{... | collective-permute-start | bytes 786440 | tf_op jit(solution)/shard_map/ppermute | solution.py:264
  22.5 9.2 %collective-permute-start.17 = (bf16[80,256]{1,0:T(8,128)(2,1)S(1)}, bf16[80,256]{1,0:T(8,128)(2,1)S(1)}, u32[]{:S(2)}, u32[]{:S(2)}) collective-permute-start(bf16[80,256]{1,0:T(8,128)(2,1)S(1)} %shard_map.81.mine), channel_id=1, source_target_pairs={{0,4},{4,0},{8,12},{12,8},{16,20},{20,16},{24,28},{28,24},{1,5},{5... | collective-permute-start | bytes 122888 | tf_op jit(solution)/shard_map/ppermute | solution.py:268
  32.6 3.9 %collective-permute-start.18 = (bf16[80,256]{1,0:T(8,128)(2,1)S(1)}, bf16[80,256]{1,0:T(8,128)(2,1)S(1)}, u32[]{:S(2)}, u32[]{:S(2)}) collective-permute-start(bf16[80,256]{1,0:T(8,128)(2,1)S(1)} %shard_map.82.mine), channel_id=1, source_target_pairs={{0,8},{4,12},{8,0},{12,4},{16,24},{20,28},{24,16},{28,20},{1,9},{5... | collective-permute-start | bytes 122888 | tf_op jit(solution)/shard_map/ppermute | solution.py:268
  34.6 20.8 %collective-permute-start.4 = (bf16[2,8,256]{2,1,0:T(8,128)(2,1)}, bf16[2,8,256]{2,1,0:T(8,128)(2,1)S(1)}, u32[]{:S(2)}, u32[]{:S(2)}) collective-permute-start(bf16[2,8,256]{2,1,0:T(8,128)(2,1)} %pad_maximum_fusion.3), channel_id=1, source_target_pairs={{0,4},{2,6},{4,8},{5,1},{6,10},{7,3},{8,12},{9,5},{10,14},{11,7},{... | collective-permute-start | bytes 24584 | tf_op jit(solution)/shard_map/ppermute | solution.py:264
  37.5 15.3 %collective-permute-start.19 = (bf16[80,256]{1,0:T(8,128)(2,1)S(1)}, bf16[80,256]{1,0:T(8,128)(2,1)}, u32[]{:S(2)}, u32[]{:S(2)}) collective-permute-start(bf16[80,256]{1,0:T(8,128)(2,1)S(1)} %shard_map.83.mine), channel_id=1, source_target_pairs={{0,16},{4,20},{8,24},{12,28},{16,0},{20,4},{24,8},{28,12},{1,17},{... | collective-permute-start | bytes 122888 | tf_op jit(solution)/shard_map/ppermute | solution.py:268
  38.2 17.2 %collective-permute-start.6 = (bf16[2,8,256]{2,1,0:T(8,128)(2,1)}, bf16[2,8,256]{2,1,0:T(8,128)(2,1)S(1)}, u32[]{:S(2)}, u32[]{:S(2)}) collective-permute-start(bf16[2,8,256]{2,1,0:T(8,128)(2,1)} %pad_maximum_fusion.4), channel_id=1, source_target_pairs={{0,4},{2,6},{4,8},{5,1},{6,10},{7,3},{8,12},{9,5},{10,14},{11,7},{... | collective-permute-start | bytes 24584 | tf_op jit(solution)/shard_map/ppermute | solution.py:264
  59.9 7.2 %collective-permute-start.8 = (bf16[2,128,256]{2,1,0:T(8,128)(2,1)S(1)}, bf16[2,128,256]{2,1,0:T(8,128)(2,1)S(1)}, u32[]{:S(2)}, u32[]{:S(2)}) collective-permute-start(bf16[2,128,256]{2,1,0:T(8,128)(2,1)S(1)} %get-tuple-element.23), channel_id=1, source_target_pairs={{0,2},{1,3},{2,0},{3,1},{4,6},{5,7},{6,4},{7,5},{8,10},{9,11},{10,... | collective-permute-start | bytes 393224 | tf_op jit(solution)/shard_map/ppermute | solution.py:255
  60.2 8.4 %collective-permute-start.10 = (bf16[2,128,256]{2,1,0:T(8,128)(2,1)S(1)}, bf16[2,128,256]{2,1,0:T(8,128)(2,1)S(1)}, u32[]{:S(2)}, u32[]{:S(2)}) collective-permute-start(bf16[2,128,256]{2,1,0:T(8,128)(2,1)S(1)} %get-tuple-element.24), channel_id=1, source_target_pairs={{0,3},{1,2},{2,1},{3,0},{4,7},{5,6},{6,5},{7,4},{8,11},{9,10},{10,... | collective-permute-start | bytes 393224 | tf_op jit(solution)/shard_map/ppermute | solution.py:255
  62.4 6.3 %collective-permute-start.9 = (bf16[2,128,256]{2,1,0:T(8,128)(2,1)S(1)}, bf16[2,128,256]{2,1,0:T(8,128)(2,1)S(1)}, u32[]{:S(2)}, u32[]{:S(2)}) collective-permute-start(bf16[2,128,256]{2,1,0:T(8,128)(2,1)S(1)} %get-tuple-element.25), channel_id=1, source_target_pairs={{0,1},{1,0},{2,3},{3,2},{4,5},{5,4},{6,7},{7,6},{8,9},{9,8},{10,11... | collective-permute-start | bytes 393224 | tf_op jit(solution)/shard_map/ppermute | solution.py:255
  64.9 5.6 %collective-permute-start.11 = (bf16[2,128,256]{2,1,0:T(8,128)(2,1)S(1)}, bf16[2,128,256]{2,1,0:T(8,128)(2,1)S(1)}, u32[]{:S(2)}, u32[]{:S(2)}) collective-permute-start(bf16[2,128,256]{2,1,0:T(8,128)(2,1)S(1)} %get-tuple-element.20), channel_id=1, source_target_pairs={{0,2},{1,3},{2,0},{3,1},{4,6},{5,7},{6,4},{7,5},{8,10},{9,11},{10,... | collective-permute-start | bytes 393224 | tf_op jit(solution)/shard_map/ppermute | solution.py:255
  65.2 8.5 %collective-permute-start.13 = (bf16[2,128,256]{2,1,0:T(8,128)(2,1)S(1)}, bf16[2,128,256]{2,1,0:T(8,128)(2,1)S(1)}, u32[]{:S(2)}, u32[]{:S(2)}) collective-permute-start(bf16[2,128,256]{2,1,0:T(8,128)(2,1)S(1)} %get-tuple-element.21), channel_id=1, source_target_pairs={{0,3},{1,2},{2,1},{3,0},{4,7},{5,6},{6,5},{7,4},{8,11},{9,10},{10,... | collective-permute-start | bytes 393224 | tf_op jit(solution)/shard_map/ppermute | solution.py:255
  67.1 6.5 %collective-permute-start.12 = (bf16[2,128,256]{2,1,0:T(8,128)(2,1)S(1)}, bf16[2,128,256]{2,1,0:T(8,128)(2,1)S(1)}, u32[]{:S(2)}, u32[]{:S(2)}) collective-permute-start(bf16[2,128,256]{2,1,0:T(8,128)(2,1)S(1)} %get-tuple-element.22), channel_id=1, source_target_pairs={{0,1},{1,0},{2,3},{3,2},{4,5},{5,4},{6,7},{7,6},{8,9},{9,8},{10,11... | collective-permute-start | bytes 393224 | tf_op jit(solution)/shard_map/ppermute | solution.py:255
where the time goes:
time: 75.3 us; the launch traced here: 74.6 us
  Pallas kernels  25.3 us (34%)
  starting transfers between devices  23.6 us (31%)
  waiting for transfers between devices  14.4 us (19%)
  local copies, waits for them, and re-layouts  6.5 us (9%)
  other arithmetic  3.73 us (5%)
  between operations  0.98 us (1%)
    ppermute x4, starting transfers between devices, to_halo(): return lax.ppermute(x, ('cluster', 'tile'), route)  11.4 us
    pallas_call x1, Pallas kernels, on_device(): call(near_own_kernel, out_shape, 3, 6, [pltpu.VMEM((boxes, 48, 2 * rows),...  10.2 us
    ppermute x13, starting transfers between devices, to_tile(): return lax.ppermute(x, 'tile', [(i, i ^ d) for i in range(tiles)])  9.48 us
    ppermute x3, waiting for transfers between devices, partner(): return lax.ppermute(x, 'cluster', route)  7.92 us
    pallas_call x2, Pallas kernels, on_device(): call(functools.partial(near_halo_kernel, part), (jax.ShapeDtypeStruct((pa...  6.97 us
    ppermute x13, waiting for transfers between devices, to_tile(): return lax.ppermute(x, 'tile', [(i, i ^ d) for i in range(tiles)])  6.47 us
    pallas_call x3, Pallas kernels, on_device(): call(functools.partial(level_kernel, last), jax.ShapeDtypeStruct(shape, b...  3.76 us
    pallas_call x1, Pallas kernels, on_device(): call(tree_kernel, jax.ShapeDtypeStruct((4, width + 16, rank), bf16), 1, 8...  2.93 us
  transfers between devices with their start and end apart: 20, of which 4 were waited for; matrix products, arithmetic and copies ran while one was open for 10% of the time, Pallas kernels for 24%

commit v1 on v0

v1 whole, which is shorter than its diff:
```python
import functools
import math

import jax
import jax.numpy as jnp
from jax import lax
from jax.experimental import pallas as pl
from jax.experimental.pallas import tpu as pltpu
from jax.sharding import PartitionSpec as P

SPAN = 4
lengthscale = 0.7
KAPPA = math.log2(math.e) / lengthscale
FLOOR = 1e-30
VMEM_LIMIT = 16 * 1024 * 1024
f32 = jnp.float32
bf16 = jnp.bfloat16
VMEM = pl.BlockSpec(memory_space=pltpu.VMEM)
SMEM = pl.BlockSpec(memory_space=pltpu.SMEM)
ANY = pl.BlockSpec(memory_space=pl.ANY)


def features(coords, centre):
    shifted = (coords - centre) * KAPPA
    high = shifted.astype(bf16).astype(f32)
    low = (shifted - high).astype(bf16).astype(f32)
    both = high + low
    norm = jnp.sum(both * both, axis=0, keepdims=True)
    first = norm.astype(bf16).astype(f32)
    second = (norm - first).astype(bf16).astype(f32)
    third = norm - first - second
    row = lax.broadcasted_iota(jnp.int32, coords.shape, 0)
    one = jnp.ones_like(coords)
    nil = jnp.zeros_like(coords)

    def six(a, b, c, d, e, f):
        out = jnp.where(row == 0, a, jnp.where(row == 1, b, jnp.where(row == 2, c, nil)))
        return jnp.where(row == 3, d, jnp.where(row == 4, e, jnp.where(row == 5, f, out)))

    left = [-2 * high, -2 * high, -2 * low, -2 * low, six(first, second, third, one, one, one), nil]
    right = [high, low, high, low, six(one, one, one, first, second, third), nil]
    return jnp.concatenate(left, axis=0), jnp.concatenate(right, axis=0).astype(bf16)


def kernel_values(squares):
    squares = jnp.maximum(squares, FLOOR)
    return jnp.exp2(-(squares * lax.rsqrt(squares))).astype(bf16)


def dot(a, b):
    return jnp.dot(a, b, preferred_element_type=f32)


def choose(coords, pivots):
    place = lax.broadcasted_iota(jnp.int32, (coords.shape[1], pivots.shape[1]), 0)
    return dot(coords.astype(bf16), jnp.where(place == pivots, 1.0, 0.0).astype(bf16))


def lanes(*parts):
    return jnp.concatenate(parts, axis=1)


def centre_of(coords):
    return jnp.mean(coords.astype(f32), axis=1, keepdims=True)


def position():
    tile = lax.axis_index("tile")
    return lax.axis_index("cluster"), lax.rem(tile, 2), tile


def load_kernel(points, charges, points_out, charges_out):
    points_out[...] = points[...]
    charges_out[...] = charges[...]


def stage_kernel(points, got1, charges, mate, after2, after3, to_send, joined):
    boxes, feat, rows = got1.shape
    joined[:, :rows, :] = charges[...]
    joined[:, rows:, :] = mate[...]
    count = to_send.shape[0]
    start = jnp.where(position()[1] == 0, boxes - count, 0)
    for i in range(count):
        box = start + i
        to_send[i, :rows, :] = charges[box]
        to_send[i, rows : 2 * rows, :] = mate[box]
        coords = lanes(points[box], got1[box]).astype(f32)
        to_send[i, 2 * rows :, :] = jnp.concatenate([coords, jnp.zeros_like(coords)], axis=0).astype(bf16)


def with_coords(weights, coords):
    return jnp.concatenate([weights, coords, jnp.zeros_like(coords)], axis=0).astype(bf16)


def tree_kernel(pts0, pts1, pts2, pts3, joined, leaf_pv, merge_pv, *refs):
    outs, held = refs[:4], refs[4]
    half = leaf_pv.shape[0] // 2
    rows = pts0.shape[2]
    _, group, tile = position()
    centre = centre_of(pts0[half])
    coords, weights = [], []
    for i in range(half):
        box = group * half + i
        whole = lanes(pts0[box], pts1[box], pts2[box], pts3[box]).astype(f32)
        chosen = choose(whole, leaf_pv[pl.ds(box, 1), :] ^ (tile * rows))
        left, _ = features(chosen, centre)
        _, right = features(whole[:, : 2 * rows], centre)
        values = kernel_values(dot(left.T.astype(bf16), right))
        coords.append(chosen)
        weights.append(dot(values, joined[box]))
    level = 0
    while len(coords) > 1:
        next_coords, next_weights = [], []
        for i in range(len(coords) // 2):
            cand = lanes(coords[2 * i], coords[2 * i + 1])
            pair = group * (half // 2) + i * 2**level
            chosen = choose(cand, merge_pv[level, pl.ds(pair, 1), :])
            left, _ = features(chosen, centre)
            _, right = features(cand, centre)
            values = kernel_values(dot(left.T.astype(bf16), right))
            charge = jnp.concatenate([weights[2 * i], weights[2 * i + 1]], axis=0).astype(bf16)
            next_coords.append(chosen)
            next_weights.append(dot(values, charge))
        coords, weights = next_coords, next_weights
        level += 1
    held[...] = weights[0].T
    width = held.shape[0] // 4
    for d, out in enumerate(outs):
        out[...] = with_coords(held[pl.ds(pl.multiple_of((tile ^ d) * width, width), width), :], coords[0])


def merged_pair(ours, theirs, our_coords, their_coords, pivots):
    coords = lanes(our_coords.astype(f32)[:8], their_coords.astype(f32)[:8])
    chosen = choose(coords, pivots)
    across = coords.T
    squares = None
    for f in range(coords.shape[0]):
        diff = across[:, f : f + 1] - chosen[f : f + 1, :]
        squares = diff * diff if squares is None else squares + diff * diff
    values = kernel_values(squares * (KAPPA * KAPPA))
    return dot(lanes(ours, theirs), values), chosen


def join_kernel(level, mine, got1, got2, got3, merge_pv, after, out):
    width = mine.shape[0] - 16
    _, group, _ = position()
    ours = (mine[:width, :].astype(f32) + got2[:width, :].astype(f32)).astype(bf16)
    theirs = (got1[:width, :].astype(f32) + got3[:width, :].astype(f32)).astype(bf16)
    pivots = merge_pv[level, :1, :] ^ (group * mine.shape[1])
    out[...] = with_coords(*merged_pair(ours, theirs, mine[width:, :], got1[width:, :], pivots))


def merge_kernel(level, bit, last, mine, got, merge_pv, after, out):
    width = mine.shape[0] - 16
    upper = lax.rem(lax.div(lax.axis_index("cluster"), 2**bit), 2)
    pivots = merge_pv[level, :1, :] ^ (upper * mine.shape[1])
    merged, chosen = merged_pair(mine[:width, :], got[:width, :], mine[width:, :], got[width:, :], pivots)
    if last:
        out[0] = merged.astype(bf16)
    else:
        out[...] = with_coords(merged, chosen)


def collect(ids, count, base, boxes_of, wanted, place, pad, list_v, list_n):
    found = 0
    for v, box in enumerate(boxes_of):
        used = count[box]
        for slot in range(1, ids.shape[1]):
            n = ids[box, slot] - base
            list_v[found] = v
            list_n[found] = place(n)
            found = found + ((slot < used) & wanted(n)).astype(jnp.int32)
    for i in range(3):
        list_v[found + i] = 0
        list_n[found + i] = pad
    return lax.div(found + 3, 4)


def far_row(right):
    row = lax.broadcasted_iota(jnp.int32, right.shape, 0)
    return jnp.where(row == 35, 1e30, 0.0).astype(bf16)


def near_own_kernel(part, ids, count, pts0, pts1, pts2, pts3, joined, *refs):
    if part == 0:
        after, out, left_ref, right_ref, list_v, list_n = refs
    else:
        right_ref, after, out, left_ref, list_v, list_n = refs
    boxes = joined.shape[0]
    half = boxes // 2
    pair = half // 2
    cluster, group, _ = position()
    centre = centre_of(pts0[half])
    if part == 0:
        for n in range(boxes):
            right_ref[n] = features(lanes(pts0[n], pts1[n]).astype(f32), centre)[1]
        right_ref[boxes] = far_row(right_ref[0])
    order = [group * half + part * pair + v for v in range(pair)]
    for v, box in enumerate(order):
        whole = lanes(pts0[box], pts1[box], pts2[box], pts3[box]).astype(f32)
        left_ref[v] = features(whole, centre)[0].T.astype(bf16)

    def one(v, n):
        return dot(kernel_values(dot(left_ref[v], right_ref[n])), joined[jnp.minimum(n, boxes - 1)])

    for v, box in enumerate(order):
        out[v] = one(v, box)
    groups = collect(
        ids, count, cluster * boxes, order, lambda n: (n >= 0) & (n < boxes), lambda n: n, boxes, list_v, list_n
    )

    def step(i, _):
        for k in range(4):
            v = list_v[4 * i + k]
            out[v] += one(v, list_n[4 * i + k])
        return 0

    lax.fori_loop(0, groups, step, 0)


def near_halo_kernel(
    ids, count, pts0, total0, total1, left0, left1, halo, after, keep, send1, send2, send3, right_ref, left_ref, acc, list_v, list_n
):
    boxes, feat, rows = pts0.shape
    half = boxes // 2
    pair = half // 2
    cluster, group, _ = position()
    centre = centre_of(pts0[half])
    for h in range(half):
        right_ref[h] = features(halo[h, 2 * rows :, :].astype(f32)[:feat], centre)[1]
    right_ref[half] = far_row(right_ref[0])
    order = [group * half + v for v in range(half)]
    for part, (total, left) in enumerate(((total0, left0), (total1, left1))):
        acc[part * pair : (part + 1) * pair] = total[...]
        left_ref[part * pair : (part + 1) * pair] = left[...]
    groups = collect(
        ids,
        count,
        cluster * boxes,
        order,
        lambda n: (n < 0) | (n >= boxes),
        lambda n: jnp.where(group == 0, n + half, n - boxes),
        half,
        list_v,
        list_n,
    )

    def step(i, _):
        for k in range(4):
            v = list_v[4 * i + k]
            h = list_n[4 * i + k]
            values = kernel_values(dot(left_ref[v], right_ref[h]))
            acc[v] += dot(values, halo[jnp.minimum(h, half - 1), : 2 * rows, :])
        return 0

    lax.fori_loop(0, groups, step, 0)
    keep[...] = acc[:, :rows, :]
    for d, send in enumerate((send1, send2, send3)):
        send[...] = acc[:, (d + 1) * rows : (d + 2) * rows, :].astype(bf16)


def finish_kernel(keep, back1, back2, back3, near):
    half = near.shape[0] // 2
    _, group, _ = position()
    near[pl.ds(group * half, half)] = (keep[...] + back2[...].astype(f32)).astype(bf16)
    near[pl.ds((1 - group) * half, half)] = (back1[...].astype(f32) + back3[...].astype(f32)).astype(bf16)


def call(body, out_shape, specs, micros, scratch=()):
    return pl.pallas_call(
        body,
        out_shape=out_shape,
        in_specs=specs,
        out_specs=jax.tree.map(lambda _: VMEM, out_shape),
        scratch_shapes=list(scratch),
        compiler_params=pltpu.CompilerParams(vmem_limit_bytes=VMEM_LIMIT),
        cost_estimate=pl.CostEstimate(flops=int(micros * 1e6), bytes_accessed=1024, transcendentals=0),
    )


def on_device(points, charges, near_ids, near_count, leaf_pivots, merge_pivots):
    boxes, feat, rows = points.shape
    probes = charges.shape[2]
    rank = leaf_pivots.shape[1]
    half = boxes // 2
    pair = half // 2
    tiles = lax.axis_size("tile")
    clusters = lax.axis_size("cluster")
    local_levels = boxes.bit_length() - 1
    levels_above = merge_pivots.shape[1] - local_levels

    def to_tile(x, d):
        return lax.ppermute(x, "tile", [(i, i ^ d) for i in range(tiles)])

    def to_halo(x):
        route = []
        for i in range(clusters):
            for k in range(tiles):
                target = i + 1 if k % 2 == 0 else i - 1
                if 0 <= target < clusters:
                    route.append((i * tiles + k, target * tiles + k))
        return lax.ppermute(x, ("cluster", "tile"), route)

    def partner(x, stride):
        route = [(i, i ^ stride) for i in range(clusters) if i ^ stride < clusters]
        return lax.ppermute(x, "cluster", route)

    def shape(*dims, dtype=bf16):
        return jax.ShapeDtypeStruct(dims, dtype)

    got = [to_tile(points, d) for d in range(1, 4)]
    mate = to_tile(charges, 1)
    points, charges = call(
        load_kernel, (shape(*points.shape), shape(*charges.shape)), [VMEM, VMEM], 1
    )(points, charges)
    to_send, joined = call(
        stage_kernel, (shape(half, 2 * rows + 16, probes), shape(boxes, 2 * rows, probes)), [VMEM] * 4 + [ANY] * 2, 0.5
    )(points, got[0], charges, mate, got[1], got[2])
    halo = to_halo(to_send)
    pts = [points] + got

    merge_pv = jnp.transpose(merge_pivots, (1, 0, 2))
    width = probes // tiles
    wide_shape = shape(width + 16, rank)
    mine, *sends = call(tree_kernel, (wide_shape,) * 4, [VMEM] * 7, 3, [pltpu.VMEM((probes, rank), f32)])(
        *pts, joined, leaf_pivots, merge_pv
    )
    others = [to_tile(sends[d - 1], d) for d in range(1, 4)]

    lists = [pltpu.SMEM((half * near_ids.shape[1] + 4,), jnp.int32)] * 2

    def near_own(part, extra, after):
        out = (shape(pair, 4 * rows, probes, dtype=f32), shape(pair, 4 * rows, 48))
        if part == 0:
            out += (shape(boxes + 1, 48, 2 * rows),)
        specs = [SMEM] * 2 + [VMEM] * (5 + len(extra)) + [ANY]
        return call(functools.partial(near_own_kernel, part), out, specs, 4, lists)(
            near_ids, near_count, *pts, joined, *extra, after
        )

    total0, left0, right = near_own(0, [], mine)
    wide = call(functools.partial(join_kernel, local_levels - 1), wide_shape, [VMEM] * 5 + [ANY], 1.5)(
        mine, *others, merge_pv, left0
    )
    total1, left1 = near_own(1, [right], wide)
    def level_up(bit, wide, after):
        last = bit == levels_above - 1
        out = shape(1, width, rank) if last else wide_shape
        body = functools.partial(merge_kernel, local_levels + bit, bit, last)
        return call(body, out, [VMEM] * 3 + [ANY], 1.5)(wide, partner(wide, 2**bit), merge_pv, after)

    wide = level_up(0, wide, total1)
    keep, *sends = call(
        near_halo_kernel,
        (shape(half, rows, probes, dtype=f32),) + (shape(half, rows, probes),) * 3,
        [SMEM] * 2 + [VMEM] * 6 + [ANY],
        3,
        [
            pltpu.VMEM((half + 1, 48, 2 * rows), bf16),
            pltpu.VMEM((half, 4 * rows, 48), bf16),
            pltpu.VMEM((half, 4 * rows, probes), f32),
        ]
        + lists,
    )(near_ids, near_count, points, total0, total1, left0, left1, halo, wide)
    back = [to_tile(sends[d - 1], d) for d in range(1, 4)]

    for bit in range(1, levels_above):
        wide = level_up(bit, wide, keep)
    near = call(finish_kernel, shape(boxes, rows, probes), [VMEM] * 4, 1.5)(keep, *back)
    return near, jnp.swapaxes(wide, 1, 2)


def solution(mesh):
    return jax.shard_map(
        on_device,
        mesh=mesh,
        in_specs=(
            P("cluster", None, "tile"),
            P("cluster", "tile", None),
            P("cluster", None),
            P("cluster"),
            P("cluster", None),
            P("cluster", None, None),
        ),
        out_specs=(P("cluster", "tile", None), P("cluster", None, "tile")),
        check_vma=False,
    )
```

time: 75.3 us -> 44.4 us (0.59)
  the two profiles are of different devices: /device:TPU:21 before, /device:TPU:0 now
where the time goes in v1:
time: 44.4 us
  starting transfers between devices  19.5 us (44%)
  Pallas kernels  13.4 us (30%)
  waiting for transfers between devices  9.01 us (20%)
  local copies, waits for them, and re-layouts  1.78 us (4%)
  between operations  0.78 us (2%)
    ppermute x3, starting transfers between devices, partner(): return lax.ppermute(x, 'cluster', route)  8.64 us
    ppermute x10, starting transfers between devices, to_tile(): return lax.ppermute(x, 'tile', [(i, i ^ d) for i in range(tiles)])  7.41 us
    ppermute x3, waiting for transfers between devices, partner(): return lax.ppermute(x, 'cluster', route)  6.87 us
    pallas_call x2, Pallas kernels, near_own(): call(functools.partial(near_own_kernel, part), out, specs, 4, lists)  4.35 us
    pallas_call x3, Pallas kernels, level_up(): call(body, out, [VMEM] * 3 + [ANY], 1.5)  3.53 us
    ppermute x1, starting transfers between devices, to_halo(): return lax.ppermute(x, ('cluster', 'tile'), route)  3.43 us
    pallas_call x1, Pallas kernels, on_device(): call(tree_kernel, (wide_shape,) * 4, [VMEM] * 7, 3, [pltpu.VMEM((probes,...  2.41 us
    ppermute x10, waiting for transfers between devices, to_tile(): return lax.ppermute(x, 'tile', [(i, i ^ d) for i in range(tiles)])  2.14 us
  transfers between devices with their start and end apart: 14, of which 6 were waited for; matrix products, arithmetic and copies ran while one was open for 0% of the time, Pallas kernels for 25%

profile of v1, /device:TPU:0, one launch (start us, length us, event | category | flops | bytes accessed | tf_op | source)
XLA Modules:
  0.0 44.4 jit_solution(3432845488476838460)
XLA Ops:
  0.6 0.5 %collective-permute-start.3 = (bf16[8,128,256]{2,1,0:T(8,128)(2,1)}, bf16[8,128,256]{2,1,0:T(8,128)(2,1)S(1)}, u32[]{:S(2)}, u32[]{:S(2)}) collective-permute-start(bf16[8,128,256]{2,1,0:T(8,128)(2,1)} %charges.1), channel_id=1, source_target_pairs={{0,1},{1,0},{2,3},{3,2},{4,5},{5,4},{6,7},{7,6},{8,9},{9,8},{10,11... | collective-permute-start | bytes 1572872 | tf_op jit(solution)/shard_map/ppermute | solution.py:293
  1.1 0.1 collective-permute-start
  1.2 2.9 %collective-permute-start.1 = (bf16[8,8,128]{2,1,0:T(8,128)(2,1)}, bf16[8,8,128]{2,1,0:T(8,128)(2,1)S(1)}, u32[]{:S(2)}, u32[]{:S(2)}) collective-permute-start(bf16[8,8,128]{2,1,0:T(8,128)(2,1)} %points.1), channel_id=1, source_target_pairs={{0,2},{1,3},{2,0},{3,1},{4,6},{5,7},{6,4},{7,5},{8,10},{9,11},{10,... | collective-permute-start | bytes 49160 | tf_op jit(solution)/shard_map/ppermute | solution.py:293
  4.2 0.0 collective-permute-start.2
  4.2 0.0 copy-start.1
  4.2 1.0 %copy-done.1 = bf16[8,128,256]{2,1,0:T(8,128)(2,1)S(1)} copy-done((bf16[8,128,256]{2,1,0:T(8,128)(2,1)S(1)}, bf16[8,128,256]{2,1,0:T(8,128)(2,1)}, u32[]{:S(2)}) %copy-start.1) | copy-done | bytes 524312
  5.2 0.0 copy-start.3
  5.2 0.7 %copy-done.3 = bf16[8,8,128]{2,1,0:T(8,128)(2,1)S(1)} copy-done((bf16[8,8,128]{2,1,0:T(8,128)(2,1)S(1)}, bf16[8,8,128]{2,1,0:T(8,128)(2,1)}, u32[]{:S(2)}) %copy-start.3) | copy-done | bytes 16408
  6.0 0.0 collective-permute-done.got1.pts1
  6.0 0.1 collective-permute-done.1.after2.pts2
  6.1 1.6 %collective-permute-done.2.after3.pts3 = bf16[8,8,128]{2,1,0:T(8,128)(2,1)S(1)} collective-permute-done((bf16[8,8,128]{2,1,0:T(8,128)(2,1)}, bf16[8,8,128]{2,1,0:T(8,128)(2,1)S(1)}, u32[]{:S(2)}, u32[]{:S(2)}) %collective-permute-start.2) | collective-permute-done | bytes 16416 | tf_op jit(solution)/shard_map/ppermute | solution.py:293
  7.7 0.0 collective-permute-done.3.mate
  7.7 0.0 copy-start
  7.7 0.1 shard_map.78
  7.8 3.4 %collective-permute-start.7 = (bf16[4,272,256]{2,1,0:T(8,128)(2,1)S(1)}, bf16[4,272,256]{2,1,0:T(8,128)(2,1)S(1)}, u32[]{:S(2)}, u32[]{:S(2)}) collective-permute-start(bf16[4,272,256]{2,1,0:T(8,128)(2,1)S(1)} %get-tuple-element.31), channel_id=1, source_target_pairs={{0,4},{2,6},{4,8},{5,1},{6,10},{7,3},{8,12},{9,5},{10,14},{11,7},{... | collective-permute-start | bytes 1671176 | tf_op jit(solution)/shard_map/ppermute | solution.py:302
  11.3 0.0 copy-done
  11.3 0.0 copy-done.4
  11.3 2.4 %shard_map.79 = (bf16[80,256]{1,0:T(8,128)(2,1)S(1)}, bf16[80,256]{1,0:T(8,128)(2,1)S(1)}, bf16[80,256]{1,0:T(8,128)(2,1)S(1)}, bf16[80,256]{1,0:T(8,128)(2,1)S(1)}) custom-call(bf16[8,8,128]{2,1,0:T(8,128)(2,1)S(1)} %get-tuple-element.19.points.pts0, bf16[8,8,128]{2,1,0:T(8,128)(2,1)S(1)} %collective-permute-done.got1.pts1, ...), custom_call_target="tpu_custom_call" | custom-call | flops 3000000 | bytes 1024 | tf_op jit(solution)/shard_map/pallas_call | solution.py:325
  13.7 0.0 copy-start.2
  13.7 0.1 collective-permute-start.4
  13.8 0.6 %collective-permute-start.5 = (bf16[80,256]{1,0:T(8,128)(2,1)S(1)}, bf16[80,256]{1,0:T(8,128)(2,1)S(1)}, u32[]{:S(2)}, u32[]{:S(2)}) collective-permute-start(bf16[80,256]{1,0:T(8,128)(2,1)S(1)} %get-tuple-element.26), channel_id=1, source_target_pairs={{0,2},{1,3},{2,0},{3,1},{4,6},{5,7},{6,4},{7,5},{8,10},{9,11},{10,... | collective-permute-start | bytes 122888 | tf_op jit(solution)/shard_map/ppermute | solution.py:293
  14.4 1.2 %collective-permute-start.6 = (bf16[80,256]{1,0:T(8,128)(2,1)S(1)}, bf16[80,256]{1,0:T(8,128)(2,1)S(1)}, u32[]{:S(2)}, u32[]{:S(2)}) collective-permute-start(bf16[80,256]{1,0:T(8,128)(2,1)S(1)} %get-tuple-element.27), channel_id=1, source_target_pairs={{0,3},{1,2},{2,1},{3,0},{4,7},{5,6},{6,5},{7,4},{8,11},{9,10},{10,... | collective-permute-start | bytes 122888 | tf_op jit(solution)/shard_map/ppermute | solution.py:293
  15.6 0.0 copy-done.2
  15.7 0.0 copy-done.5
  15.7 2.2 %shard_map.80 = (f32[2,512,256]{2,1,0:T(8,128)S(1)}, bf16[2,512,48]{2,1,0:T(8,128)(2,1)S(1)}, bf16[9,48,256]{2,1,0:T(8,128)(2,1)S(1)}) custom-call(s32[8,8]{1,0:T(8,128)S(1)} %copy-done.2, s32[8]{0:T(128)S(1)} %copy-done.5, bf16[8,8,128]{2,1,0:T(8,128)(2,1)S(1)} %get-tuple-element.19.points.pts0, bf16[8,8,128]{2,1,0:T(8,128)(2,1)S(1)} %collective-permute-done.got1.pts1, ...), custom_call_target="tpu_custom_call" | custom-call | flops 4000000 | bytes 1024 | tf_op jit(solution)/shard_map/pallas_call | solution.py:337
  17.8 0.0 collective-permute-done.4.got1
  17.9 0.4 collective-permute-done.5.got2
  18.3 0.0 collective-permute-done.6.got3
  18.3 1.0 %shard_map.81.refs_1_.mine = bf16[80,256]{1,0:T(8,128)(2,1)S(1)} custom-call(bf16[80,256]{1,0:T(8,128)(2,1)S(1)} %get-tuple-element.22.refs_0_.mine, bf16[80,256]{1,0:T(8,128)(2,1)S(1)} %collective-permute-done.4.got1, bf16[80,256]{1,0:T(8,128)(2,1)S(1)} %collective-permute-done.5.got2, bf16[80,256]{1,0:T(8,128)(2,1)S(1)} %collective-permute-done.6.got3, ...), custom_call_target="tpu_custom_call" | custom-call | flops 1500000 | bytes 1024 | tf_op jit(solution)/shard_map/pallas_call | solution.py:342
  19.3 1.6 %collective-permute-start.8 = (bf16[80,256]{1,0:T(8,128)(2,1)S(1)}, bf16[80,256]{1,0:T(8,128)(2,1)S(1)}, u32[]{:S(2)}, u32[]{:S(2)}) collective-permute-start(bf16[80,256]{1,0:T(8,128)(2,1)S(1)} %shard_map.81.refs_1_.mine), channel_id=1, source_target_pairs={{0,4},{4,0},{8,12},{12,8},{16,20},{20,16},{24,28},{28,24},{1,5},{5... | collective-permute-start | bytes 122888 | tf_op jit(solution)/shard_map/ppermute | solution.py:306
  20.8 2.2 %shard_map.82 = (f32[2,512,256]{2,1,0:T(8,128)S(1)}, bf16[2,512,48]{2,1,0:T(8,128)(2,1)S(1)}) custom-call(s32[8,8]{1,0:T(8,128)S(1)} %copy-done.2, s32[8]{0:T(128)S(1)} %copy-done.5, bf16[8,8,128]{2,1,0:T(8,128)(2,1)S(1)} %get-tuple-element.19.points.pts0, bf16[8,8,128]{2,1,0:T(8,128)(2,1)S(1)} %collective-permute-done.got1.pts1, ...), custom_call_target="tpu_custom_call" | custom-call | flops 4000000 | bytes 1024 | tf_op jit(solution)/shard_map/pallas_call | solution.py:337
  23.0 2.1 %collective-permute-done.8.got = bf16[80,256]{1,0:T(8,128)(2,1)S(1)} collective-permute-done((bf16[80,256]{1,0:T(8,128)(2,1)S(1)}, bf16[80,256]{1,0:T(8,128)(2,1)S(1)}, u32[]{:S(2)}, u32[]{:S(2)}) %collective-permute-start.8) | collective-permute-done | bytes 40992 | tf_op jit(solution)/shard_map/ppermute | solution.py:306
  25.1 1.0 %shard_map.83.after.mine = bf16[80,256]{1,0:T(8,128)(2,1)S(1)} custom-call(bf16[80,256]{1,0:T(8,128)(2,1)S(1)} %shard_map.81.refs_1_.mine, bf16[80,256]{1,0:T(8,128)(2,1)S(1)} %collective-permute-done.8.got, s32[6,4,256]{2,1,0:T(4,128)S(1)} %bitcast.4, f32[2,512,256]{2,1,0:T(8,128)S(1)} %get-tuple-element.29.after.total1), custom_call_target="tpu_custom_call" | custom-call | flops 1500000 | bytes 1024 | tf_op jit(solution)/shard_map/pallas_call | solution.py:350
  26.1 0.0 collective-permute-done.7.halo
  26.1 1.1 %shard_map.84 = (f32[4,128,256]{2,1,0:T(8,128)S(1)}, bf16[4,128,256]{2,1,0:T(8,128)(2,1)S(1)}, bf16[4,128,256]{2,1,0:T(8,128)(2,1)S(1)}, bf16[4,128,256]{2,1,0:T(8,128)(2,1)S(1)}) custom-call(s32[8,8]{1,0:T(8,128)S(1)} %copy-done.2, s32[8]{0:T(128)S(1)} %copy-done.5, bf16[8,8,128]{2,1,0:T(8,128)(2,1)S(1)} %get-tuple-element.19.points.pts0, ...), custom_call_target="tpu_custom_call" | custom-call | flops 3000000 | bytes 1024 | tf_op jit(solution)/shard_map/pallas_call | solution.py:353
  27.1 0.1 collective-permute-start.9
  27.2 0.6 %collective-permute-start.10 = (bf16[4,128,256]{2,1,0:T(8,128)(2,1)S(1)}, bf16[4,128,256]{2,1,0:T(8,128)(2,1)S(1)}, u32[]{:S(2)}, u32[]{:S(2)}) collective-permute-start(bf16[4,128,256]{2,1,0:T(8,128)(2,1)S(1)} %get-tuple-element.34), channel_id=1, source_target_pairs={{0,2},{1,3},{2,0},{3,1},{4,6},{5,7},{6,4},{7,5},{8,10},{9,11},{10,... | collective-permute-start | bytes 786440 | tf_op jit(solution)/shard_map/ppermute | solution.py:293
  27.8 1.2 %collective-permute-start.11 = (bf16[4,128,256]{2,1,0:T(8,128)(2,1)S(1)}, bf16[4,128,256]{2,1,0:T(8,128)(2,1)S(1)}, u32[]{:S(2)}, u32[]{:S(2)}) collective-permute-start(bf16[4,128,256]{2,1,0:T(8,128)(2,1)S(1)} %get-tuple-element.35), channel_id=1, source_target_pairs={{0,3},{1,2},{2,1},{3,0},{4,7},{5,6},{6,5},{7,4},{8,11},{9,10},{10,... | collective-permute-start | bytes 786440 | tf_op jit(solution)/shard_map/ppermute | solution.py:293
  29.1 2.4 %collective-permute-start.12 = (bf16[80,256]{1,0:T(8,128)(2,1)S(1)}, bf16[80,256]{1,0:T(8,128)(2,1)S(1)}, u32[]{:S(2)}, u32[]{:S(2)}) collective-permute-start(bf16[80,256]{1,0:T(8,128)(2,1)S(1)} %shard_map.83.after.mine), channel_id=1, source_target_pairs={{0,8},{4,12},{8,0},{12,4},{16,24},{20,28},{24,16},{28,20},{1,9},{5... | collective-permute-start | bytes 122888 | tf_op jit(solution)/shard_map/ppermute | solution.py:306
  31.5 2.1 %collective-permute-done.12.got = bf16[80,256]{1,0:T(8,128)(2,1)S(1)} collective-permute-done((bf16[80,256]{1,0:T(8,128)(2,1)S(1)}, bf16[80,256]{1,0:T(8,128)(2,1)S(1)}, u32[]{:S(2)}, u32[]{:S(2)}) %collective-permute-start.12) | collective-permute-done | bytes 40992 | tf_op jit(solution)/shard_map/ppermute | solution.py:306
  33.6 1.0 %shard_map.86.mine = bf16[80,256]{1,0:T(8,128)(2,1)S(1)} custom-call(bf16[80,256]{1,0:T(8,128)(2,1)S(1)} %shard_map.83.after.mine, bf16[80,256]{1,0:T(8,128)(2,1)S(1)} %collective-permute-done.12.got, s32[6,4,256]{2,1,0:T(4,128)S(1)} %bitcast.5, f32[4,128,256]{2,1,0:T(8,128)S(1)} %get-tuple-element.32.keep.after), custom_call_target="tpu_custom_call" | custom-call | flops 1500000 | bytes 1024 | tf_op jit(solution)/shard_map/pallas_call | solution.py:350
  34.5 4.7 %collective-permute-start.13 = (bf16[80,256]{1,0:T(8,128)(2,1)S(1)}, bf16[80,256]{1,0:T(8,128)(2,1)S(1)}, u32[]{:S(2)}, u32[]{:S(2)}) collective-permute-start(bf16[80,256]{1,0:T(8,128)(2,1)S(1)} %shard_map.86.mine), channel_id=1, source_target_pairs={{0,16},{4,20},{8,24},{12,28},{16,0},{20,4},{24,8},{28,12},{1,17},{... | collective-permute-start | bytes 122888 | tf_op jit(solution)/shard_map/ppermute | solution.py:306
  39.2 2.7 %collective-permute-done.13.got = bf16[80,256]{1,0:T(8,128)(2,1)S(1)} collective-permute-done((bf16[80,256]{1,0:T(8,128)(2,1)S(1)}, bf16[80,256]{1,0:T(8,128)(2,1)S(1)}, u32[]{:S(2)}, u32[]{:S(2)}) %collective-permute-start.13) | collective-permute-done | bytes 40992 | tf_op jit(solution)/shard_map/ppermute | solution.py:306
  41.9 1.6 %shard_map.87 = bf16[1,64,256]{2,1,0:T(8,128)(2,1)} custom-call(bf16[80,256]{1,0:T(8,128)(2,1)S(1)} %shard_map.86.mine, bf16[80,256]{1,0:T(8,128)(2,1)S(1)} %collective-permute-done.13.got, s32[6,4,256]{2,1,0:T(4,128)S(1)} %bitcast.6, f32[4,128,256]{2,1,0:T(8,128)S(1)} %get-tuple-element.32.keep.after), custom_call_target="tpu_custom_call" | custom-call | flops 1500000 | bytes 1024 | tf_op jit(solution)/shard_map/pallas_call | solution.py:350
  43.5 0.0 collective-permute-done.9.back1
  43.5 0.0 collective-permute-done.10.back2
  43.5 0.0 collective-permute-done.11.back3
  43.5 0.9 %shard_map.85 = bf16[8,128,256]{2,1,0:T(8,128)(2,1)} custom-call(f32[4,128,256]{2,1,0:T(8,128)S(1)} %get-tuple-element.32.keep.after, bf16[4,128,256]{2,1,0:T(8,128)(2,1)S(1)} %collective-permute-done.9.back1, bf16[4,128,256]{2,1,0:T(8,128)(2,1)S(1)} %collective-permute-done.10.back2, bf16[4,128,256]{2,1,0:T(8,128)(2,1)S(1)} %collective-permute-done.11.back3), custom_call_target="tpu_custom_call" | custom-call | flops 1500000 | bytes 1024 | tf_op jit(solution)/shard_map/pallas_call | solution.py:369
  (3 shorter events, 0.0 us)
Async XLA Ops:
  0.6 7.1 %collective-permute-start.3 = (bf16[8,128,256]{2,1,0:T(8,128)(2,1)}, bf16[8,128,256]{2,1,0:T(8,128)(2,1)S(1)}, u32[]{:S(2)}, u32[]{:S(2)}) collective-permute-start(bf16[8,128,256]{2,1,0:T(8,128)(2,1)} %charges.1), channel_id=1, source_target_pairs={{0,1},{1,0},{2,3},{3,2},{4,5},{5,4},{6,7},{7,6},{8,9},{9,8},{10,11... | collective-permute-start | bytes 1572872 | tf_op jit(solution)/shard_map/ppermute | solution.py:293
  1.1 4.8 %collective-permute-start = (bf16[8,8,128]{2,1,0:T(8,128)(2,1)}, bf16[8,8,128]{2,1,0:T(8,128)(2,1)S(1)}, u32[]{:S(2)}, u32[]{:S(2)}) collective-permute-start(bf16[8,8,128]{2,1,0:T(8,128)(2,1)} %points.1), channel_id=1, source_target_pairs={{0,1},{1,0},{2,3},{3,2},{4,5},{5,4},{6,7},{7,6},{8,9},{9,8},{10,11... | collective-permute-start | bytes 49160 | tf_op jit(solution)/shard_map/ppermute | solution.py:293
  1.2 4.9 %collective-permute-start.1 = (bf16[8,8,128]{2,1,0:T(8,128)(2,1)}, bf16[8,8,128]{2,1,0:T(8,128)(2,1)S(1)}, u32[]{:S(2)}, u32[]{:S(2)}) collective-permute-start(bf16[8,8,128]{2,1,0:T(8,128)(2,1)} %points.1), channel_id=1, source_target_pairs={{0,2},{1,3},{2,0},{3,1},{4,6},{5,7},{6,4},{7,5},{8,10},{9,11},{10,... | collective-permute-start | bytes 49160 | tf_op jit(solution)/shard_map/ppermute | solution.py:293
  4.2 3.5 %collective-permute-start.2 = (bf16[8,8,128]{2,1,0:T(8,128)(2,1)}, bf16[8,8,128]{2,1,0:T(8,128)(2,1)S(1)}, u32[]{:S(2)}, u32[]{:S(2)}) collective-permute-start(bf16[8,8,128]{2,1,0:T(8,128)(2,1)} %points.1), channel_id=1, source_target_pairs={{0,3},{1,2},{2,1},{3,0},{4,7},{5,6},{6,5},{7,4},{8,11},{9,10},{10,... | collective-permute-start | bytes 49160 | tf_op jit(solution)/shard_map/ppermute | solution.py:293
  4.2 1.0 %copy-start.1 = (bf16[8,128,256]{2,1,0:T(8,128)(2,1)S(1)}, bf16[8,128,256]{2,1,0:T(8,128)(2,1)}, u32[]{:S(2)}) copy-start(bf16[8,128,256]{2,1,0:T(8,128)(2,1)} %charges.1) | copy-start | bytes 1572868
  5.2 0.7 %copy-start.3 = (bf16[8,8,128]{2,1,0:T(8,128)(2,1)S(1)}, bf16[8,8,128]{2,1,0:T(8,128)(2,1)}, u32[]{:S(2)}) copy-start(bf16[8,8,128]{2,1,0:T(8,128)(2,1)} %points.1) | copy-start | bytes 49156
  7.7 3.6 %copy-start = (s32[4,6,256]{2,0,1:T(4,128)S(1)}, s32[4,6,256]{2,0,1:T(4,128)}, u32[]{:S(2)}) copy-start(s32[4,6,256]{2,0,1:T(4,128)} %param.11) | copy-start | bytes 73732
  7.7 3.6 %copy-start.4 = (s32[8,256]{1,0:T(8,128)S(1)}, s32[8,256]{1,0:T(8,128)}, u32[]{:S(2)}) copy-start(s32[8,256]{1,0:T(8,128)} %leaf_pv.1) | copy-start | bytes 24580
  7.8 18.3 %collective-permute-start.7 = (bf16[4,272,256]{2,1,0:T(8,128)(2,1)S(1)}, bf16[4,272,256]{2,1,0:T(8,128)(2,1)S(1)}, u32[]{:S(2)}, u32[]{:S(2)}) collective-permute-start(bf16[4,272,256]{2,1,0:T(8,128)(2,1)S(1)} %get-tuple-element.31), channel_id=1, source_target_pairs={{0,4},{2,6},{4,8},{5,1},{6,10},{7,3},{8,12},{9,5},{10,14},{11,7},{... | collective-permute-start | bytes 1671176 | tf_op jit(solution)/shard_map/ppermute | solution.py:302
  13.7 2.0 %copy-start.2 = (s32[8,8]{1,0:T(8,128)S(1)}, s32[8,8]{1,0:T(8,128)}, u32[]{:S(2)}) copy-start(s32[8,8]{1,0:T(8,128)} %ids.5) | copy-start | bytes 772
  13.7 4.1 %collective-permute-start.4 = (bf16[80,256]{1,0:T(8,128)(2,1)S(1)}, bf16[80,256]{1,0:T(8,128)(2,1)S(1)}, u32[]{:S(2)}, u32[]{:S(2)}) collective-permute-start(bf16[80,256]{1,0:T(8,128)(2,1)S(1)} %get-tuple-element.25), channel_id=1, source_target_pairs={{0,1},{1,0},{2,3},{3,2},{4,5},{5,4},{6,7},{7,6},{8,9},{9,8},{10,11... | collective-permute-start | bytes 122888 | tf_op jit(solution)/shard_map/ppermute | solution.py:293
  13.8 4.5 %collective-permute-start.5 = (bf16[80,256]{1,0:T(8,128)(2,1)S(1)}, bf16[80,256]{1,0:T(8,128)(2,1)S(1)}, u32[]{:S(2)}, u32[]{:S(2)}) collective-permute-start(bf16[80,256]{1,0:T(8,128)(2,1)S(1)} %get-tuple-element.26), channel_id=1, source_target_pairs={{0,2},{1,3},{2,0},{3,1},{4,6},{5,7},{6,4},{7,5},{8,10},{9,11},{10,... | collective-permute-start | bytes 122888 | tf_op jit(solution)/shard_map/ppermute | solution.py:293
  14.4 1.3 %copy-start.5 = (s32[8]{0:T(128)S(1)}, s32[8]{0:T(128)}, u32[]{:S(2)}) copy-start(s32[8]{0:T(128)} %count.5) | copy-start | bytes 100
  14.4 3.9 %collective-permute-start.6 = (bf16[80,256]{1,0:T(8,128)(2,1)S(1)}, bf16[80,256]{1,0:T(8,128)(2,1)S(1)}, u32[]{:S(2)}, u32[]{:S(2)}) collective-permute-start(bf16[80,256]{1,0:T(8,128)(2,1)S(1)} %get-tuple-element.27), channel_id=1, source_target_pairs={{0,3},{1,2},{2,1},{3,0},{4,7},{5,6},{6,5},{7,4},{8,11},{9,10},{10,... | collective-permute-start | bytes 122888 | tf_op jit(solution)/shard_map/ppermute | solution.py:293
  19.3 5.8 %collective-permute-start.8 = (bf16[80,256]{1,0:T(8,128)(2,1)S(1)}, bf16[80,256]{1,0:T(8,128)(2,1)S(1)}, u32[]{:S(2)}, u32[]{:S(2)}) collective-permute-start(bf16[80,256]{1,0:T(8,128)(2,1)S(1)} %shard_map.81.refs_1_.mine), channel_id=1, source_target_pairs={{0,4},{4,0},{8,12},{12,8},{16,20},{20,16},{24,28},{28,24},{1,5},{5... | collective-permute-start | bytes 122888 | tf_op jit(solution)/shard_map/ppermute | solution.py:306
  27.1 16.3 %collective-permute-start.9 = (bf16[4,128,256]{2,1,0:T(8,128)(2,1)S(1)}, bf16[4,128,256]{2,1,0:T(8,128)(2,1)S(1)}, u32[]{:S(2)}, u32[]{:S(2)}) collective-permute-start(bf16[4,128,256]{2,1,0:T(8,128)(2,1)S(1)} %get-tuple-element.33), channel_id=1, source_target_pairs={{0,1},{1,0},{2,3},{3,2},{4,5},{5,4},{6,7},{7,6},{8,9},{9,8},{10,11... | collective-permute-start | bytes 786440 | tf_op jit(solution)/shard_map/ppermute | solution.py:293
  27.2 16.3 %collective-permute-start.10 = (bf16[4,128,256]{2,1,0:T(8,128)(2,1)S(1)}, bf16[4,128,256]{2,1,0:T(8,128)(2,1)S(1)}, u32[]{:S(2)}, u32[]{:S(2)}) collective-permute-start(bf16[4,128,256]{2,1,0:T(8,128)(2,1)S(1)} %get-tuple-element.34), channel_id=1, source_target_pairs={{0,2},{1,3},{2,0},{3,1},{4,6},{5,7},{6,4},{7,5},{8,10},{9,11},{10,... | collective-permute-start | bytes 786440 | tf_op jit(solution)/shard_map/ppermute | solution.py:293
  27.8 15.7 %collective-permute-start.11 = (bf16[4,128,256]{2,1,0:T(8,128)(2,1)S(1)}, bf16[4,128,256]{2,1,0:T(8,128)(2,1)S(1)}, u32[]{:S(2)}, u32[]{:S(2)}) collective-permute-start(bf16[4,128,256]{2,1,0:T(8,128)(2,1)S(1)} %get-tuple-element.35), channel_id=1, source_target_pairs={{0,3},{1,2},{2,1},{3,0},{4,7},{5,6},{6,5},{7,4},{8,11},{9,10},{10,... | collective-permute-start | bytes 786440 | tf_op jit(solution)/shard_map/ppermute | solution.py:293
  29.1 4.5 %collective-permute-start.12 = (bf16[80,256]{1,0:T(8,128)(2,1)S(1)}, bf16[80,256]{1,0:T(8,128)(2,1)S(1)}, u32[]{:S(2)}, u32[]{:S(2)}) collective-permute-start(bf16[80,256]{1,0:T(8,128)(2,1)S(1)} %shard_map.83.after.mine), channel_id=1, source_target_pairs={{0,8},{4,12},{8,0},{12,4},{16,24},{20,28},{24,16},{28,20},{1,9},{5... | collective-permute-start | bytes 122888 | tf_op jit(solution)/shard_map/ppermute | solution.py:306
  34.5 7.4 %collective-permute-start.13 = (bf16[80,256]{1,0:T(8,128)(2,1)S(1)}, bf16[80,256]{1,0:T(8,128)(2,1)S(1)}, u32[]{:S(2)}, u32[]{:S(2)}) collective-permute-start(bf16[80,256]{1,0:T(8,128)(2,1)S(1)} %shard_map.86.mine), channel_id=1, source_target_pairs={{0,16},{4,20},{8,24},{12,28},{16,0},{20,4},{24,8},{28,12},{1,17},{... | collective-permute-start | bytes 122888 | tf_op jit(solution)/shard_map/ppermute | solution.py:306

commit v2 on v1

--- a/solution.py
+++ b/solution.py
@@ -12,6 +12,7 @@
 lengthscale = 0.7
 KAPPA = math.log2(math.e) / lengthscale
 FLOOR = 1e-30
+COST = dict(load=0.001, stage=0.001, tree=3, own=1, join=1, merge=1, halo=5, finish=0.001)
 VMEM_LIMIT = 16 * 1024 * 1024
 f32 = jnp.float32
 bf16 = jnp.bfloat16
@@ -69,12 +70,11 @@
     return lax.axis_index("cluster"), lax.rem(tile, 2), tile
 
 
-def load_kernel(points, charges, points_out, charges_out):
-    points_out[...] = points[...]
-    charges_out[...] = charges[...]
-
-
-def stage_kernel(points, got1, charges, mate, after2, after3, to_send, joined):
+def load_kernel(charges, out):
+    out[...] = charges[...]
+
+
+def stage_kernel(points, got1, charges, mate, after, to_send, joined):
     boxes, feat, rows = got1.shape
     joined[:, :rows, :] = charges[...]
     joined[:, rows:, :] = mate[...]
@@ -150,20 +150,41 @@
     out[...] = with_coords(*merged_pair(ours, theirs, mine[width:, :], got1[width:, :], pivots))
 
 
-def merge_kernel(level, bit, last, mine, got, merge_pv, after, out):
+def upper_half(bit):
+    return lax.rem(lax.div(lax.axis_index("cluster"), 2**bit), 2)
+
+
+def merge_kernel(level, bit, mine, got, merge_pv, after, out):
     width = mine.shape[0] - 16
-    upper = lax.rem(lax.div(lax.axis_index("cluster"), 2**bit), 2)
-    pivots = merge_pv[level, :1, :] ^ (upper * mine.shape[1])
+    pivots = merge_pv[level, :1, :] ^ (upper_half(bit) * mine.shape[1])
     merged, chosen = merged_pair(mine[:width, :], got[:width, :], mine[width:, :], got[width:, :], pivots)
-    if last:
-        out[0] = merged.astype(bf16)
-    else:
-        out[...] = with_coords(merged, chosen)
-
-
-def collect(ids, count, base, boxes_of, wanted, place, pad, list_v, list_n):
+    ahead = merge_pv[level + 1, :1, :]
+    row = lax.broadcasted_iota(jnp.int32, chosen.shape, 0)
+    digits = jnp.where(row == 0, ahead & 255, jnp.where(row == 1, ahead >> 8, 0)).astype(f32)
+    out[...] = jnp.concatenate([merged, chosen, digits], axis=0).astype(bf16)
+
+
+def top_kernel(level, bit, mine, got1, got2, got3, merge_pv, out):
+    width, rank = mine.shape[0] - 16, mine.shape[1]
+    flip = upper_half(bit) * rank
+    digits = got2[width:, :].astype(f32)[8:].astype(jnp.int32)
+    pairs = []
+    for left, right, pivots in (
+        (mine, got1, merge_pv[level, :1, :]),
+        (got2, got3, digits[0:1] + 256 * digits[1:2]),
+    ):
+        merged, chosen = merged_pair(
+            left[:width, :], right[:width, :], left[width:, :], right[width:, :], pivots ^ flip
+        )
+        pairs.append((merged.astype(bf16), chosen))
+    (ours, our_coords), (theirs, their_coords) = pairs
+    pivots = merge_pv[level + 1, :1, :] ^ (upper_half(bit + 1) * rank)
+    out[...] = merged_pair(ours, theirs, our_coords, their_coords, pivots)[0].astype(bf16)
+
+
+def collect(ids, count, base, slots_of, boxes_of, wanted, place, pad, list_v, list_n):
     found = 0
-    for v, box in enumerate(boxes_of):
+    for v, box in zip(slots_of, boxes_of):
         used = count[box]
         for slot in range(1, ids.shape[1]):
             n = ids[box, slot] - base
@@ -171,9 +192,26 @@
             list_n[found] = place(n)
             found = found + ((slot < used) & wanted(n)).astype(jnp.int32)
     for i in range(3):
-        list_v[found + i] = 0
+        list_v[found + i] = slots_of[0]
         list_n[found + i] = pad
-    return lax.div(found + 3, 4)
+    return found
+
+
+def for_each(found, add):
+    eights = lax.div(found, 8)
+
+    def eight(i, _):
+        for k in range(8):
+            add(8 * i + k)
+        return 0
+
+    def four(i, _):
+        for k in range(4):
+            add(8 * eights + 4 * i + k)
+        return 0
+
+    lax.fori_loop(0, eights, eight, 0)
+    lax.fori_loop(0, lax.div(found - 8 * eights + 3, 4), four, 0)
 
 
 def far_row(right):
@@ -182,10 +220,7 @@
 
 
 def near_own_kernel(part, ids, count, pts0, pts1, pts2, pts3, joined, *refs):
-    if part == 0:
-        after, out, left_ref, right_ref, list_v, list_n = refs
-    else:
-        right_ref, after, out, left_ref, list_v, list_n = refs
+    after, out, left_ref, right_ref, list_v, list_n = refs[3 * part :]
     boxes = joined.shape[0]
     half = boxes // 2
     pair = half // 2
@@ -195,48 +230,44 @@
         for n in range(boxes):
             right_ref[n] = features(lanes(pts0[n], pts1[n]).astype(f32), centre)[1]
         right_ref[boxes] = far_row(right_ref[0])
-    order = [group * half + part * pair + v for v in range(pair)]
-    for v, box in enumerate(order):
+    mine = [part * pair + v for v in range(pair)]
+    order = [group * half + v for v in mine]
+    for v, box in zip(mine, order):
         whole = lanes(pts0[box], pts1[box], pts2[box], pts3[box]).astype(f32)
         left_ref[v] = features(whole, centre)[0].T.astype(bf16)
 
     def one(v, n):
         return dot(kernel_values(dot(left_ref[v], right_ref[n])), joined[jnp.minimum(n, boxes - 1)])
 
-    for v, box in enumerate(order):
+    for v, box in zip(mine, order):
         out[v] = one(v, box)
-    groups = collect(
-        ids, count, cluster * boxes, order, lambda n: (n >= 0) & (n < boxes), lambda n: n, boxes, list_v, list_n
-    )
-
-    def step(i, _):
-        for k in range(4):
-            v = list_v[4 * i + k]
-            out[v] += one(v, list_n[4 * i + k])
-        return 0
-
-    lax.fori_loop(0, groups, step, 0)
+    found = collect(
+        ids, count, cluster * boxes, mine, order, lambda n: (n >= 0) & (n < boxes), lambda n: n, boxes, list_v, list_n
+    )
+
+    def add(i):
+        v = list_v[i]
+        out[v] += one(v, list_n[i])
+
+    for_each(found, add)
 
 
 def near_halo_kernel(
-    ids, count, pts0, total0, total1, left0, left1, halo, after, keep, send1, send2, send3, right_ref, left_ref, acc, list_v, list_n
+    ids, count, pts0, total, left_ref, halo, after, keep, send1, send2, send3, acc, right_ref, list_v, list_n
 ):
     boxes, feat, rows = pts0.shape
     half = boxes // 2
-    pair = half // 2
     cluster, group, _ = position()
     centre = centre_of(pts0[half])
     for h in range(half):
         right_ref[h] = features(halo[h, 2 * rows :, :].astype(f32)[:feat], centre)[1]
     right_ref[half] = far_row(right_ref[0])
     order = [group * half + v for v in range(half)]
-    for part, (total, left) in enumerate(((total0, left0), (total1, left1))):
-        acc[part * pair : (part + 1) * pair] = total[...]
-        left_ref[part * pair : (part + 1) * pair] = left[...]
-    groups = collect(
+    found = collect(
         ids,
         count,
         cluster * boxes,
+        range(half),
         order,
         lambda n: (n < 0) | (n >= boxes),
         lambda n: jnp.where(group == 0, n + half, n - boxes),
@@ -245,36 +276,36 @@
         list_n,
     )
 
-    def step(i, _):
-        for k in range(4):
-            v = list_v[4 * i + k]
-            h = list_n[4 * i + k]
-            values = kernel_values(dot(left_ref[v], right_ref[h]))
-            acc[v] += dot(values, halo[jnp.minimum(h, half - 1), : 2 * rows, :])
-        return 0
-
-    lax.fori_loop(0, groups, step, 0)
+    def add(i):
+        v = list_v[i]
+        h = list_n[i]
+        values = kernel_values(dot(left_ref[v], right_ref[h]))
+        acc[v] += dot(values, halo[jnp.minimum(h, half - 1), : 2 * rows, :])
+
+    for_each(found, add)
     keep[...] = acc[:, :rows, :]
     for d, send in enumerate((send1, send2, send3)):
         send[...] = acc[:, (d + 1) * rows : (d + 2) * rows, :].astype(bf16)
 
 
-def finish_kernel(keep, back1, back2, back3, near):
+def finish_kernel(keep, back1, back2, back3, wide, near, top):
     half = near.shape[0] // 2
     _, group, _ = position()
     near[pl.ds(group * half, half)] = (keep[...] + back2[...].astype(f32)).astype(bf16)
     near[pl.ds((1 - group) * half, half)] = (back1[...].astype(f32) + back3[...].astype(f32)).astype(bf16)
-
-
-def call(body, out_shape, specs, micros, scratch=()):
+    top[0] = wide[...]
+
+
+def call(body, out_shape, specs, micros, scratch=(), aliases={}):
     return pl.pallas_call(
         body,
         out_shape=out_shape,
         in_specs=specs,
         out_specs=jax.tree.map(lambda _: VMEM, out_shape),
         scratch_shapes=list(scratch),
+        input_output_aliases=aliases,
         compiler_params=pltpu.CompilerParams(vmem_limit_bytes=VMEM_LIMIT),
-        cost_estimate=pl.CostEstimate(flops=int(micros * 1e6), bytes_accessed=1024, transcendentals=0),
+        cost_estimate=pl.CostEstimate(flops=int(micros * 1.1e9), bytes_accessed=1024, transcendentals=0),
     )
 
 
@@ -287,7 +318,6 @@
     tiles = lax.axis_size("tile")
     clusters = lax.axis_size("cluster")
     local_levels = boxes.bit_length() - 1
-    levels_above = merge_pivots.shape[1] - local_levels
 
     def to_tile(x, d):
         return lax.ppermute(x, "tile", [(i, i ^ d) for i in range(tiles)])
@@ -310,64 +340,62 @@
 
     got = [to_tile(points, d) for d in range(1, 4)]
     mate = to_tile(charges, 1)
-    points, charges = call(
-        load_kernel, (shape(*points.shape), shape(*charges.shape)), [VMEM, VMEM], 1
-    )(points, charges)
+    charges = call(load_kernel, shape(*charges.shape), [VMEM], COST["load"])(charges)
     to_send, joined = call(
-        stage_kernel, (shape(half, 2 * rows + 16, probes), shape(boxes, 2 * rows, probes)), [VMEM] * 4 + [ANY] * 2, 0.5
-    )(points, got[0], charges, mate, got[1], got[2])
+        stage_kernel, (shape(half, 2 * rows + 16, probes), shape(boxes, 2 * rows, probes)), [VMEM] * 4 + [ANY], COST["stage"]
+    )(points, got[0], charges, mate, got[2])
     halo = to_halo(to_send)
     pts = [points] + got
 
     merge_pv = jnp.transpose(merge_pivots, (1, 0, 2))
     width = probes // tiles
     wide_shape = shape(width + 16, rank)
-    mine, *sends = call(tree_kernel, (wide_shape,) * 4, [VMEM] * 7, 3, [pltpu.VMEM((probes, rank), f32)])(
+    mine, *sends = call(tree_kernel, (wide_shape,) * 4, [VMEM] * 7, COST["tree"], [pltpu.VMEM((probes, rank), f32)])(
         *pts, joined, leaf_pivots, merge_pv
     )
     others = [to_tile(sends[d - 1], d) for d in range(1, 4)]
 
     lists = [pltpu.SMEM((half * near_ids.shape[1] + 4,), jnp.int32)] * 2
 
-    def near_own(part, extra, after):
-        out = (shape(pair, 4 * rows, probes, dtype=f32), shape(pair, 4 * rows, 48))
-        if part == 0:
-            out += (shape(boxes + 1, 48, 2 * rows),)
-        specs = [SMEM] * 2 + [VMEM] * (5 + len(extra)) + [ANY]
-        return call(functools.partial(near_own_kernel, part), out, specs, 4, lists)(
-            near_ids, near_count, *pts, joined, *extra, after
+    sums = (
+        shape(half, 4 * rows, probes, dtype=f32),
+        shape(half, 4 * rows, 48),
+        shape(boxes + 1, 48, 2 * rows),
+    )
+
+    def near_own(part, begun, after):
+        specs = [SMEM] * 2 + [VMEM] * (5 + len(begun)) + [ANY]
+        aliases = {7 + i: i for i in range(len(begun))}
+        return call(functools.partial(near_own_kernel, part), sums, specs, COST["own"], lists, aliases)(
+            near_ids, near_count, *pts, joined, *begun, after
         )
 
-    total0, left0, right = near_own(0, [], mine)
-    wide = call(functools.partial(join_kernel, local_levels - 1), wide_shape, [VMEM] * 5 + [ANY], 1.5)(
-        mine, *others, merge_pv, left0
-    )
-    total1, left1 = near_own(1, [right], wide)
-    def level_up(bit, wide, after):
-        last = bit == levels_above - 1
-        out = shape(1, width, rank) if last else wide_shape
-        body = functools.partial(merge_kernel, local_levels + bit, bit, last)
-        return call(body, out, [VMEM] * 3 + [ANY], 1.5)(wide, partner(wide, 2**bit), merge_pv, after)
-
-    wide = level_up(0, wide, total1)
+    begun = near_own(0, [], mine)
+    wide = call(functools.partial(join_kernel, local_levels - 1), wide_shape, [VMEM] * 5 + [ANY], COST["join"])(
+        mine, *others, merge_pv, begun[2]
+    )
+    total, left, _ = near_own(1, begun, wide)
+    other = partner(wide, 1)
     keep, *sends = call(
         near_halo_kernel,
-        (shape(half, rows, probes, dtype=f32),) + (shape(half, rows, probes),) * 3,
-        [SMEM] * 2 + [VMEM] * 6 + [ANY],
-        3,
-        [
-            pltpu.VMEM((half + 1, 48, 2 * rows), bf16),
-            pltpu.VMEM((half, 4 * rows, 48), bf16),
-            pltpu.VMEM((half, 4 * rows, probes), f32),
-        ]
-        + lists,
-    )(near_ids, near_count, points, total0, total1, left0, left1, halo, wide)
+        (shape(half, rows, probes, dtype=f32),) + (shape(half, rows, probes),) * 3 + sums[:1],
+        [SMEM] * 2 + [VMEM] * 4 + [ANY],
+        COST["halo"],
+        [pltpu.VMEM((half + 1, 48, 2 * rows), bf16)] + lists,
+        {3: 4},
+    )(near_ids, near_count, points, total, left, halo, other)
     back = [to_tile(sends[d - 1], d) for d in range(1, 4)]
 
-    for bit in range(1, levels_above):
-        wide = level_up(bit, wide, keep)
-    near = call(finish_kernel, shape(boxes, rows, probes), [VMEM] * 4, 1.5)(keep, *back)
-    return near, jnp.swapaxes(wide, 1, 2)
+    wide = call(functools.partial(merge_kernel, local_levels, 0), wide_shape, [VMEM] * 3 + [ANY], COST["merge"])(
+        wide, other, merge_pv, back[0]
+    )
+    top = call(functools.partial(top_kernel, local_levels + 1, 1), shape(width, rank), [VMEM] * 5, COST["merge"])(
+        wide, partner(wide, 2), partner(wide, 4), partner(wide, 6), merge_pv
+    )
+    near, top = call(
+        finish_kernel, (shape(boxes, rows, probes), shape(1, width, rank)), [VMEM] * 5, COST["finish"]
+    )(keep, *back, top)
+    return near, jnp.swapaxes(top, 1, 2)
 
 
 def solution(mesh):

time: 44.4 us -> 41.1 us (0.926)
  waiting for transfers between devices: 9.01 us -> 7.19 us
  starting transfers between devices: 19.5 us -> 18 us
    ppermute x3 -> x4, starting transfers between devices: 8.64 us -> 7.01 us  [partner(): return lax.ppermute(x, 'cluster', route)]
    ppermute x3 -> x4, waiting for transfers between devices: 6.87 us -> 5.95 us  [partner(): return lax.ppermute(x, 'cluster', route)]
    ppermute x10, waiting for transfers between devices: 2.14 us -> 1.23 us  [to_tile(): return lax.ppermute(x, 'tile', [(i, i ^ d) for i in range(tiles)])]
    pallas_call x8 -> x7, Pallas kernels: 11.2 us -> 10.9 us  [the longest x2 4.35 us: near_own(): call(functools.partial(near_own_kernel, part), sums, specs, COST['own'],...]
    unnamed x12 -> x14, local copies, waits for them, and re-layouts: 1.78 us -> 1.78 us
  transfers between devices with their start and end apart: 14 -> 15, of which waited for: 6 -> 5; matrix products, arithmetic and copies ran while one was open for 0% -> 0% of each run, Pallas kernels for 25% -> 27%
where the time goes in v2:
time: 41.1 us; the launch traced here: 40.8 us
  starting transfers between devices  18 us (44%)
  Pallas kernels  13.1 us (32%)
  waiting for transfers between devices  7.19 us (17%)
  local copies, waits for them, and re-layouts  1.78 us (4%)
  between operations  0.81 us (2%)
    ppermute x10, starting transfers between devices, to_tile(): return lax.ppermute(x, 'tile', [(i, i ^ d) for i in range(tiles)])  7.41 us
    ppermute x4, starting transfers between devices, partner(): return lax.ppermute(x, 'cluster', route)  7.01 us
    ppermute x4, waiting for transfers between devices, partner(): return lax.ppermute(x, 'cluster', route)  5.95 us
    pallas_call x2, Pallas kernels, near_own(): call(functools.partial(near_own_kernel, part), sums, specs, COST['own'],...  4.35 us
    ppermute x1, starting transfers between devices, to_halo(): return lax.ppermute(x, ('cluster', 'tile'), route)  3.58 us
    pallas_call x1, Pallas kernels, on_device(): call(tree_kernel, (wide_shape,) * 4, [VMEM] * 7, COST['tree'], [pltpu.VME...  2.41 us
    pallas_call x1, Pallas kernels, on_device(): call(functools.partial(top_kernel, local_levels + 1, 1), shape(width, ran...  2.28 us
    unnamed x14, local copies, waits for them, and re-layouts  1.78 us
  transfers between devices with their start and end apart: 15, of which 5 were waited for; matrix products, arithmetic and copies ran while one was open for 0% of the time, Pallas kernels for 27%

profile of v2, /device:TPU:0, one launch (start us, length us, event | category | flops | bytes accessed | tf_op | source)
XLA Modules:
  0.0 40.8 jit_solution(4784544625997560745)
XLA Ops:
  0.6 0.5 %collective-permute-start.3 = (bf16[8,128,256]{2,1,0:T(8,128)(2,1)}, bf16[8,128,256]{2,1,0:T(8,128)(2,1)S(1)}, u32[]{:S(2)}, u32[]{:S(2)}) collective-permute-start(bf16[8,128,256]{2,1,0:T(8,128)(2,1)} %charges.1), channel_id=1, source_target_pairs={{0,1},{1,0},{2,3},{3,2},{4,5},{5,4},{6,7},{7,6},{8,9},{9,8},{10,11... | collective-permute-start | bytes 1572872 | tf_op jit(solution)/shard_map/ppermute | solution.py:323
  1.1 2.6 %collective-permute-start.2 = (bf16[8,8,128]{2,1,0:T(8,128)(2,1)}, bf16[8,8,128]{2,1,0:T(8,128)(2,1)S(1)}, u32[]{:S(2)}, u32[]{:S(2)}) collective-permute-start(bf16[8,8,128]{2,1,0:T(8,128)(2,1)} %pts0.7), channel_id=1, source_target_pairs={{0,3},{1,2},{2,1},{3,0},{4,7},{5,6},{6,5},{7,4},{8,11},{9,10},{10,... | collective-permute-start | bytes 49160 | tf_op jit(solution)/shard_map/ppermute | solution.py:323
  3.8 0.1 collective-permute-start
  3.9 0.3 collective-permute-start.1
  4.2 1.0 %copy-done = bf16[8,128,256]{2,1,0:T(8,128)(2,1)S(1)} copy-done((bf16[8,128,256]{2,1,0:T(8,128)(2,1)S(1)}, bf16[8,128,256]{2,1,0:T(8,128)(2,1)}, u32[]{:S(2)}) %copy-start) | copy-done | bytes 524312
  5.3 0.2 collective-permute-done.2.after.pts3
  5.4 0.0 collective-permute-done.got1.pts1
  5.5 0.0 collective-permute-done.3.mate
  5.5 0.7 %copy-done.1 = bf16[8,8,128]{2,1,0:T(8,128)(2,1)S(1)} copy-done((bf16[8,8,128]{2,1,0:T(8,128)(2,1)S(1)}, bf16[8,8,128]{2,1,0:T(8,128)(2,1)}, u32[]{:S(2)}) %copy-start.1) | copy-done | bytes 16408
  6.2 0.1 shard_map.78
  6.3 3.6 %collective-permute-start.7 = (bf16[4,272,256]{2,1,0:T(8,128)(2,1)S(1)}, bf16[4,272,256]{2,1,0:T(8,128)(2,1)S(1)}, u32[]{:S(2)}, u32[]{:S(2)}) collective-permute-start(bf16[4,272,256]{2,1,0:T(8,128)(2,1)S(1)} %get-tuple-element.29), channel_id=1, source_target_pairs={{0,4},{2,6},{4,8},{5,1},{6,10},{7,3},{8,12},{9,5},{10,14},{11,7},{... | collective-permute-start | bytes 1671176 | tf_op jit(solution)/shard_map/ppermute | solution.py:332
  9.9 0.0 collective-permute-done.1.pts2
  9.9 0.0 copy-done.2
  9.9 0.0 copy-done.3
  9.9 0.0 copy-done.4
  9.9 0.0 copy-start.5
  9.9 0.0 copy-start.6
  9.9 2.4 %shard_map.79 = (bf16[80,256]{1,0:T(8,128)(2,1)S(1)}, bf16[80,256]{1,0:T(8,128)(2,1)S(1)}, bf16[80,256]{1,0:T(8,128)(2,1)S(1)}, bf16[80,256]{1,0:T(8,128)(2,1)S(1)}) custom-call(bf16[8,8,128]{2,1,0:T(8,128)(2,1)S(1)} %copy-done.2, bf16[8,8,128]{2,1,0:T(8,128)(2,1)S(1)} %collective-permute-done.got1.pts1, bf16[8,8,128]{2,1,0:T(8,128)(2,1)S(1)} %collective-permute-done.1.pts2, ...), custom_call_target="tpu_custom_call" | custom-call | flops 3300000000 | bytes 1024 | tf_op jit(solution)/shard_map/pallas_call | solution.py:353
  12.3 0.1 collective-permute-start.4
  12.4 1.6 %collective-permute-start.5 = (bf16[80,256]{1,0:T(8,128)(2,1)S(1)}, bf16[80,256]{1,0:T(8,128)(2,1)S(1)}, u32[]{:S(2)}, u32[]{:S(2)}) collective-permute-start(bf16[80,256]{1,0:T(8,128)(2,1)S(1)} %get-tuple-element.25), channel_id=1, source_target_pairs={{0,2},{1,3},{2,0},{3,1},{4,6},{5,7},{6,4},{7,5},{8,10},{9,11},{10,... | collective-permute-start | bytes 122888 | tf_op jit(solution)/shard_map/ppermute | solution.py:323
  14.0 0.3 collective-permute-start.6
  14.3 0.0 copy-done.5
  14.3 0.0 copy-done.6
  14.3 2.2 %shard_map.80 = (f32[4,512,256]{2,1,0:T(8,128)S(1)}, bf16[4,512,48]{2,1,0:T(8,128)(2,1)S(1)}, bf16[9,48,256]{2,1,0:T(8,128)(2,1)S(1)}) custom-call(s32[8,8]{1,0:T(8,128)S(1)} %copy-done.5, s32[8]{0:T(128)S(1)} %copy-done.6, bf16[8,8,128]{2,1,0:T(8,128)(2,1)S(1)} %copy-done.2, bf16[8,8,128]{2,1,0:T(8,128)(2,1)S(1)} %collective-permute-done.got1.pts1, ...), custom_call_target="tpu_custom_call" | custom-call | flops 1100000000 | bytes 1024 | tf_op jit(solution)/shard_map/pallas_call | solution.py:369
  16.5 0.0 collective-permute-done.4.got1
  16.5 0.0 collective-permute-done.5.got2
  16.5 1.0 %collective-permute-done.6.got3 = bf16[80,256]{1,0:T(8,128)(2,1)S(1)} collective-permute-done((bf16[80,256]{1,0:T(8,128)(2,1)S(1)}, bf16[80,256]{1,0:T(8,128)(2,1)S(1)}, u32[]{:S(2)}, u32[]{:S(2)}) %collective-permute-start.6) | collective-permute-done | bytes 40992 | tf_op jit(solution)/shard_map/ppermute | solution.py:323
  17.5 1.0 %shard_map.81.refs_3_.mine = bf16[80,256]{1,0:T(8,128)(2,1)S(1)} custom-call(bf16[80,256]{1,0:T(8,128)(2,1)S(1)} %get-tuple-element.20.refs_0_.mine, bf16[80,256]{1,0:T(8,128)(2,1)S(1)} %collective-permute-done.4.got1, bf16[80,256]{1,0:T(8,128)(2,1)S(1)} %collective-permute-done.5.got2, bf16[80,256]{1,0:T(8,128)(2,1)S(1)} %collective-permute-done.6.got3, ...), custom_call_target="tpu_custom_call" | custom-call | flops 1100000000 | bytes 1024 | tf_op jit(solution)/shard_map/pallas_call | solution.py:374
  18.5 1.6 %collective-permute-start.8 = (bf16[80,256]{1,0:T(8,128)(2,1)S(1)}, bf16[80,256]{1,0:T(8,128)(2,1)S(1)}, u32[]{:S(2)}, u32[]{:S(2)}) collective-permute-start(bf16[80,256]{1,0:T(8,128)(2,1)S(1)} %shard_map.81.refs_3_.mine), channel_id=1, source_target_pairs={{0,4},{4,0},{8,12},{12,8},{16,20},{20,16},{24,28},{28,24},{1,5},{5... | collective-permute-start | bytes 122888 | tf_op jit(solution)/shard_map/ppermute | solution.py:336
  20.1 2.2 %shard_map.82 = (f32[4,512,256]{2,1,0:T(8,128)S(1)}, bf16[4,512,48]{2,1,0:T(8,128)(2,1)S(1)}, bf16[9,48,256]{2,1,0:T(8,128)(2,1)S(1)}) custom-call(s32[8,8]{1,0:T(8,128)S(1)} %copy-done.5, s32[8]{0:T(128)S(1)} %copy-done.6, bf16[8,8,128]{2,1,0:T(8,128)(2,1)S(1)} %copy-done.2, ...), custom_call_target="tpu_custom_call", output_to_operand_aliasing={{0}: (7, {}), {1}: (8, {}), {2}: (9, {})} | custom-call | flops 1100000000 | bytes 1024 | tf_op jit(solution)/shard_map/pallas_call | solution.py:369
  22.3 1.4 %collective-permute-done.8.after.got = bf16[80,256]{1,0:T(8,128)(2,1)S(1)} collective-permute-done((bf16[80,256]{1,0:T(8,128)(2,1)S(1)}, bf16[80,256]{1,0:T(8,128)(2,1)S(1)}, u32[]{:S(2)}, u32[]{:S(2)}) %collective-permute-start.8) | collective-permute-done | bytes 40992 | tf_op jit(solution)/shard_map/ppermute | solution.py:336
  23.7 0.0 collective-permute-done.7.halo
  23.7 1.1 %shard_map.83 = (f32[4,128,256]{2,1,0:T(8,128)S(1)}, bf16[4,128,256]{2,1,0:T(8,128)(2,1)S(1)}, bf16[4,128,256]{2,1,0:T(8,128)(2,1)S(1)}, bf16[4,128,256]{2,1,0:T(8,128)(2,1)S(1)}, f32[4,512,256]{2,1,0:T(8,128)S(1)}) custom-call(s32[8,8]{1,0:T(8,128)S(1)} %copy-done.5, s32[8]{0:T(128)S(1)} %copy-done.6, ...), custom_call_target="tpu_custom_call", output_to_operand_aliasing={{4}: (3, {})} | custom-call | flops 5500000256 | bytes 1024 | tf_op jit(solution)/shard_map/pallas_call | solution.py:379
  24.8 0.1 collective-permute-start.9
  24.9 1.6 %collective-permute-start.10 = (bf16[4,128,256]{2,1,0:T(8,128)(2,1)S(1)}, bf16[4,128,256]{2,1,0:T(8,128)(2,1)S(1)}, u32[]{:S(2)}, u32[]{:S(2)}) collective-permute-start(bf16[4,128,256]{2,1,0:T(8,128)(2,1)S(1)} %get-tuple-element.32), channel_id=1, source_target_pairs={{0,2},{1,3},{2,0},{3,1},{4,6},{5,7},{6,4},{7,5},{8,10},{9,11},{10,... | collective-permute-start | bytes 786440 | tf_op jit(solution)/shard_map/ppermute | solution.py:323
  26.5 0.3 collective-permute-start.11
  26.7 0.0 collective-permute-done.9.after.back1
  26.7 1.0 %shard_map.84.mine = bf16[80,256]{1,0:T(8,128)(2,1)S(1)} custom-call(bf16[80,256]{1,0:T(8,128)(2,1)S(1)} %shard_map.81.refs_3_.mine, bf16[80,256]{1,0:T(8,128)(2,1)S(1)} %collective-permute-done.8.after.got, s32[6,4,256]{2,1,0:T(4,128)S(1)} %bitcast.4, bf16[4,128,256]{2,1,0:T(8,128)(2,1)S(1)} %collective-permute-done.9.after.back1), custom_call_target="tpu_custom_call" | custom-call | flops 1100000000 | bytes 1024 | tf_op jit(solution)/shard_map/pallas_call | solution.py:389
  27.7 4.6 %collective-permute-start.14 = (bf16[80,256]{1,0:T(8,128)(2,1)S(1)}, bf16[80,256]{1,0:T(8,128)(2,1)S(1)}, u32[]{:S(2)}, u32[]{:S(2)}) collective-permute-start(bf16[80,256]{1,0:T(8,128)(2,1)S(1)} %shard_map.84.mine), channel_id=1, source_target_pairs={{0,24},{4,28},{8,16},{12,20},{16,8},{20,12},{24,0},{28,4},{1,25},{... | collective-permute-start | bytes 122888 | tf_op jit(solution)/shard_map/ppermute | solution.py:336
  32.2 0.4 collective-permute-start.13
  32.6 0.5 %collective-permute-start.12 = (bf16[80,256]{1,0:T(8,128)(2,1)S(1)}, bf16[80,256]{1,0:T(8,128)(2,1)S(1)}, u32[]{:S(2)}, u32[]{:S(2)}) collective-permute-start(bf16[80,256]{1,0:T(8,128)(2,1)S(1)} %shard_map.84.mine), channel_id=1, source_target_pairs={{0,8},{4,12},{8,0},{12,4},{16,24},{20,28},{24,16},{28,20},{1,9},{5... | collective-permute-start | bytes 122888 | tf_op jit(solution)/shard_map/ppermute | solution.py:336
  33.1 1.4 %collective-permute-done.14.got3 = bf16[80,256]{1,0:T(8,128)(2,1)S(1)} collective-permute-done((bf16[80,256]{1,0:T(8,128)(2,1)S(1)}, bf16[80,256]{1,0:T(8,128)(2,1)S(1)}, u32[]{:S(2)}, u32[]{:S(2)}) %collective-permute-start.14) | collective-permute-done | bytes 40992 | tf_op jit(solution)/shard_map/ppermute | solution.py:336
  34.5 3.1 %collective-permute-done.13.got2 = bf16[80,256]{1,0:T(8,128)(2,1)S(1)} collective-permute-done((bf16[80,256]{1,0:T(8,128)(2,1)S(1)}, bf16[80,256]{1,0:T(8,128)(2,1)S(1)}, u32[]{:S(2)}, u32[]{:S(2)}) %collective-permute-start.13) | collective-permute-done | bytes 40992 | tf_op jit(solution)/shard_map/ppermute | solution.py:336
  37.6 0.0 collective-permute-done.12.got1
  37.6 2.3 %shard_map.85.wide = bf16[64,256]{1,0:T(8,128)(2,1)S(1)} custom-call(bf16[80,256]{1,0:T(8,128)(2,1)S(1)} %shard_map.84.mine, bf16[80,256]{1,0:T(8,128)(2,1)S(1)} %collective-permute-done.12.got1, bf16[80,256]{1,0:T(8,128)(2,1)S(1)} %collective-permute-done.13.got2, bf16[80,256]{1,0:T(8,128)(2,1)S(1)} %collective-permute-done.14.got3, s32[6,4,256]{2,1,0:T(4,128)S(1)} %bitcast.5), custom_call_target="tpu_custom_call" | custom-call | flops 1100000000 | bytes 1024 | tf_op jit(solution)/shard_map/pallas_call | solution.py:392
  39.9 0.0 collective-permute-done.10.back2
  39.9 0.0 collective-permute-done.11.back3
  39.9 0.9 %shard_map.86 = (bf16[8,128,256]{2,1,0:T(8,128)(2,1)}, bf16[1,64,256]{2,1,0:T(8,128)(2,1)}) custom-call(f32[4,128,256]{2,1,0:T(8,128)S(1)} %get-tuple-element.30.keep, bf16[4,128,256]{2,1,0:T(8,128)(2,1)S(1)} %collective-permute-done.9.after.back1, bf16[4,128,256]{2,1,0:T(8,128)(2,1)S(1)} %collective-permute-done.10.back2, ...), custom_call_target="tpu_custom_call" | custom-call | flops 1100000 | bytes 1024 | tf_op jit(solution)/shard_map/pallas_call | solution.py:395
  (6 shorter events, 0.0 us)
Async XLA Ops:
  0.6 4.8 %collective-permute-start.3 = (bf16[8,128,256]{2,1,0:T(8,128)(2,1)}, bf16[8,128,256]{2,1,0:T(8,128)(2,1)S(1)}, u32[]{:S(2)}, u32[]{:S(2)}) collective-permute-start(bf16[8,128,256]{2,1,0:T(8,128)(2,1)} %charges.1), channel_id=1, source_target_pairs={{0,1},{1,0},{2,3},{3,2},{4,5},{5,4},{6,7},{7,6},{8,9},{9,8},{10,11... | collective-permute-start | bytes 1572872 | tf_op jit(solution)/shard_map/ppermute | solution.py:323
  1.1 4.3 %collective-permute-start.2 = (bf16[8,8,128]{2,1,0:T(8,128)(2,1)}, bf16[8,8,128]{2,1,0:T(8,128)(2,1)S(1)}, u32[]{:S(2)}, u32[]{:S(2)}) collective-permute-start(bf16[8,8,128]{2,1,0:T(8,128)(2,1)} %pts0.7), channel_id=1, source_target_pairs={{0,3},{1,2},{2,1},{3,0},{4,7},{5,6},{6,5},{7,4},{8,11},{9,10},{10,... | collective-permute-start | bytes 49160 | tf_op jit(solution)/shard_map/ppermute | solution.py:323
  3.8 1.7 %collective-permute-start = (bf16[8,8,128]{2,1,0:T(8,128)(2,1)}, bf16[8,8,128]{2,1,0:T(8,128)(2,1)S(1)}, u32[]{:S(2)}, u32[]{:S(2)}) collective-permute-start(bf16[8,8,128]{2,1,0:T(8,128)(2,1)} %pts0.7), channel_id=1, source_target_pairs={{0,1},{1,0},{2,3},{3,2},{4,5},{5,4},{6,7},{7,6},{8,9},{9,8},{10,11... | collective-permute-start | bytes 49160 | tf_op jit(solution)/shard_map/ppermute | solution.py:323
  3.9 6.0 %collective-permute-start.1 = (bf16[8,8,128]{2,1,0:T(8,128)(2,1)}, bf16[8,8,128]{2,1,0:T(8,128)(2,1)S(1)}, u32[]{:S(2)}, u32[]{:S(2)}) collective-permute-start(bf16[8,8,128]{2,1,0:T(8,128)(2,1)} %pts0.7), channel_id=1, source_target_pairs={{0,2},{1,3},{2,0},{3,1},{4,6},{5,7},{6,4},{7,5},{8,10},{9,11},{10,... | collective-permute-start | bytes 49160 | tf_op jit(solution)/shard_map/ppermute | solution.py:323
  4.2 1.0 %copy-start = (bf16[8,128,256]{2,1,0:T(8,128)(2,1)S(1)}, bf16[8,128,256]{2,1,0:T(8,128)(2,1)}, u32[]{:S(2)}) copy-start(bf16[8,128,256]{2,1,0:T(8,128)(2,1)} %charges.1) | copy-start | bytes 1572868
  5.2 4.7 %copy-start.2 = (bf16[8,8,128]{2,1,0:T(8,128)(2,1)S(1)}, bf16[8,8,128]{2,1,0:T(8,128)(2,1)}, u32[]{:S(2)}) copy-start(bf16[8,8,128]{2,1,0:T(8,128)(2,1)} %pts0.7) | copy-start | bytes 49156
  5.2 4.7 %copy-start.3 = (s32[4,6,256]{2,0,1:T(4,128)S(1)}, s32[4,6,256]{2,0,1:T(4,128)}, u32[]{:S(2)}) copy-start(s32[4,6,256]{2,0,1:T(4,128)} %param.11) | copy-start | bytes 73732
  5.2 4.7 %copy-start.4 = (s32[8,256]{1,0:T(8,128)S(1)}, s32[8,256]{1,0:T(8,128)}, u32[]{:S(2)}) copy-start(s32[8,256]{1,0:T(8,128)} %leaf_pv.1) | copy-start | bytes 24580
  5.5 0.7 %copy-start.1 = (bf16[8,8,128]{2,1,0:T(8,128)(2,1)S(1)}, bf16[8,8,128]{2,1,0:T(8,128)(2,1)}, u32[]{:S(2)}) copy-start(bf16[8,8,128]{2,1,0:T(8,128)(2,1)} %pts0.7) | copy-start | bytes 49156
  6.3 17.4 %collective-permute-start.7 = (bf16[4,272,256]{2,1,0:T(8,128)(2,1)S(1)}, bf16[4,272,256]{2,1,0:T(8,128)(2,1)S(1)}, u32[]{:S(2)}, u32[]{:S(2)}) collective-permute-start(bf16[4,272,256]{2,1,0:T(8,128)(2,1)S(1)} %get-tuple-element.29), channel_id=1, source_target_pairs={{0,4},{2,6},{4,8},{5,1},{6,10},{7,3},{8,12},{9,5},{10,14},{11,7},{... | collective-permute-start | bytes 1671176 | tf_op jit(solution)/shard_map/ppermute | solution.py:332
  9.9 4.4 %copy-start.5 = (s32[8,8]{1,0:T(8,128)S(1)}, s32[8,8]{1,0:T(8,128)}, u32[]{:S(2)}) copy-start(s32[8,8]{1,0:T(8,128)} %ids.5) | copy-start | bytes 772
  9.9 4.4 %copy-start.6 = (s32[8]{0:T(128)S(1)}, s32[8]{0:T(128)}, u32[]{:S(2)}) copy-start(s32[8]{0:T(128)} %count.5) | copy-start | bytes 100
  12.3 4.1 %collective-permute-start.4 = (bf16[80,256]{1,0:T(8,128)(2,1)S(1)}, bf16[80,256]{1,0:T(8,128)(2,1)S(1)}, u32[]{:S(2)}, u32[]{:S(2)}) collective-permute-start(bf16[80,256]{1,0:T(8,128)(2,1)S(1)} %get-tuple-element.24), channel_id=1, source_target_pairs={{0,1},{1,0},{2,3},{3,2},{4,5},{5,4},{6,7},{7,6},{8,9},{9,8},{10,11... | collective-permute-start | bytes 122888 | tf_op jit(solution)/shard_map/ppermute | solution.py:323
  12.4 4.1 %collective-permute-start.5 = (bf16[80,256]{1,0:T(8,128)(2,1)S(1)}, bf16[80,256]{1,0:T(8,128)(2,1)S(1)}, u32[]{:S(2)}, u32[]{:S(2)}) collective-permute-start(bf16[80,256]{1,0:T(8,128)(2,1)S(1)} %get-tuple-element.25), channel_id=1, source_target_pairs={{0,2},{1,3},{2,0},{3,1},{4,6},{5,7},{6,4},{7,5},{8,10},{9,11},{10,... | collective-permute-start | bytes 122888 | tf_op jit(solution)/shard_map/ppermute | solution.py:323
  14.0 3.5 %collective-permute-start.6 = (bf16[80,256]{1,0:T(8,128)(2,1)S(1)}, bf16[80,256]{1,0:T(8,128)(2,1)S(1)}, u32[]{:S(2)}, u32[]{:S(2)}) collective-permute-start(bf16[80,256]{1,0:T(8,128)(2,1)S(1)} %get-tuple-element.26), channel_id=1, source_target_pairs={{0,3},{1,2},{2,1},{3,0},{4,7},{5,6},{6,5},{7,4},{8,11},{9,10},{10,... | collective-permute-start | bytes 122888 | tf_op jit(solution)/shard_map/ppermute | solution.py:323
  18.5 5.2 %collective-permute-start.8 = (bf16[80,256]{1,0:T(8,128)(2,1)S(1)}, bf16[80,256]{1,0:T(8,128)(2,1)S(1)}, u32[]{:S(2)}, u32[]{:S(2)}) collective-permute-start(bf16[80,256]{1,0:T(8,128)(2,1)S(1)} %shard_map.81.refs_3_.mine), channel_id=1, source_target_pairs={{0,4},{4,0},{8,12},{12,8},{16,20},{20,16},{24,28},{28,24},{1,5},{5... | collective-permute-start | bytes 122888 | tf_op jit(solution)/shard_map/ppermute | solution.py:336
  24.8 1.9 %collective-permute-start.9 = (bf16[4,128,256]{2,1,0:T(8,128)(2,1)S(1)}, bf16[4,128,256]{2,1,0:T(8,128)(2,1)S(1)}, u32[]{:S(2)}, u32[]{:S(2)}) collective-permute-start(bf16[4,128,256]{2,1,0:T(8,128)(2,1)S(1)} %get-tuple-element.31), channel_id=1, source_target_pairs={{0,1},{1,0},{2,3},{3,2},{4,5},{5,4},{6,7},{7,6},{8,9},{9,8},{10,11... | collective-permute-start | bytes 786440 | tf_op jit(solution)/shard_map/ppermute | solution.py:323
  24.9 15.1 %collective-permute-start.10 = (bf16[4,128,256]{2,1,0:T(8,128)(2,1)S(1)}, bf16[4,128,256]{2,1,0:T(8,128)(2,1)S(1)}, u32[]{:S(2)}, u32[]{:S(2)}) collective-permute-start(bf16[4,128,256]{2,1,0:T(8,128)(2,1)S(1)} %get-tuple-element.32), channel_id=1, source_target_pairs={{0,2},{1,3},{2,0},{3,1},{4,6},{5,7},{6,4},{7,5},{8,10},{9,11},{10,... | collective-permute-start | bytes 786440 | tf_op jit(solution)/shard_map/ppermute | solution.py:323
  26.5 13.5 %collective-permute-start.11 = (bf16[4,128,256]{2,1,0:T(8,128)(2,1)S(1)}, bf16[4,128,256]{2,1,0:T(8,128)(2,1)S(1)}, u32[]{:S(2)}, u32[]{:S(2)}) collective-permute-start(bf16[4,128,256]{2,1,0:T(8,128)(2,1)S(1)} %get-tuple-element.33), channel_id=1, source_target_pairs={{0,3},{1,2},{2,1},{3,0},{4,7},{5,6},{6,5},{7,4},{8,11},{9,10},{10,... | collective-permute-start | bytes 786440 | tf_op jit(solution)/shard_map/ppermute | solution.py:323
  27.7 6.9 %collective-permute-start.14 = (bf16[80,256]{1,0:T(8,128)(2,1)S(1)}, bf16[80,256]{1,0:T(8,128)(2,1)S(1)}, u32[]{:S(2)}, u32[]{:S(2)}) collective-permute-start(bf16[80,256]{1,0:T(8,128)(2,1)S(1)} %shard_map.84.mine), channel_id=1, source_target_pairs={{0,24},{4,28},{8,16},{12,20},{16,8},{20,12},{24,0},{28,4},{1,25},{... | collective-permute-start | bytes 122888 | tf_op jit(solution)/shard_map/ppermute | solution.py:336
  32.2 5.4 %collective-permute-start.13 = (bf16[80,256]{1,0:T(8,128)(2,1)S(1)}, bf16[80,256]{1,0:T(8,128)(2,1)S(1)}, u32[]{:S(2)}, u32[]{:S(2)}) collective-permute-start(bf16[80,256]{1,0:T(8,128)(2,1)S(1)} %shard_map.84.mine), channel_id=1, source_target_pairs={{0,16},{4,20},{8,24},{12,28},{16,0},{20,4},{24,8},{28,12},{1,17},{... | collective-permute-start | bytes 122888 | tf_op jit(solution)/shard_map/ppermute | solution.py:336
  32.6 5.0 %collective-permute-start.12 = (bf16[80,256]{1,0:T(8,128)(2,1)S(1)}, bf16[80,256]{1,0:T(8,128)(2,1)S(1)}, u32[]{:S(2)}, u32[]{:S(2)}) collective-permute-start(bf16[80,256]{1,0:T(8,128)(2,1)S(1)} %shard_map.84.mine), channel_id=1, source_target_pairs={{0,8},{4,12},{8,0},{12,4},{16,24},{20,28},{24,16},{28,20},{1,9},{5... | collective-permute-start | bytes 122888 | tf_op jit(solution)/shard_map/ppermute | solution.py:336

commit v3 on v2

--- a/solution.py
+++ b/solution.py
@@ -12,13 +12,14 @@
 lengthscale = 0.7
 KAPPA = math.log2(math.e) / lengthscale
 FLOOR = 1e-30
-COST = dict(load=0.001, stage=0.001, tree=3, own=1, join=1, merge=1, halo=5, finish=0.001)
+COST = dict(load=0.001, stage=0.001, tree=3, own=1, join=1, merge=1, halo=5, rest=1, finish=0.001)
 VMEM_LIMIT = 16 * 1024 * 1024
 f32 = jnp.float32
 bf16 = jnp.bfloat16
 VMEM = pl.BlockSpec(memory_space=pltpu.VMEM)
 SMEM = pl.BlockSpec(memory_space=pltpu.SMEM)
 ANY = pl.BlockSpec(memory_space=pl.ANY)
+HBM = pl.BlockSpec(memory_space=pltpu.HBM)
 
 
 def features(coords, centre):
@@ -70,22 +71,25 @@
     return lax.axis_index("cluster"), lax.rem(tile, 2), tile
 
 
-def load_kernel(charges, out):
-    out[...] = charges[...]
+def load_kernel(*refs):
+    count = len(refs) // 2
+    for copy in start_copies(list(zip(refs[:count], refs[count:])), refs[-1]):
+        copy.wait()
 
 
 def stage_kernel(points, got1, charges, mate, after, to_send, joined):
     boxes, feat, rows = got1.shape
     joined[:, :rows, :] = charges[...]
     joined[:, rows:, :] = mate[...]
-    count = to_send.shape[0]
+    count = boxes // 2
     start = jnp.where(position()[1] == 0, boxes - count, 0)
+    coords = []
     for i in range(count):
         box = start + i
-        to_send[i, :rows, :] = charges[box]
-        to_send[i, rows : 2 * rows, :] = mate[box]
-        coords = lanes(points[box], got1[box]).astype(f32)
-        to_send[i, 2 * rows :, :] = jnp.concatenate([coords, jnp.zeros_like(coords)], axis=0).astype(bf16)
+        to_send[2 * i * rows : (2 * i + 1) * rows, :] = charges[box]
+        to_send[(2 * i + 1) * rows : 2 * (i + 1) * rows, :] = mate[box]
+        coords.append(lanes(points[box], got1[box]).astype(f32))
+    to_send[2 * count * rows :, :] = jnp.concatenate(coords, axis=0).astype(bf16)
 
 
 def with_coords(weights, coords):
@@ -129,9 +133,13 @@
         out[...] = with_coords(held[pl.ds(pl.multiple_of((tile ^ d) * width, width), width), :], coords[0])
 
 
-def merged_pair(ours, theirs, our_coords, their_coords, pivots):
+def merged_pair(ours, theirs, our_coords, their_coords, pivots, near=False):
     coords = lanes(our_coords.astype(f32)[:8], their_coords.astype(f32)[:8])
     chosen = choose(coords, pivots)
+    if near:
+        centre = centre_of(coords)
+        left, right = features(coords, centre)[0], features(chosen, centre)[1]
+        return dot(lanes(ours, theirs), kernel_values(dot(left.T.astype(bf16), right))), chosen
     across = coords.T
     squares = None
     for f in range(coords.shape[0]):
@@ -147,7 +155,7 @@
     ours = (mine[:width, :].astype(f32) + got2[:width, :].astype(f32)).astype(bf16)
     theirs = (got1[:width, :].astype(f32) + got3[:width, :].astype(f32)).astype(bf16)
     pivots = merge_pv[level, :1, :] ^ (group * mine.shape[1])
-    out[...] = with_coords(*merged_pair(ours, theirs, mine[width:, :], got1[width:, :], pivots))
+    out[...] = with_coords(*merged_pair(ours, theirs, mine[width:, :], got1[width:, :], pivots, True))
 
 
 def upper_half(bit):
@@ -182,6 +190,13 @@
     out[...] = merged_pair(ours, theirs, our_coords, their_coords, pivots)[0].astype(bf16)
 
 
+def start_copies(pairs, sem):
+    copies = [pltpu.make_async_copy(one, other, sem.at[i]) for i, (one, other) in enumerate(pairs)]
+    for copy in copies:
+        copy.start()
+    return copies
+
+
 def collect(ids, count, base, slots_of, boxes_of, wanted, place, pad, list_v, list_n):
     found = 0
     for v, box in zip(slots_of, boxes_of):
@@ -199,19 +214,21 @@
 
 def for_each(found, add):
     eights = lax.div(found, 8)
-
-    def eight(i, _):
-        for k in range(8):
-            add(8 * i + k)
-        return 0
-
-    def four(i, _):
-        for k in range(4):
-            add(8 * eights + 4 * i + k)
-        return 0
-
-    lax.fori_loop(0, eights, eight, 0)
-    lax.fori_loop(0, lax.div(found - 8 * eights + 3, 4), four, 0)
+    rest = found - 8 * eights
+    fours = lax.div(rest + 1, 4)
+    twos = lax.div(rest - 4 * fours + 1, 2)
+
+    def run(first, steps, size):
+        def step(i, _):
+            for k in range(size):
+                add(first + size * i + k)
+            return 0
+
+        lax.fori_loop(0, steps, step, 0)
+
+    run(0, eights, 8)
+    run(8 * eights, fours, 4)
+    run(8 * eights + 4 * fours, twos, 2)
 
 
 def far_row(right):
@@ -219,8 +236,9 @@
     return jnp.where(row == 35, 1e30, 0.0).astype(bf16)
 
 
-def near_own_kernel(part, ids, count, pts0, pts1, pts2, pts3, joined, *refs):
-    after, out, left_ref, right_ref, list_v, list_n = refs[3 * part :]
+def near_own_kernel(part, all_ids, all_counts, pts0, pts1, pts2, pts3, joined, *refs):
+    after, out, left_ref, right_ref, list_v, list_n, ids, count, sem = refs[3 * part :]
+    copies = start_copies([(all_ids, ids), (all_counts, count)], sem)
     boxes = joined.shape[0]
     half = boxes // 2
     pair = half // 2
@@ -241,6 +259,8 @@
 
     for v, box in zip(mine, order):
         out[v] = one(v, box)
+    for copy in copies:
+        copy.wait()
     found = collect(
         ids, count, cluster * boxes, mine, order, lambda n: (n >= 0) & (n < boxes), lambda n: n, boxes, list_v, list_n
     )
@@ -252,17 +272,24 @@
     for_each(found, add)
 
 
-def near_halo_kernel(
-    ids, count, pts0, total, left_ref, halo, after, keep, send1, send2, send3, acc, right_ref, list_v, list_n
-):
+def near_halo_kernel(part, all_ids, all_counts, pts0, total, left_ref, halo, after, *refs):
+    if part == 0:
+        send1, send2, send3, acc, right_ref, list_v, list_n, ids, count, sem = refs
+    else:
+        right_ref, keep, acc, list_v, list_n, ids, count, sem = refs
+    copies = start_copies([(all_ids, ids), (all_counts, count)], sem)
     boxes, feat, rows = pts0.shape
     half = boxes // 2
     cluster, group, _ = position()
-    centre = centre_of(pts0[half])
-    for h in range(half):
-        right_ref[h] = features(halo[h, 2 * rows :, :].astype(f32)[:feat], centre)[1]
-    right_ref[half] = far_row(right_ref[0])
+    if part == 0:
+        centre = centre_of(pts0[half])
+        coords = halo[2 * half * rows :, :].astype(f32)
+        for h in range(half):
+            right_ref[h] = features(coords[h * feat : (h + 1) * feat], centre)[1]
+        right_ref[half] = far_row(right_ref[0])
     order = [group * half + v for v in range(half)]
+    for copy in copies:
+        copy.wait()
     found = collect(
         ids,
         count,
@@ -275,33 +302,44 @@
         list_v,
         list_n,
     )
+    mine = slice(0, rows) if part else slice(rows, 4 * rows)
 
     def add(i):
         v = list_v[i]
         h = list_n[i]
-        values = kernel_values(dot(left_ref[v], right_ref[h]))
-        acc[v] += dot(values, halo[jnp.minimum(h, half - 1), : 2 * rows, :])
+        values = kernel_values(dot(left_ref[v, mine, :], right_ref[h]))
+        start = pl.multiple_of(jnp.minimum(h, half - 1) * (2 * rows), 2 * rows)
+        acc[v, mine, :] += dot(values, halo[pl.ds(start, 2 * rows), :])
 
     for_each(found, add)
-    keep[...] = acc[:, :rows, :]
-    for d, send in enumerate((send1, send2, send3)):
-        send[...] = acc[:, (d + 1) * rows : (d + 2) * rows, :].astype(bf16)
-
-
-def finish_kernel(keep, back1, back2, back3, wide, near, top):
-    half = near.shape[0] // 2
+    if part == 0:
+        for d, send in enumerate((send1, send2, send3)):
+            send[...] = acc[:, (d + 1) * rows : (d + 2) * rows, :].astype(bf16)
+    else:
+        keep[...] = acc[:, :rows, :]
+
+
+def finish_kernel(keep, back1, back2, back3, wide, near, top, held, sem, top_sem):
+    half = held.shape[0] // 2
     _, group, _ = position()
-    near[pl.ds(group * half, half)] = (keep[...] + back2[...].astype(f32)).astype(bf16)
-    near[pl.ds((1 - group) * half, half)] = (back1[...].astype(f32) + back3[...].astype(f32)).astype(bf16)
-    top[0] = wide[...]
-
-
-def call(body, out_shape, specs, micros, scratch=(), aliases={}):
+    copies = [pltpu.make_async_copy(wide, top.at[0], top_sem)]
+    copies[0].start()
+    for side, (one, two) in enumerate(((keep, back2), (back1, back3))):
+        for i in range(half):
+            j = side * half + i
+            held[j] = (one[i].astype(f32) + two[i].astype(f32)).astype(bf16)
+            copies.append(pltpu.make_async_copy(held.at[j], near.at[(group ^ side) * half + i], sem.at[j]))
+            copies[-1].start()
+    for copy in copies:
+        copy.wait()
+
+
+def call(body, out_shape, specs, micros, scratch=(), aliases={}, out_spec=VMEM):
     return pl.pallas_call(
         body,
         out_shape=out_shape,
         in_specs=specs,
-        out_specs=jax.tree.map(lambda _: VMEM, out_shape),
+        out_specs=jax.tree.map(lambda _: out_spec, out_shape),
         scratch_shapes=list(scratch),
         input_output_aliases=aliases,
         compiler_params=pltpu.CompilerParams(vmem_limit_bytes=VMEM_LIMIT),
@@ -340,22 +378,30 @@
 
     got = [to_tile(points, d) for d in range(1, 4)]
     mate = to_tile(charges, 1)
-    charges = call(load_kernel, shape(*charges.shape), [VMEM], COST["load"])(charges)
+    merge_pv = jnp.transpose(merge_pivots, (1, 0, 2))
+    arguments = [points, charges, leaf_pivots, merge_pv, near_ids, near_count]
+    points, charges, leaf_pv, merge_pv, near_ids, near_count = call(
+        load_kernel,
+        tuple(jax.ShapeDtypeStruct(x.shape, x.dtype) for x in arguments),
+        [HBM] * len(arguments),
+        COST["load"],
+        [pltpu.SemaphoreType.DMA((len(arguments),))],
+    )(*[pltpu.with_memory_space_constraint(x, pltpu.HBM) for x in arguments])
     to_send, joined = call(
-        stage_kernel, (shape(half, 2 * rows + 16, probes), shape(boxes, 2 * rows, probes)), [VMEM] * 4 + [ANY], COST["stage"]
+        stage_kernel, (shape(half * (2 * rows + feat), probes), shape(boxes, 2 * rows, probes)), [VMEM] * 4 + [ANY], COST["stage"]
     )(points, got[0], charges, mate, got[2])
     halo = to_halo(to_send)
     pts = [points] + got
 
-    merge_pv = jnp.transpose(merge_pivots, (1, 0, 2))
     width = probes // tiles
     wide_shape = shape(width + 16, rank)
     mine, *sends = call(tree_kernel, (wide_shape,) * 4, [VMEM] * 7, COST["tree"], [pltpu.VMEM((probes, rank), f32)])(
-        *pts, joined, leaf_pivots, merge_pv
+        *pts, joined, leaf_pv, merge_pv
     )
     others = [to_tile(sends[d - 1], d) for d in range(1, 4)]
 
     lists = [pltpu.SMEM((half * near_ids.shape[1] + 4,), jnp.int32)] * 2
+    lists += [pltpu.SMEM(x.shape, jnp.int32) for x in (near_ids, near_count)] + [pltpu.SemaphoreType.DMA((2,))]
 
     sums = (
         shape(half, 4 * rows, probes, dtype=f32),
@@ -364,7 +410,7 @@
     )
 
     def near_own(part, begun, after):
-        specs = [SMEM] * 2 + [VMEM] * (5 + len(begun)) + [ANY]
+        specs = [ANY] * 2 + [VMEM] * (5 + len(begun)) + [ANY]
         aliases = {7 + i: i for i in range(len(begun))}
         return call(functools.partial(near_own_kernel, part), sums, specs, COST["own"], lists, aliases)(
             near_ids, near_count, *pts, joined, *begun, after
@@ -376,15 +422,25 @@
     )
     total, left, _ = near_own(1, begun, wide)
     other = partner(wide, 1)
-    keep, *sends = call(
-        near_halo_kernel,
-        (shape(half, rows, probes, dtype=f32),) + (shape(half, rows, probes),) * 3 + sums[:1],
-        [SMEM] * 2 + [VMEM] * 4 + [ANY],
+    quarter = shape(half, rows, probes)
+    inputs = (near_ids, near_count, points)
+    *sends, total, right = call(
+        functools.partial(near_halo_kernel, 0),
+        (quarter, quarter, quarter, sums[0], shape(half + 1, 48, 2 * rows)),
+        [ANY] * 2 + [VMEM] * 4 + [ANY],
         COST["halo"],
-        [pltpu.VMEM((half + 1, 48, 2 * rows), bf16)] + lists,
-        {3: 4},
-    )(near_ids, near_count, points, total, left, halo, other)
+        lists,
+        {3: 3},
+    )(*inputs, total, left, halo, other)
     back = [to_tile(sends[d - 1], d) for d in range(1, 4)]
+    keep, _ = call(
+        functools.partial(near_halo_kernel, 1),
+        (shape(half, rows, probes, dtype=f32), sums[0]),
+        [ANY] * 2 + [VMEM] * 4 + [ANY, VMEM],
+        COST["rest"],
+        lists,
+        {3: 1},
+    )(*inputs, total, left, halo, back[0], right)
 
     wide = call(functools.partial(merge_kernel, local_levels, 0), wide_shape, [VMEM] * 3 + [ANY], COST["merge"])(
         wide, other, merge_pv, back[0]
@@ -393,7 +449,13 @@
         wide, partner(wide, 2), partner(wide, 4), partner(wide, 6), merge_pv
     )
     near, top = call(
-        finish_kernel, (shape(boxes, rows, probes), shape(1, width, rank)), [VMEM] * 5, COST["finish"]
+        finish_kernel,
+        (shape(boxes, rows, probes), shape(1, width, rank)),
+        [VMEM] * 5,
+        COST["finish"],
+        [pltpu.VMEM((boxes, rows, probes), bf16), pltpu.SemaphoreType.DMA((boxes,)), pltpu.SemaphoreType.DMA],
+        {},
+        HBM,
     )(keep, *back, top)
     return near, jnp.swapaxes(top, 1, 2)
 

time: 41.1 us -> 40 us (0.973)
  local copies, waits for them, and re-layouts: 1.78 us -> 0 us
  waiting for transfers between devices: 7.19 us -> 7.86 us
    pallas_call x3 -> x4, Pallas kernels: 1.2 us -> 3.09 us  [the longest x1 1.12 us: on_device(): call(load_kernel, tuple((jax.ShapeDtypeStruct(x.shape, x.dtype) for x in...]
    unnamed x14 -> x0, local copies, waits for them, and re-layouts: 1.78 us -> none
    pallas_call x2, Pallas kernels: 4.35 us -> 3.11 us  [near_own(): call(functools.partial(near_own_kernel, part), sums, specs, COST['own'],...]
    ppermute x4, starting transfers between devices: 7.01 us -> 6.25 us  [partner(): return lax.ppermute(x, 'cluster', route)]
    ppermute x10, waiting for transfers between devices: 1.23 us -> 1.99 us  [to_tile(): return lax.ppermute(x, 'tile', [(i, i ^ d) for i in range(tiles)])]
  transfers between devices with their start and end apart: 15 -> 15, of which waited for: 5 -> 6; matrix products, arithmetic and copies ran while one was open for 0% -> 0% of each run, Pallas kernels for 27% -> 29%
where the time goes in v3:
time: 40 us; the launch traced here: 39.8 us
  starting transfers between devices  17.6 us (44%)
  Pallas kernels  13.3 us (33%)
  waiting for transfers between devices  7.86 us (20%)
  between operations  0.98 us (2%)
    ppermute x10, starting transfers between devices, to_tile(): return lax.ppermute(x, 'tile', [(i, i ^ d) for i in range(tiles)])  7.44 us
    ppermute x4, starting transfers between devices, partner(): return lax.ppermute(x, 'cluster', route)  6.25 us
    ppermute x4, waiting for transfers between devices, partner(): return lax.ppermute(x, 'cluster', route)  5.88 us
    ppermute x1, starting transfers between devices, to_halo(): return lax.ppermute(x, ('cluster', 'tile'), route)  3.95 us
    pallas_call x2, Pallas kernels, near_own(): call(functools.partial(near_own_kernel, part), sums, specs, COST['own'],...  3.11 us
    pallas_call x1, Pallas kernels, on_device(): call(tree_kernel, (wide_shape,) * 4, [VMEM] * 7, COST['tree'], [pltpu.VME...  2.41 us
    pallas_call x1, Pallas kernels, on_device(): call(functools.partial(top_kernel, local_levels + 1, 1), shape(width, ran...  2.28 us
    ppermute x10, waiting for transfers between devices, to_tile(): return lax.ppermute(x, 'tile', [(i, i ^ d) for i in range(tiles)])  1.99 us
  transfers between devices with their start and end apart: 15, of which 6 were waited for; matrix products, arithmetic and copies ran while one was open for 0% of the time, Pallas kernels for 29%

profile of v3, /device:TPU:0, one launch (start us, length us, event | category | flops | bytes accessed | tf_op | source)
XLA Modules:
  0.0 39.8 jit_solution(5342129100485284831)
XLA Ops:
  0.6 0.5 %collective-permute-start.3 = (bf16[8,128,256]{2,1,0:T(8,128)(2,1)}, bf16[8,128,256]{2,1,0:T(8,128)(2,1)S(1)}, u32[]{:S(2)}, u32[]{:S(2)}) collective-permute-start(bf16[8,128,256]{2,1,0:T(8,128)(2,1)} %refs_1_.1), channel_id=1, source_target_pairs={{0,1},{1,0},{2,3},{3,2},{4,5},{5,4},{6,7},{7,6},{8,9},{9,8},{10,11... | collective-permute-start | bytes 1572872 | tf_op jit(solution)/shard_map/ppermute | solution.py:361
  1.1 0.1 collective-permute-start
  1.2 2.6 %collective-permute-start.2 = (bf16[8,8,128]{2,1,0:T(8,128)(2,1)}, bf16[8,8,128]{2,1,0:T(8,128)(2,1)S(1)}, u32[]{:S(2)}, u32[]{:S(2)}) collective-permute-start(bf16[8,8,128]{2,1,0:T(8,128)(2,1)} %refs_0_.1), channel_id=1, source_target_pairs={{0,3},{1,2},{2,1},{3,0},{4,7},{5,6},{6,5},{7,4},{8,11},{9,10},{10,... | collective-permute-start | bytes 49160 | tf_op jit(solution)/shard_map/ppermute | solution.py:361
  3.9 0.4 collective-permute-start.1
  4.2 1.1 %shard_map.77 = (bf16[8,8,128]{2,1,0:T(8,128)(2,1)S(1)}, bf16[8,128,256]{2,1,0:T(8,128)(2,1)S(1)}, s32[8,256]{1,0:T(8,128)S(1)}, s32[6,4,256]{2,1,0:T(4,128)S(1)}, s32[8,8]{1,0:T(8,128)S(1)}, /*index=5*/s32[8]{0:T(128)S(1)}) custom-call(bf16[8,8,128]{2,1,0:T(8,128)(2,1)} %refs_0_.1, bf16[8,128,256]{2,1,0:T(8,128)(2,1)} %refs_1_.1, s32[8,256]{1,0:T(8,128)} %refs_2_.1, ...), custom_call_target="tpu_custom_call" | custom-call | flops 1100000 | bytes 1024 | tf_op jit(solution)/shard_map/pallas_call | solution.py:383
  5.3 0.0 collective-permute-done.got1.pts1
  5.3 0.2 collective-permute-done.2.after.pts3
  5.5 0.0 collective-permute-done.3.mate
  5.5 0.1 shard_map.78
  5.6 3.9 %collective-permute-start.7 = (bf16[1056,256]{1,0:T(8,128)(2,1)S(1)}, bf16[1056,256]{1,0:T(8,128)(2,1)S(1)}, u32[]{:S(2)}, u32[]{:S(2)}) collective-permute-start(bf16[1056,256]{1,0:T(8,128)(2,1)S(1)} %get-tuple-element.43), channel_id=1, source_target_pairs={{0,4},{2,6},{4,8},{5,1},{6,10},{7,3},{8,12},{9,5},{10,14},{11,7},{... | collective-permute-start | bytes 1622024 | tf_op jit(solution)/shard_map/ppermute | solution.py:370
  9.6 0.0 collective-permute-done.1.pts2
  9.6 2.4 %shard_map.79 = (bf16[80,256]{1,0:T(8,128)(2,1)S(1)}, bf16[80,256]{1,0:T(8,128)(2,1)S(1)}, bf16[80,256]{1,0:T(8,128)(2,1)S(1)}, bf16[80,256]{1,0:T(8,128)(2,1)S(1)}) custom-call(bf16[8,8,128]{2,1,0:T(8,128)(2,1)S(1)} %get-tuple-element.29.points.pts0, bf16[8,8,128]{2,1,0:T(8,128)(2,1)S(1)} %collective-permute-done.got1.pts1, ...), custom_call_target="tpu_custom_call" | custom-call | flops 3300000000 | bytes 1024 | tf_op jit(solution)/shard_map/pallas_call | solution.py:398
  12.0 0.1 collective-permute-start.4
  12.1 1.6 %collective-permute-start.5 = (bf16[80,256]{1,0:T(8,128)(2,1)S(1)}, bf16[80,256]{1,0:T(8,128)(2,1)S(1)}, u32[]{:S(2)}, u32[]{:S(2)}) collective-permute-start(bf16[80,256]{1,0:T(8,128)(2,1)S(1)} %get-tuple-element.39), channel_id=1, source_target_pairs={{0,2},{1,3},{2,0},{3,1},{4,6},{5,7},{6,4},{7,5},{8,10},{9,11},{10,... | collective-permute-start | bytes 122888 | tf_op jit(solution)/shard_map/ppermute | solution.py:361
  13.7 0.3 collective-permute-start.6
  13.9 1.4 %shard_map.80 = (f32[4,512,256]{2,1,0:T(8,128)S(1)}, bf16[4,512,48]{2,1,0:T(8,128)(2,1)S(1)}, bf16[9,48,256]{2,1,0:T(8,128)(2,1)S(1)}) custom-call(s32[8,8]{1,0:T(8,128)S(1)} %get-tuple-element.27.all_ids, s32[8]{0:T(128)S(1)} %get-tuple-element.28.all_counts, bf16[8,8,128]{2,1,0:T(8,128)(2,1)S(1)} %get-tuple-element.29.points.pts0, ...), custom_call_target="tpu_custom_call" | custom-call | flops 1100000000 | bytes 1024 | tf_op jit(solution)/shard_map/pallas_call | solution.py:415
  15.4 0.0 collective-permute-done.4.got1
  15.4 0.8 %collective-permute-done.5.got2 = bf16[80,256]{1,0:T(8,128)(2,1)S(1)} collective-permute-done((bf16[80,256]{1,0:T(8,128)(2,1)S(1)}, bf16[80,256]{1,0:T(8,128)(2,1)S(1)}, u32[]{:S(2)}, u32[]{:S(2)}) %collective-permute-start.5) | collective-permute-done | bytes 40992 | tf_op jit(solution)/shard_map/ppermute | solution.py:361
  16.2 1.0 %collective-permute-done.6.got3 = bf16[80,256]{1,0:T(8,128)(2,1)S(1)} collective-permute-done((bf16[80,256]{1,0:T(8,128)(2,1)S(1)}, bf16[80,256]{1,0:T(8,128)(2,1)S(1)}, u32[]{:S(2)}, u32[]{:S(2)}) %collective-permute-start.6) | collective-permute-done | bytes 40992 | tf_op jit(solution)/shard_map/ppermute | solution.py:361
  17.2 0.6 %shard_map.81.refs_3_.mine = bf16[80,256]{1,0:T(8,128)(2,1)S(1)} custom-call(bf16[80,256]{1,0:T(8,128)(2,1)S(1)} %get-tuple-element.34.refs_0_.mine, bf16[80,256]{1,0:T(8,128)(2,1)S(1)} %collective-permute-done.4.got1, bf16[80,256]{1,0:T(8,128)(2,1)S(1)} %collective-permute-done.5.got2, bf16[80,256]{1,0:T(8,128)(2,1)S(1)} %collective-permute-done.6.got3, ...), custom_call_target="tpu_custom_call" | custom-call | flops 1100000000 | bytes 1024 | tf_op jit(solution)/shard_map/pallas_call | solution.py:420
  17.8 1.6 %collective-permute-start.8 = (bf16[80,256]{1,0:T(8,128)(2,1)S(1)}, bf16[80,256]{1,0:T(8,128)(2,1)S(1)}, u32[]{:S(2)}, u32[]{:S(2)}) collective-permute-start(bf16[80,256]{1,0:T(8,128)(2,1)S(1)} %shard_map.81.refs_3_.mine), channel_id=1, source_target_pairs={{0,4},{4,0},{8,12},{12,8},{16,20},{20,16},{24,28},{28,24},{1,5},{5... | collective-permute-start | bytes 122888 | tf_op jit(solution)/shard_map/ppermute | solution.py:374
  19.4 1.7 %shard_map.82 = (f32[4,512,256]{2,1,0:T(8,128)S(1)}, bf16[4,512,48]{2,1,0:T(8,128)(2,1)S(1)}, bf16[9,48,256]{2,1,0:T(8,128)(2,1)S(1)}) custom-call(s32[8,8]{1,0:T(8,128)S(1)} %get-tuple-element.27.all_ids, s32[8]{0:T(128)S(1)} %get-tuple-element.28.all_counts, ...), custom_call_target="tpu_custom_call", output_to_operand_aliasing={{0}: (7, {}), {1}: (8, {}), {2}: (9, {})} | custom-call | flops 1100000000 | bytes 1024 | tf_op jit(solution)/shard_map/pallas_call | solution.py:415
  21.1 2.0 %collective-permute-done.8.after.got = bf16[80,256]{1,0:T(8,128)(2,1)S(1)} collective-permute-done((bf16[80,256]{1,0:T(8,128)(2,1)S(1)}, bf16[80,256]{1,0:T(8,128)(2,1)S(1)}, u32[]{:S(2)}, u32[]{:S(2)}) %collective-permute-start.8) | collective-permute-done | bytes 40992 | tf_op jit(solution)/shard_map/ppermute | solution.py:374
  23.1 0.0 collective-permute-done.7.halo
  23.1 1.0 %shard_map.83 = (bf16[4,128,256]{2,1,0:T(8,128)(2,1)S(1)}, bf16[4,128,256]{2,1,0:T(8,128)(2,1)S(1)}, bf16[4,128,256]{2,1,0:T(8,128)(2,1)S(1)}, f32[4,512,256]{2,1,0:T(8,128)S(1)}, bf16[5,48,256]{2,1,0:T(8,128)(2,1)S(1)}) custom-call(s32[8,8]{1,0:T(8,128)S(1)} %get-tuple-element.27.all_ids, ...), custom_call_target="tpu_custom_call", output_to_operand_aliasing={{3}: (3, {})} | custom-call | flops 5500000256 | bytes 1024 | tf_op jit(solution)/shard_map/pallas_call | solution.py:427
  24.1 0.1 collective-permute-start.9
  24.2 1.6 %collective-permute-start.10 = (bf16[4,128,256]{2,1,0:T(8,128)(2,1)S(1)}, bf16[4,128,256]{2,1,0:T(8,128)(2,1)S(1)}, u32[]{:S(2)}, u32[]{:S(2)}) collective-permute-start(bf16[4,128,256]{2,1,0:T(8,128)(2,1)S(1)} %get-tuple-element.48), channel_id=1, source_target_pairs={{0,2},{1,3},{2,0},{3,1},{4,6},{5,7},{6,4},{7,5},{8,10},{9,11},{10,... | collective-permute-start | bytes 786440 | tf_op jit(solution)/shard_map/ppermute | solution.py:361
  25.8 0.3 collective-permute-start.11
  26.1 0.0 collective-permute-done.9.after.back1
  26.1 1.0 %shard_map.85.mine = bf16[80,256]{1,0:T(8,128)(2,1)S(1)} custom-call(bf16[80,256]{1,0:T(8,128)(2,1)S(1)} %shard_map.81.refs_3_.mine, bf16[80,256]{1,0:T(8,128)(2,1)S(1)} %collective-permute-done.8.after.got, s32[6,4,256]{2,1,0:T(4,128)S(1)} %get-tuple-element.33.merge_pv, bf16[4,128,256]{2,1,0:T(8,128)(2,1)S(1)} %collective-permute-done.9.after.back1), custom_call_target="tpu_custom_call" | custom-call | flops 1100000000 | bytes 1024 | tf_op jit(solution)/shard_map/pallas_call | solution.py:445
  27.0 3.9 %collective-permute-start.14 = (bf16[80,256]{1,0:T(8,128)(2,1)S(1)}, bf16[80,256]{1,0:T(8,128)(2,1)S(1)}, u32[]{:S(2)}, u32[]{:S(2)}) collective-permute-start(bf16[80,256]{1,0:T(8,128)(2,1)S(1)} %shard_map.85.mine), channel_id=1, source_target_pairs={{0,24},{4,28},{8,16},{12,20},{16,8},{20,12},{24,0},{28,4},{1,25},{... | collective-permute-start | bytes 122888 | tf_op jit(solution)/shard_map/ppermute | solution.py:374
  31.0 0.3 collective-permute-start.13
  31.2 0.5 %collective-permute-start.12 = (bf16[80,256]{1,0:T(8,128)(2,1)S(1)}, bf16[80,256]{1,0:T(8,128)(2,1)S(1)}, u32[]{:S(2)}, u32[]{:S(2)}) collective-permute-start(bf16[80,256]{1,0:T(8,128)(2,1)S(1)} %shard_map.85.mine), channel_id=1, source_target_pairs={{0,8},{4,12},{8,0},{12,4},{16,24},{20,28},{24,16},{28,20},{1,9},{5... | collective-permute-start | bytes 122888 | tf_op jit(solution)/shard_map/ppermute | solution.py:374
  31.7 0.8 %shard_map.84 = (f32[4,128,256]{2,1,0:T(8,128)S(1)}, f32[4,512,256]{2,1,0:T(8,128)S(1)}) custom-call(s32[8,8]{1,0:T(8,128)S(1)} %get-tuple-element.27.all_ids, s32[8]{0:T(128)S(1)} %get-tuple-element.28.all_counts, bf16[8,8,128]{2,1,0:T(8,128)(2,1)S(1)} %get-tuple-element.29.points.pts0, ...), custom_call_target="tpu_custom_call", output_to_operand_aliasing={{1}: (3, {})} | custom-call | flops 1100000000 | bytes 1024 | tf_op jit(solution)/shard_map/pallas_call | solution.py:436
  32.5 0.7 %collective-permute-done.14.got3 = bf16[80,256]{1,0:T(8,128)(2,1)S(1)} collective-permute-done((bf16[80,256]{1,0:T(8,128)(2,1)S(1)}, bf16[80,256]{1,0:T(8,128)(2,1)S(1)}, u32[]{:S(2)}, u32[]{:S(2)}) %collective-permute-start.14) | collective-permute-done | bytes 40992 | tf_op jit(solution)/shard_map/ppermute | solution.py:374
  33.3 3.2 %collective-permute-done.13.got2 = bf16[80,256]{1,0:T(8,128)(2,1)S(1)} collective-permute-done((bf16[80,256]{1,0:T(8,128)(2,1)S(1)}, bf16[80,256]{1,0:T(8,128)(2,1)S(1)}, u32[]{:S(2)}, u32[]{:S(2)}) %collective-permute-start.13) | collective-permute-done | bytes 40992 | tf_op jit(solution)/shard_map/ppermute | solution.py:374
  36.4 0.0 collective-permute-done.12.got1
  36.4 2.3 %shard_map.86.wide = bf16[64,256]{1,0:T(8,128)(2,1)S(1)} custom-call(bf16[80,256]{1,0:T(8,128)(2,1)S(1)} %shard_map.85.mine, bf16[80,256]{1,0:T(8,128)(2,1)S(1)} %collective-permute-done.12.got1, bf16[80,256]{1,0:T(8,128)(2,1)S(1)} %collective-permute-done.13.got2, bf16[80,256]{1,0:T(8,128)(2,1)S(1)} %collective-permute-done.14.got3, ...), custom_call_target="tpu_custom_call" | custom-call | flops 1100000000 | bytes 1024 | tf_op jit(solution)/shard_map/pallas_call | solution.py:448
  38.7 0.0 collective-permute-done.10.back2
  38.7 0.0 collective-permute-done.11.back3
  38.7 0.9 %shard_map.87 = (bf16[8,128,256]{2,1,0:T(8,128)(2,1)}, bf16[1,64,256]{2,1,0:T(8,128)(2,1)}) custom-call(f32[4,128,256]{2,1,0:T(8,128)S(1)} %get-tuple-element.47.keep, bf16[4,128,256]{2,1,0:T(8,128)(2,1)S(1)} %collective-permute-done.9.after.back1, bf16[4,128,256]{2,1,0:T(8,128)(2,1)S(1)} %collective-permute-done.10.back2, ...), custom_call_target="tpu_custom_call" | custom-call | flops 1100000 | bytes 1024 | tf_op jit(solution)/shard_map/pallas_call | solution.py:451
Async XLA Ops:
  0.6 4.9 %collective-permute-start.3 = (bf16[8,128,256]{2,1,0:T(8,128)(2,1)}, bf16[8,128,256]{2,1,0:T(8,128)(2,1)S(1)}, u32[]{:S(2)}, u32[]{:S(2)}) collective-permute-start(bf16[8,128,256]{2,1,0:T(8,128)(2,1)} %refs_1_.1), channel_id=1, source_target_pairs={{0,1},{1,0},{2,3},{3,2},{4,5},{5,4},{6,7},{7,6},{8,9},{9,8},{10,11... | collective-permute-start | bytes 1572872 | tf_op jit(solution)/shard_map/ppermute | solution.py:361
  1.1 4.2 %collective-permute-start = (bf16[8,8,128]{2,1,0:T(8,128)(2,1)}, bf16[8,8,128]{2,1,0:T(8,128)(2,1)S(1)}, u32[]{:S(2)}, u32[]{:S(2)}) collective-permute-start(bf16[8,8,128]{2,1,0:T(8,128)(2,1)} %refs_0_.1), channel_id=1, source_target_pairs={{0,1},{1,0},{2,3},{3,2},{4,5},{5,4},{6,7},{7,6},{8,9},{9,8},{10,11... | collective-permute-start | bytes 49160 | tf_op jit(solution)/shard_map/ppermute | solution.py:361
  1.2 4.3 %collective-permute-start.2 = (bf16[8,8,128]{2,1,0:T(8,128)(2,1)}, bf16[8,8,128]{2,1,0:T(8,128)(2,1)S(1)}, u32[]{:S(2)}, u32[]{:S(2)}) collective-permute-start(bf16[8,8,128]{2,1,0:T(8,128)(2,1)} %refs_0_.1), channel_id=1, source_target_pairs={{0,3},{1,2},{2,1},{3,0},{4,7},{5,6},{6,5},{7,4},{8,11},{9,10},{10,... | collective-permute-start | bytes 49160 | tf_op jit(solution)/shard_map/ppermute | solution.py:361
  3.9 5.7 %collective-permute-start.1 = (bf16[8,8,128]{2,1,0:T(8,128)(2,1)}, bf16[8,8,128]{2,1,0:T(8,128)(2,1)S(1)}, u32[]{:S(2)}, u32[]{:S(2)}) collective-permute-start(bf16[8,8,128]{2,1,0:T(8,128)(2,1)} %refs_0_.1), channel_id=1, source_target_pairs={{0,2},{1,3},{2,0},{3,1},{4,6},{5,7},{6,4},{7,5},{8,10},{9,11},{10,... | collective-permute-start | bytes 49160 | tf_op jit(solution)/shard_map/ppermute | solution.py:361
  5.6 17.5 %collective-permute-start.7 = (bf16[1056,256]{1,0:T(8,128)(2,1)S(1)}, bf16[1056,256]{1,0:T(8,128)(2,1)S(1)}, u32[]{:S(2)}, u32[]{:S(2)}) collective-permute-start(bf16[1056,256]{1,0:T(8,128)(2,1)S(1)} %get-tuple-element.43), channel_id=1, source_target_pairs={{0,4},{2,6},{4,8},{5,1},{6,10},{7,3},{8,12},{9,5},{10,14},{11,7},{... | collective-permute-start | bytes 1622024 | tf_op jit(solution)/shard_map/ppermute | solution.py:370
  12.0 3.4 %collective-permute-start.4 = (bf16[80,256]{1,0:T(8,128)(2,1)S(1)}, bf16[80,256]{1,0:T(8,128)(2,1)S(1)}, u32[]{:S(2)}, u32[]{:S(2)}) collective-permute-start(bf16[80,256]{1,0:T(8,128)(2,1)S(1)} %get-tuple-element.38), channel_id=1, source_target_pairs={{0,1},{1,0},{2,3},{3,2},{4,5},{5,4},{6,7},{7,6},{8,9},{9,8},{10,11... | collective-permute-start | bytes 122888 | tf_op jit(solution)/shard_map/ppermute | solution.py:361
  12.1 4.1 %collective-permute-start.5 = (bf16[80,256]{1,0:T(8,128)(2,1)S(1)}, bf16[80,256]{1,0:T(8,128)(2,1)S(1)}, u32[]{:S(2)}, u32[]{:S(2)}) collective-permute-start(bf16[80,256]{1,0:T(8,128)(2,1)S(1)} %get-tuple-element.39), channel_id=1, source_target_pairs={{0,2},{1,3},{2,0},{3,1},{4,6},{5,7},{6,4},{7,5},{8,10},{9,11},{10,... | collective-permute-start | bytes 122888 | tf_op jit(solution)/shard_map/ppermute | solution.py:361
  13.7 3.5 %collective-permute-start.6 = (bf16[80,256]{1,0:T(8,128)(2,1)S(1)}, bf16[80,256]{1,0:T(8,128)(2,1)S(1)}, u32[]{:S(2)}, u32[]{:S(2)}) collective-permute-start(bf16[80,256]{1,0:T(8,128)(2,1)S(1)} %get-tuple-element.40), channel_id=1, source_target_pairs={{0,3},{1,2},{2,1},{3,0},{4,7},{5,6},{6,5},{7,4},{8,11},{9,10},{10,... | collective-permute-start | bytes 122888 | tf_op jit(solution)/shard_map/ppermute | solution.py:361
  17.8 5.3 %collective-permute-start.8 = (bf16[80,256]{1,0:T(8,128)(2,1)S(1)}, bf16[80,256]{1,0:T(8,128)(2,1)S(1)}, u32[]{:S(2)}, u32[]{:S(2)}) collective-permute-start(bf16[80,256]{1,0:T(8,128)(2,1)S(1)} %shard_map.81.refs_3_.mine), channel_id=1, source_target_pairs={{0,4},{4,0},{8,12},{12,8},{16,20},{20,16},{24,28},{28,24},{1,5},{5... | collective-permute-start | bytes 122888 | tf_op jit(solution)/shard_map/ppermute | solution.py:374
  24.1 1.9 %collective-permute-start.9 = (bf16[4,128,256]{2,1,0:T(8,128)(2,1)S(1)}, bf16[4,128,256]{2,1,0:T(8,128)(2,1)S(1)}, u32[]{:S(2)}, u32[]{:S(2)}) collective-permute-start(bf16[4,128,256]{2,1,0:T(8,128)(2,1)S(1)} %get-tuple-element.45), channel_id=1, source_target_pairs={{0,1},{1,0},{2,3},{3,2},{4,5},{5,4},{6,7},{7,6},{8,9},{9,8},{10,11... | collective-permute-start | bytes 786440 | tf_op jit(solution)/shard_map/ppermute | solution.py:361
  24.2 14.5 %collective-permute-start.10 = (bf16[4,128,256]{2,1,0:T(8,128)(2,1)S(1)}, bf16[4,128,256]{2,1,0:T(8,128)(2,1)S(1)}, u32[]{:S(2)}, u32[]{:S(2)}) collective-permute-start(bf16[4,128,256]{2,1,0:T(8,128)(2,1)S(1)} %get-tuple-element.48), channel_id=1, source_target_pairs={{0,2},{1,3},{2,0},{3,1},{4,6},{5,7},{6,4},{7,5},{8,10},{9,11},{10,... | collective-permute-start | bytes 786440 | tf_op jit(solution)/shard_map/ppermute | solution.py:361
  25.8 12.9 %collective-permute-start.11 = (bf16[4,128,256]{2,1,0:T(8,128)(2,1)S(1)}, bf16[4,128,256]{2,1,0:T(8,128)(2,1)S(1)}, u32[]{:S(2)}, u32[]{:S(2)}) collective-permute-start(bf16[4,128,256]{2,1,0:T(8,128)(2,1)S(1)} %get-tuple-element.49), channel_id=1, source_target_pairs={{0,3},{1,2},{2,1},{3,0},{4,7},{5,6},{6,5},{7,4},{8,11},{9,10},{10,... | collective-permute-start | bytes 786440 | tf_op jit(solution)/shard_map/ppermute | solution.py:361
  27.0 6.2 %collective-permute-start.14 = (bf16[80,256]{1,0:T(8,128)(2,1)S(1)}, bf16[80,256]{1,0:T(8,128)(2,1)S(1)}, u32[]{:S(2)}, u32[]{:S(2)}) collective-permute-start(bf16[80,256]{1,0:T(8,128)(2,1)S(1)} %shard_map.85.mine), channel_id=1, source_target_pairs={{0,24},{4,28},{8,16},{12,20},{16,8},{20,12},{24,0},{28,4},{1,25},{... | collective-permute-start | bytes 122888 | tf_op jit(solution)/shard_map/ppermute | solution.py:374
  31.0 5.5 %collective-permute-start.13 = (bf16[80,256]{1,0:T(8,128)(2,1)S(1)}, bf16[80,256]{1,0:T(8,128)(2,1)S(1)}, u32[]{:S(2)}, u32[]{:S(2)}) collective-permute-start(bf16[80,256]{1,0:T(8,128)(2,1)S(1)} %shard_map.85.mine), channel_id=1, source_target_pairs={{0,16},{4,20},{8,24},{12,28},{16,0},{20,4},{24,8},{28,12},{1,17},{... | collective-permute-start | bytes 122888 | tf_op jit(solution)/shard_map/ppermute | solution.py:374
  31.2 5.2 %collective-permute-start.12 = (bf16[80,256]{1,0:T(8,128)(2,1)S(1)}, bf16[80,256]{1,0:T(8,128)(2,1)S(1)}, u32[]{:S(2)}, u32[]{:S(2)}) collective-permute-start(bf16[80,256]{1,0:T(8,128)(2,1)S(1)} %shard_map.85.mine), channel_id=1, source_target_pairs={{0,8},{4,12},{8,0},{12,4},{16,24},{20,28},{24,16},{28,20},{1,9},{5... | collective-permute-start | bytes 122888 | tf_op jit(solution)/shard_map/ppermute | solution.py:374

commit v4 on v3

--- a/solution.py
+++ b/solution.py
@@ -12,7 +12,7 @@
 lengthscale = 0.7
 KAPPA = math.log2(math.e) / lengthscale
 FLOOR = 1e-30
-COST = dict(load=0.001, stage=0.001, tree=3, own=1, join=1, merge=1, halo=5, rest=1, finish=0.001)
+COST = dict(load=0.001, stage=0.001, tree=3, own=1, join=1, merge=5, halo=5, rest=1, top=0.001, finish=0.001)
 VMEM_LIMIT = 16 * 1024 * 1024
 f32 = jnp.float32
 bf16 = jnp.bfloat16
@@ -274,7 +274,7 @@
 
 def near_halo_kernel(part, all_ids, all_counts, pts0, total, left_ref, halo, after, *refs):
     if part == 0:
-        send1, send2, send3, acc, right_ref, list_v, list_n, ids, count, sem = refs
+        send1, send2, send3, acc, right_ref, mark, list_v, list_n, ids, count, sem = refs
     else:
         right_ref, keep, acc, list_v, list_n, ids, count, sem = refs
     copies = start_copies([(all_ids, ids), (all_counts, count)], sem)
@@ -313,10 +313,15 @@
 
     for_each(found, add)
     if part == 0:
+        mark[...] = jnp.zeros_like(mark)
         for d, send in enumerate((send1, send2, send3)):
             send[...] = acc[:, (d + 1) * rows : (d + 2) * rows, :].astype(bf16)
     else:
         keep[...] = acc[:, :rows, :]
+
+
+def pass_kernel(given, after, out):
+    out[...] = given[...]
 
 
 def finish_kernel(keep, back1, back2, back3, wide, near, top, held, sem, top_sem):
@@ -424,15 +429,16 @@
     other = partner(wide, 1)
     quarter = shape(half, rows, probes)
     inputs = (near_ids, near_count, points)
-    *sends, total, right = call(
+    *sends, total, right, mark = call(
         functools.partial(near_halo_kernel, 0),
-        (quarter, quarter, quarter, sums[0], shape(half + 1, 48, 2 * rows)),
+        (quarter, quarter, quarter, sums[0], shape(half + 1, 48, 2 * rows), shape(16, 128)),
         [ANY] * 2 + [VMEM] * 4 + [ANY],
         COST["halo"],
         lists,
         {3: 3},
-    )(*inputs, total, left, halo, other)
-    back = [to_tile(sends[d - 1], d) for d in range(1, 4)]
+    )(*inputs, total, left, halo, left)
+    back2, back3, back1 = [to_tile(sends[d - 1], d) for d in (2, 3, 1)]
+    back = [back1, back2, back3]
     keep, _ = call(
         functools.partial(near_halo_kernel, 1),
         (shape(half, rows, probes, dtype=f32), sums[0]),
@@ -443,9 +449,10 @@
     )(*inputs, total, left, halo, back[0], right)
 
     wide = call(functools.partial(merge_kernel, local_levels, 0), wide_shape, [VMEM] * 3 + [ANY], COST["merge"])(
-        wide, other, merge_pv, back[0]
-    )
-    top = call(functools.partial(top_kernel, local_levels + 1, 1), shape(width, rank), [VMEM] * 5, COST["merge"])(
+        wide, other, merge_pv, to_tile(mark, 1)
+    )
+    wide = call(pass_kernel, wide_shape, [VMEM, ANY], COST["load"])(wide, back[0])
+    top = call(functools.partial(top_kernel, local_levels + 1, 1), shape(width, rank), [VMEM] * 5, COST["top"])(
         wide, partner(wide, 2), partner(wide, 4), partner(wide, 6), merge_pv
     )
     near, top = call(

time: 40 us -> 39.8 us (level)
    ppermute x4, waiting for transfers between devices: 5.88 us -> 3.8 us  [partner(): return lax.ppermute(x, 'cluster', route)]
    ppermute x1, waiting for transfers between devices: 0.01 us -> 1.83 us  [to_halo(): return lax.ppermute(x, ('cluster', 'tile'), route)]
    ppermute x10 -> x11, starting transfers between devices: 7.44 us -> 7.6 us  [to_tile(): return lax.ppermute(x, 'tile', [(i, i ^ d) for i in range(tiles)])]
    ppermute x10 -> x11, waiting for transfers between devices: 1.99 us -> 1.99 us  [to_tile(): return lax.ppermute(x, 'tile', [(i, i ^ d) for i in range(tiles)])]
  transfers between devices with their start and end apart: 15 -> 16, of which waited for: 6 -> 6; matrix products, arithmetic and copies ran while one was open for 0% -> 0% of each run, Pallas kernels for 29% -> 31%
where the time goes in v4:
time: 39.8 us; the launch traced here: 39.6 us
  starting transfers between devices  18 us (45%)
  Pallas kernels  13 us (33%)
  waiting for transfers between devices  7.62 us (19%)
  between operations  1 us (3%)
    ppermute x11, starting transfers between devices, to_tile(): return lax.ppermute(x, 'tile', [(i, i ^ d) for i in range(tiles)])  7.6 us
    ppermute x4, starting transfers between devices, partner(): return lax.ppermute(x, 'cluster', route)  6.41 us
    ppermute x1, starting transfers between devices, to_halo(): return lax.ppermute(x, ('cluster', 'tile'), route)  3.95 us
    ppermute x4, waiting for transfers between devices, partner(): return lax.ppermute(x, 'cluster', route)  3.8 us
    pallas_call x2, Pallas kernels, near_own(): call(functools.partial(near_own_kernel, part), sums, specs, COST['own'],...  2.84 us
    pallas_call x1, Pallas kernels, on_device(): call(tree_kernel, (wide_shape,) * 4, [VMEM] * 7, COST['tree'], [pltpu.VME...  2.41 us
    pallas_call x1, Pallas kernels, on_device(): call(functools.partial(top_kernel, local_levels + 1, 1), shape(width, ran...  2.28 us
    ppermute x11, waiting for transfers between devices, to_tile(): return lax.ppermute(x, 'tile', [(i, i ^ d) for i in range(tiles)])  1.99 us
  transfers between devices with their start and end apart: 16, of which 6 were waited for; matrix products, arithmetic and copies ran while one was open for 0% of the time, Pallas kernels for 31%

profile of v4, /device:TPU:0, one launch (start us, length us, event | category | flops | bytes accessed | tf_op | source)
XLA Modules:
  0.0 39.6 jit_solution(5248474048388231291)
XLA Ops:
  0.6 0.5 %collective-permute-start.3 = (bf16[8,128,256]{2,1,0:T(8,128)(2,1)}, bf16[8,128,256]{2,1,0:T(8,128)(2,1)S(1)}, u32[]{:S(2)}, u32[]{:S(2)}) collective-permute-start(bf16[8,128,256]{2,1,0:T(8,128)(2,1)} %refs_1_.1), channel_id=1, source_target_pairs={{0,1},{1,0},{2,3},{3,2},{4,5},{5,4},{6,7},{7,6},{8,9},{9,8},{10,11... | collective-permute-start | bytes 1572872 | tf_op jit(solution)/shard_map/ppermute | solution.py:366
  1.1 0.1 collective-permute-start
  1.2 2.6 %collective-permute-start.2 = (bf16[8,8,128]{2,1,0:T(8,128)(2,1)}, bf16[8,8,128]{2,1,0:T(8,128)(2,1)S(1)}, u32[]{:S(2)}, u32[]{:S(2)}) collective-permute-start(bf16[8,8,128]{2,1,0:T(8,128)(2,1)} %refs_0_.1), channel_id=1, source_target_pairs={{0,3},{1,2},{2,1},{3,0},{4,7},{5,6},{6,5},{7,4},{8,11},{9,10},{10,... | collective-permute-start | bytes 49160 | tf_op jit(solution)/shard_map/ppermute | solution.py:366
  3.9 0.4 collective-permute-start.1
  4.2 1.1 %shard_map.77 = (bf16[8,8,128]{2,1,0:T(8,128)(2,1)S(1)}, bf16[8,128,256]{2,1,0:T(8,128)(2,1)S(1)}, s32[8,256]{1,0:T(8,128)S(1)}, s32[6,4,256]{2,1,0:T(4,128)S(1)}, s32[8,8]{1,0:T(8,128)S(1)}, /*index=5*/s32[8]{0:T(128)S(1)}) custom-call(bf16[8,8,128]{2,1,0:T(8,128)(2,1)} %refs_0_.1, bf16[8,128,256]{2,1,0:T(8,128)(2,1)} %refs_1_.1, s32[8,256]{1,0:T(8,128)} %refs_2_.1, ...), custom_call_target="tpu_custom_call" | custom-call | flops 1100000 | bytes 1024 | tf_op jit(solution)/shard_map/pallas_call | solution.py:388
  5.3 0.0 collective-permute-done.got1.pts1
  5.3 0.2 collective-permute-done.2.after.pts3
  5.5 0.0 collective-permute-done.3.mate
  5.5 0.1 shard_map.78
  5.6 3.9 %collective-permute-start.7 = (bf16[1056,256]{1,0:T(8,128)(2,1)S(1)}, bf16[1056,256]{1,0:T(8,128)(2,1)S(1)}, u32[]{:S(2)}, u32[]{:S(2)}) collective-permute-start(bf16[1056,256]{1,0:T(8,128)(2,1)S(1)} %get-tuple-element.44), channel_id=1, source_target_pairs={{0,4},{2,6},{4,8},{5,1},{6,10},{7,3},{8,12},{9,5},{10,14},{11,7},{... | collective-permute-start | bytes 1622024 | tf_op jit(solution)/shard_map/ppermute | solution.py:375
  9.6 0.0 collective-permute-done.1.pts2
  9.6 2.4 %shard_map.79 = (bf16[80,256]{1,0:T(8,128)(2,1)S(1)}, bf16[80,256]{1,0:T(8,128)(2,1)S(1)}, bf16[80,256]{1,0:T(8,128)(2,1)S(1)}, bf16[80,256]{1,0:T(8,128)(2,1)S(1)}) custom-call(bf16[8,8,128]{2,1,0:T(8,128)(2,1)S(1)} %get-tuple-element.30.points.pts0, bf16[8,8,128]{2,1,0:T(8,128)(2,1)S(1)} %collective-permute-done.got1.pts1, ...), custom_call_target="tpu_custom_call" | custom-call | flops 3300000000 | bytes 1024 | tf_op jit(solution)/shard_map/pallas_call | solution.py:403
  12.0 0.1 collective-permute-start.4
  12.1 1.6 %collective-permute-start.5 = (bf16[80,256]{1,0:T(8,128)(2,1)S(1)}, bf16[80,256]{1,0:T(8,128)(2,1)S(1)}, u32[]{:S(2)}, u32[]{:S(2)}) collective-permute-start(bf16[80,256]{1,0:T(8,128)(2,1)S(1)} %get-tuple-element.40), channel_id=1, source_target_pairs={{0,2},{1,3},{2,0},{3,1},{4,6},{5,7},{6,4},{7,5},{8,10},{9,11},{10,... | collective-permute-start | bytes 122888 | tf_op jit(solution)/shard_map/ppermute | solution.py:366
  13.7 0.3 collective-permute-start.6
  13.9 1.4 %shard_map.80 = (f32[4,512,256]{2,1,0:T(8,128)S(1)}, bf16[4,512,48]{2,1,0:T(8,128)(2,1)S(1)}, bf16[9,48,256]{2,1,0:T(8,128)(2,1)S(1)}) custom-call(s32[8,8]{1,0:T(8,128)S(1)} %get-tuple-element.28.all_ids, s32[8]{0:T(128)S(1)} %get-tuple-element.29.all_counts, bf16[8,8,128]{2,1,0:T(8,128)(2,1)S(1)} %get-tuple-element.30.points.pts0, ...), custom_call_target="tpu_custom_call" | custom-call | flops 1100000000 | bytes 1024 | tf_op jit(solution)/shard_map/pallas_call | solution.py:420
  15.4 0.0 collective-permute-done.4.got1
  15.4 0.8 %collective-permute-done.5.got2 = bf16[80,256]{1,0:T(8,128)(2,1)S(1)} collective-permute-done((bf16[80,256]{1,0:T(8,128)(2,1)S(1)}, bf16[80,256]{1,0:T(8,128)(2,1)S(1)}, u32[]{:S(2)}, u32[]{:S(2)}) %collective-permute-start.5) | collective-permute-done | bytes 40992 | tf_op jit(solution)/shard_map/ppermute | solution.py:366
  16.2 1.0 %collective-permute-done.6.got3 = bf16[80,256]{1,0:T(8,128)(2,1)S(1)} collective-permute-done((bf16[80,256]{1,0:T(8,128)(2,1)S(1)}, bf16[80,256]{1,0:T(8,128)(2,1)S(1)}, u32[]{:S(2)}, u32[]{:S(2)}) %collective-permute-start.6) | collective-permute-done | bytes 40992 | tf_op jit(solution)/shard_map/ppermute | solution.py:366
  17.2 0.6 %shard_map.81.refs_3_.mine = bf16[80,256]{1,0:T(8,128)(2,1)S(1)} custom-call(bf16[80,256]{1,0:T(8,128)(2,1)S(1)} %get-tuple-element.35.refs_0_.mine, bf16[80,256]{1,0:T(8,128)(2,1)S(1)} %collective-permute-done.4.got1, bf16[80,256]{1,0:T(8,128)(2,1)S(1)} %collective-permute-done.5.got2, bf16[80,256]{1,0:T(8,128)(2,1)S(1)} %collective-permute-done.6.got3, ...), custom_call_target="tpu_custom_call" | custom-call | flops 1100000000 | bytes 1024 | tf_op jit(solution)/shard_map/pallas_call | solution.py:425
  17.8 1.6 %collective-permute-start.11 = (bf16[80,256]{1,0:T(8,128)(2,1)S(1)}, bf16[80,256]{1,0:T(8,128)(2,1)S(1)}, u32[]{:S(2)}, u32[]{:S(2)}) collective-permute-start(bf16[80,256]{1,0:T(8,128)(2,1)S(1)} %shard_map.81.refs_3_.mine), channel_id=1, source_target_pairs={{0,4},{4,0},{8,12},{12,8},{16,20},{20,16},{24,28},{28,24},{1,5},{5... | collective-permute-start | bytes 122888 | tf_op jit(solution)/shard_map/ppermute | solution.py:379
  19.4 1.4 %shard_map.82 = (f32[4,512,256]{2,1,0:T(8,128)S(1)}, bf16[4,512,48]{2,1,0:T(8,128)(2,1)S(1)}, bf16[9,48,256]{2,1,0:T(8,128)(2,1)S(1)}) custom-call(s32[8,8]{1,0:T(8,128)S(1)} %get-tuple-element.28.all_ids, s32[8]{0:T(128)S(1)} %get-tuple-element.29.all_counts, ...), custom_call_target="tpu_custom_call", output_to_operand_aliasing={{0}: (7, {}), {1}: (8, {}), {2}: (9, {})} | custom-call | flops 1100000000 | bytes 1024 | tf_op jit(solution)/shard_map/pallas_call | solution.py:420
  20.8 1.8 %collective-permute-done.7.halo = bf16[1056,256]{1,0:T(8,128)(2,1)S(1)} collective-permute-done((bf16[1056,256]{1,0:T(8,128)(2,1)S(1)}, bf16[1056,256]{1,0:T(8,128)(2,1)S(1)}, u32[]{:S(2)}, u32[]{:S(2)}) %collective-permute-start.7) | collective-permute-done | bytes 540704 | tf_op jit(solution)/shard_map/ppermute | solution.py:375
  22.6 1.0 %shard_map.83 = (bf16[4,128,256]{2,1,0:T(8,128)(2,1)S(1)}, bf16[4,128,256]{2,1,0:T(8,128)(2,1)S(1)}, bf16[4,128,256]{2,1,0:T(8,128)(2,1)S(1)}, f32[4,512,256]{2,...) custom-call(s32[8,8]{1,0:T(8,128)S(1)} %get-tuple-element.28.all_ids, ...), custom_call_target="tpu_custom_call", output_to_operand_aliasing={{3}: (3, {})} | custom-call | flops 5500000256 | bytes 1024 | tf_op jit(solution)/shard_map/pallas_call | solution.py:432
  23.7 0.1 collective-permute-start.12
  23.8 0.5 %collective-permute-start.8 = (bf16[4,128,256]{2,1,0:T(8,128)(2,1)S(1)}, bf16[4,128,256]{2,1,0:T(8,128)(2,1)S(1)}, u32[]{:S(2)}, u32[]{:S(2)}) collective-permute-start(bf16[4,128,256]{2,1,0:T(8,128)(2,1)S(1)} %get-tuple-element.46), channel_id=1, source_target_pairs={{0,1},{1,0},{2,3},{3,2},{4,5},{5,4},{6,7},{7,6},{8,9},{9,8},{10,11... | collective-permute-start | bytes 786440 | tf_op jit(solution)/shard_map/ppermute | solution.py:366
  24.3 1.5 %collective-permute-start.9 = (bf16[4,128,256]{2,1,0:T(8,128)(2,1)S(1)}, bf16[4,128,256]{2,1,0:T(8,128)(2,1)S(1)}, u32[]{:S(2)}, u32[]{:S(2)}) collective-permute-start(bf16[4,128,256]{2,1,0:T(8,128)(2,1)S(1)} %get-tuple-element.49), channel_id=1, source_target_pairs={{0,2},{1,3},{2,0},{3,1},{4,6},{5,7},{6,4},{7,5},{8,10},{9,11},{10,... | collective-permute-start | bytes 786440 | tf_op jit(solution)/shard_map/ppermute | solution.py:366
  25.8 0.0 collective-permute-start.10
  25.8 0.0 collective-permute-done.11.got
  25.8 0.0 collective-permute-done.12.after
  25.8 1.0 %shard_map.85.given = bf16[80,256]{1,0:T(8,128)(2,1)S(1)} custom-call(bf16[80,256]{1,0:T(8,128)(2,1)S(1)} %shard_map.81.refs_3_.mine, bf16[80,256]{1,0:T(8,128)(2,1)S(1)} %collective-permute-done.11.got, s32[6,4,256]{2,1,0:T(4,128)S(1)} %get-tuple-element.34.merge_pv, bf16[16,128]{1,0:T(8,128)(2,1)S(1)} %collective-permute-done.12.after), custom_call_target="tpu_custom_call" | custom-call | flops 5500000256 | bytes 1024 | tf_op jit(solution)/shard_map/pallas_call | solution.py:451
  26.8 0.0 collective-permute-done.8.after.back1
  26.8 4.2 %collective-permute-start.15 = (bf16[80,256]{1,0:T(8,128)(2,1)S(1)}, bf16[80,256]{1,0:T(8,128)(2,1)S(1)}, u32[]{:S(2)}, u32[]{:S(2)}) collective-permute-start(bf16[80,256]{1,0:T(8,128)(2,1)S(1)} %shard_map.86.mine), channel_id=1, source_target_pairs={{0,24},{4,28},{8,16},{12,20},{16,8},{20,12},{24,0},{28,4},{1,25},{... | collective-permute-start | bytes 122888 | tf_op jit(solution)/shard_map/ppermute | solution.py:379
  31.0 0.0 collective-permute-start.14
  31.0 0.6 %collective-permute-start.13 = (bf16[80,256]{1,0:T(8,128)(2,1)S(1)}, bf16[80,256]{1,0:T(8,128)(2,1)S(1)}, u32[]{:S(2)}, u32[]{:S(2)}) collective-permute-start(bf16[80,256]{1,0:T(8,128)(2,1)S(1)} %shard_map.86.mine), channel_id=1, source_target_pairs={{0,8},{4,12},{8,0},{12,4},{16,24},{20,28},{24,16},{28,20},{1,9},{5... | collective-permute-start | bytes 122888 | tf_op jit(solution)/shard_map/ppermute | solution.py:379
  31.6 0.8 %shard_map.84 = (f32[4,128,256]{2,1,0:T(8,128)S(1)}, f32[4,512,256]{2,1,0:T(8,128)S(1)}) custom-call(s32[8,8]{1,0:T(8,128)S(1)} %get-tuple-element.28.all_ids, s32[8]{0:T(128)S(1)} %get-tuple-element.29.all_counts, bf16[8,8,128]{2,1,0:T(8,128)(2,1)S(1)} %get-tuple-element.30.points.pts0, ...), custom_call_target="tpu_custom_call", output_to_operand_aliasing={{1}: (3, {})} | custom-call | flops 1100000000 | bytes 1024 | tf_op jit(solution)/shard_map/pallas_call | solution.py:442
  32.5 0.7 %collective-permute-done.15.got3 = bf16[80,256]{1,0:T(8,128)(2,1)S(1)} collective-permute-done((bf16[80,256]{1,0:T(8,128)(2,1)S(1)}, bf16[80,256]{1,0:T(8,128)(2,1)S(1)}, u32[]{:S(2)}, u32[]{:S(2)}) %collective-permute-start.15) | collective-permute-done | bytes 40992 | tf_op jit(solution)/shard_map/ppermute | solution.py:379
  33.2 3.1 %collective-permute-done.14.got2 = bf16[80,256]{1,0:T(8,128)(2,1)S(1)} collective-permute-done((bf16[80,256]{1,0:T(8,128)(2,1)S(1)}, bf16[80,256]{1,0:T(8,128)(2,1)S(1)}, u32[]{:S(2)}, u32[]{:S(2)}) %collective-permute-start.14) | collective-permute-done | bytes 40992 | tf_op jit(solution)/shard_map/ppermute | solution.py:379
  36.2 0.0 collective-permute-done.13.got1
  36.3 2.3 %shard_map.87.wide = bf16[64,256]{1,0:T(8,128)(2,1)S(1)} custom-call(bf16[80,256]{1,0:T(8,128)(2,1)S(1)} %shard_map.86.mine, bf16[80,256]{1,0:T(8,128)(2,1)S(1)} %collective-permute-done.13.got1, bf16[80,256]{1,0:T(8,128)(2,1)S(1)} %collective-permute-done.14.got2, bf16[80,256]{1,0:T(8,128)(2,1)S(1)} %collective-permute-done.15.got3, ...), custom_call_target="tpu_custom_call" | custom-call | flops 1100000 | bytes 1024 | tf_op jit(solution)/shard_map/pallas_call | solution.py:455
  38.5 0.0 collective-permute-done.9.back2
  38.5 0.0 collective-permute-done.10.back3
  38.6 0.9 %shard_map.88 = (bf16[8,128,256]{2,1,0:T(8,128)(2,1)}, bf16[1,64,256]{2,1,0:T(8,128)(2,1)}) custom-call(f32[4,128,256]{2,1,0:T(8,128)S(1)} %get-tuple-element.48.keep, bf16[4,128,256]{2,1,0:T(8,128)(2,1)S(1)} %collective-permute-done.8.after.back1, bf16[4,128,256]{2,1,0:T(8,128)(2,1)S(1)} %collective-permute-done.9.back2, ...), custom_call_target="tpu_custom_call" | custom-call | flops 1100000 | bytes 1024 | tf_op jit(solution)/shard_map/pallas_call | solution.py:458
  (1 shorter events, 0.0 us)
Async XLA Ops:
  0.6 4.9 %collective-permute-start.3 = (bf16[8,128,256]{2,1,0:T(8,128)(2,1)}, bf16[8,128,256]{2,1,0:T(8,128)(2,1)S(1)}, u32[]{:S(2)}, u32[]{:S(2)}) collective-permute-start(bf16[8,128,256]{2,1,0:T(8,128)(2,1)} %refs_1_.1), channel_id=1, source_target_pairs={{0,1},{1,0},{2,3},{3,2},{4,5},{5,4},{6,7},{7,6},{8,9},{9,8},{10,11... | collective-permute-start | bytes 1572872 | tf_op jit(solution)/shard_map/ppermute | solution.py:366
  1.1 4.2 %collective-permute-start = (bf16[8,8,128]{2,1,0:T(8,128)(2,1)}, bf16[8,8,128]{2,1,0:T(8,128)(2,1)S(1)}, u32[]{:S(2)}, u32[]{:S(2)}) collective-permute-start(bf16[8,8,128]{2,1,0:T(8,128)(2,1)} %refs_0_.1), channel_id=1, source_target_pairs={{0,1},{1,0},{2,3},{3,2},{4,5},{5,4},{6,7},{7,6},{8,9},{9,8},{10,11... | collective-permute-start | bytes 49160 | tf_op jit(solution)/shard_map/ppermute | solution.py:366
  1.2 4.3 %collective-permute-start.2 = (bf16[8,8,128]{2,1,0:T(8,128)(2,1)}, bf16[8,8,128]{2,1,0:T(8,128)(2,1)S(1)}, u32[]{:S(2)}, u32[]{:S(2)}) collective-permute-start(bf16[8,8,128]{2,1,0:T(8,128)(2,1)} %refs_0_.1), channel_id=1, source_target_pairs={{0,3},{1,2},{2,1},{3,0},{4,7},{5,6},{6,5},{7,4},{8,11},{9,10},{10,... | collective-permute-start | bytes 49160 | tf_op jit(solution)/shard_map/ppermute | solution.py:366
  3.9 5.7 %collective-permute-start.1 = (bf16[8,8,128]{2,1,0:T(8,128)(2,1)}, bf16[8,8,128]{2,1,0:T(8,128)(2,1)S(1)}, u32[]{:S(2)}, u32[]{:S(2)}) collective-permute-start(bf16[8,8,128]{2,1,0:T(8,128)(2,1)} %refs_0_.1), channel_id=1, source_target_pairs={{0,2},{1,3},{2,0},{3,1},{4,6},{5,7},{6,4},{7,5},{8,10},{9,11},{10,... | collective-permute-start | bytes 49160 | tf_op jit(solution)/shard_map/ppermute | solution.py:366
  5.6 17.0 %collective-permute-start.7 = (bf16[1056,256]{1,0:T(8,128)(2,1)S(1)}, bf16[1056,256]{1,0:T(8,128)(2,1)S(1)}, u32[]{:S(2)}, u32[]{:S(2)}) collective-permute-start(bf16[1056,256]{1,0:T(8,128)(2,1)S(1)} %get-tuple-element.44), channel_id=1, source_target_pairs={{0,4},{2,6},{4,8},{5,1},{6,10},{7,3},{8,12},{9,5},{10,14},{11,7},{... | collective-permute-start | bytes 1622024 | tf_op jit(solution)/shard_map/ppermute | solution.py:375
  12.0 3.4 %collective-permute-start.4 = (bf16[80,256]{1,0:T(8,128)(2,1)S(1)}, bf16[80,256]{1,0:T(8,128)(2,1)S(1)}, u32[]{:S(2)}, u32[]{:S(2)}) collective-permute-start(bf16[80,256]{1,0:T(8,128)(2,1)S(1)} %get-tuple-element.39), channel_id=1, source_target_pairs={{0,1},{1,0},{2,3},{3,2},{4,5},{5,4},{6,7},{7,6},{8,9},{9,8},{10,11... | collective-permute-start | bytes 122888 | tf_op jit(solution)/shard_map/ppermute | solution.py:366
  12.1 4.1 %collective-permute-start.5 = (bf16[80,256]{1,0:T(8,128)(2,1)S(1)}, bf16[80,256]{1,0:T(8,128)(2,1)S(1)}, u32[]{:S(2)}, u32[]{:S(2)}) collective-permute-start(bf16[80,256]{1,0:T(8,128)(2,1)S(1)} %get-tuple-element.40), channel_id=1, source_target_pairs={{0,2},{1,3},{2,0},{3,1},{4,6},{5,7},{6,4},{7,5},{8,10},{9,11},{10,... | collective-permute-start | bytes 122888 | tf_op jit(solution)/shard_map/ppermute | solution.py:366
  13.7 3.5 %collective-permute-start.6 = (bf16[80,256]{1,0:T(8,128)(2,1)S(1)}, bf16[80,256]{1,0:T(8,128)(2,1)S(1)}, u32[]{:S(2)}, u32[]{:S(2)}) collective-permute-start(bf16[80,256]{1,0:T(8,128)(2,1)S(1)} %get-tuple-element.41), channel_id=1, source_target_pairs={{0,3},{1,2},{2,1},{3,0},{4,7},{5,6},{6,5},{7,4},{8,11},{9,10},{10,... | collective-permute-start | bytes 122888 | tf_op jit(solution)/shard_map/ppermute | solution.py:366
  17.8 8.0 %collective-permute-start.11 = (bf16[80,256]{1,0:T(8,128)(2,1)S(1)}, bf16[80,256]{1,0:T(8,128)(2,1)S(1)}, u32[]{:S(2)}, u32[]{:S(2)}) collective-permute-start(bf16[80,256]{1,0:T(8,128)(2,1)S(1)} %shard_map.81.refs_3_.mine), channel_id=1, source_target_pairs={{0,4},{4,0},{8,12},{12,8},{16,20},{20,16},{24,28},{28,24},{1,5},{5... | collective-permute-start | bytes 122888 | tf_op jit(solution)/shard_map/ppermute | solution.py:379
  23.7 2.1 %collective-permute-start.12 = (bf16[16,128]{1,0:T(8,128)(2,1)S(1)}, bf16[16,128]{1,0:T(8,128)(2,1)S(1)}, u32[]{:S(2)}, u32[]{:S(2)}) collective-permute-start(bf16[16,128]{1,0:T(8,128)(2,1)S(1)} %get-tuple-element.51), channel_id=1, source_target_pairs={{0,1},{1,0},{2,3},{3,2},{4,5},{5,4},{6,7},{7,6},{8,9},{9,8},{10,11... | collective-permute-start | bytes 12296 | tf_op jit(solution)/shard_map/ppermute | solution.py:366
  23.8 3.0 %collective-permute-start.8 = (bf16[4,128,256]{2,1,0:T(8,128)(2,1)S(1)}, bf16[4,128,256]{2,1,0:T(8,128)(2,1)S(1)}, u32[]{:S(2)}, u32[]{:S(2)}) collective-permute-start(bf16[4,128,256]{2,1,0:T(8,128)(2,1)S(1)} %get-tuple-element.46), channel_id=1, source_target_pairs={{0,1},{1,0},{2,3},{3,2},{4,5},{5,4},{6,7},{7,6},{8,9},{9,8},{10,11... | collective-permute-start | bytes 786440 | tf_op jit(solution)/shard_map/ppermute | solution.py:366
  24.3 14.3 %collective-permute-start.9 = (bf16[4,128,256]{2,1,0:T(8,128)(2,1)S(1)}, bf16[4,128,256]{2,1,0:T(8,128)(2,1)S(1)}, u32[]{:S(2)}, u32[]{:S(2)}) collective-permute-start(bf16[4,128,256]{2,1,0:T(8,128)(2,1)S(1)} %get-tuple-element.49), channel_id=1, source_target_pairs={{0,2},{1,3},{2,0},{3,1},{4,6},{5,7},{6,4},{7,5},{8,10},{9,11},{10,... | collective-permute-start | bytes 786440 | tf_op jit(solution)/shard_map/ppermute | solution.py:366
  25.8 12.8 %collective-permute-start.10 = (bf16[4,128,256]{2,1,0:T(8,128)(2,1)S(1)}, bf16[4,128,256]{2,1,0:T(8,128)(2,1)S(1)}, u32[]{:S(2)}, u32[]{:S(2)}) collective-permute-start(bf16[4,128,256]{2,1,0:T(8,128)(2,1)S(1)} %get-tuple-element.50), channel_id=1, source_target_pairs={{0,3},{1,2},{2,1},{3,0},{4,7},{5,6},{6,5},{7,4},{8,11},{9,10},{10,... | collective-permute-start | bytes 786440 | tf_op jit(solution)/shard_map/ppermute | solution.py:366
  26.8 6.4 %collective-permute-start.15 = (bf16[80,256]{1,0:T(8,128)(2,1)S(1)}, bf16[80,256]{1,0:T(8,128)(2,1)S(1)}, u32[]{:S(2)}, u32[]{:S(2)}) collective-permute-start(bf16[80,256]{1,0:T(8,128)(2,1)S(1)} %shard_map.86.mine), channel_id=1, source_target_pairs={{0,24},{4,28},{8,16},{12,20},{16,8},{20,12},{24,0},{28,4},{1,25},{... | collective-permute-start | bytes 122888 | tf_op jit(solution)/shard_map/ppermute | solution.py:379
  31.0 5.3 %collective-permute-start.14 = (bf16[80,256]{1,0:T(8,128)(2,1)S(1)}, bf16[80,256]{1,0:T(8,128)(2,1)S(1)}, u32[]{:S(2)}, u32[]{:S(2)}) collective-permute-start(bf16[80,256]{1,0:T(8,128)(2,1)S(1)} %shard_map.86.mine), channel_id=1, source_target_pairs={{0,16},{4,20},{8,24},{12,28},{16,0},{20,4},{24,8},{28,12},{1,17},{... | collective-permute-start | bytes 122888 | tf_op jit(solution)/shard_map/ppermute | solution.py:379
  31.0 5.3 %collective-permute-start.13 = (bf16[80,256]{1,0:T(8,128)(2,1)S(1)}, bf16[80,256]{1,0:T(8,128)(2,1)S(1)}, u32[]{:S(2)}, u32[]{:S(2)}) collective-permute-start(bf16[80,256]{1,0:T(8,128)(2,1)S(1)} %shard_map.86.mine), channel_id=1, source_target_pairs={{0,8},{4,12},{8,0},{12,4},{16,24},{20,28},{24,16},{28,20},{1,9},{5... | collective-permute-start | bytes 122888 | tf_op jit(solution)/shard_map/ppermute | solution.py:379
